TPU v7x, 32 devices: a whole 2x2x4 slice. The times are simulated.
32 devices in a mesh: qa: 8 (over z, x), qb: 4 (over y, core).
Axes of the slice: x: 2, y: 2, z: 4, core: 2. Of those that a mesh axis runs over, the one named last changes fastest.
Arguments:
- state: float32 [8, 4, 128, 8, 128], P('qa', 'qb'), may hold values from -6 to 6
- costate: float32 [8, 4, 128, 8, 128], P('qa', 'qb'), may hold values from -6 to 6
- gates: float32 [2, 4, 128, 128], replicated, may hold values from -0.5 to 0.5
- targets: int32 [2, 4], replicated, may hold values from 0 to 1
Outputs:
- start_state: float32 [8, 4, 128, 8, 128], P('qa', 'qb')
- start_costate: float32 [8, 4, 128, 8, 128], P('qa', 'qb')
- gate_grads: float32 [2, 4, 128, 128], replicated
Inputs may be any that keep to these rules, and one draw needn't show every extreme that they name: `targets`: 0 means the gate acts on the last index, 1 on the third from last.
All inputs are finite; a program needn't handle non-finite values.
Results may differ from a plain program's by a relative error of at most 0.0003.
Values sent between devices are 32-bit elements; how exact they have to be, the bound alone decides.
No kernel may reach another device: no remote copies, remote signals or barrier semaphores. Data moves between devices by JAX's collectives and lax.ppermute only.
A program may use at most 64 MiB of HBM per device.

v0:
```python
import jax
import jax.numpy as jnp
from jax import lax
from jax.sharding import PartitionSpec as P


def unapply(values, matrix, target):

    def apply_low(inner):
        return jnp.einsum("abmsi,ij->abmsj", inner, matrix, precision=lax.Precision.HIGHEST)

    def apply_middle(inner):
        return jnp.einsum("abisl,ij->abjsl", inner, matrix, precision=lax.Precision.HIGHEST)

    return lax.cond(target == 0, apply_low, apply_middle, values)


def gradient(adjoint, earlier, target):

    def from_low(inner):
        return jnp.einsum("abmsi,abmsj->ij", inner[0], inner[1], precision=lax.Precision.HIGHEST)

    def from_middle(inner):
        return jnp.einsum("abisl,abjsl->ij", inner[0], inner[1], precision=lax.Precision.HIGHEST)

    return lax.cond(target == 0, from_low, from_middle, (adjoint, earlier))


def gate_step(amplitudes, adjoint, matrix, target):
    earlier = unapply(amplitudes, matrix, target)
    derivative = gradient(adjoint, earlier, target)
    return (earlier, unapply(adjoint, matrix, target), derivative)


def shards(state, costate, gates, targets):
    layout = state.shape
    rest_count = lax.axis_size("qa") * lax.axis_size("qb") * layout[2] * layout[3]
    amplitudes = state
    adjoint = costate
    pending = None
    results = [None, None]
    for block_index in (1, 0):
        derivs = [None, None, None, None]
        last_gate = 3
        for gate_index in range(last_gate, -1, -1):
            amplitudes, adjoint, derivs[gate_index] = gate_step(
                amplitudes,
                adjoint,
                gates[block_index, gate_index],
                targets[block_index, gate_index],
            )
        stacked = jnp.stack(derivs)
        results[block_index] = stacked
        if block_index == 1:
            amplitudes, adjoint = (
                lax.all_to_all(amplitudes, "qb", split_axis=2, concat_axis=1, tiled=True),
                lax.all_to_all(adjoint, "qb", split_axis=2, concat_axis=1, tiled=True),
            )
            amplitudes = amplitudes.reshape(layout)
            adjoint = adjoint.reshape(layout)
    amplitudes, adjoint = (
        lax.all_to_all(amplitudes, "qa", split_axis=2, concat_axis=0, tiled=True),
        lax.all_to_all(adjoint, "qa", split_axis=2, concat_axis=0, tiled=True),
    )
    amplitudes = amplitudes.reshape(layout)
    adjoint = adjoint.reshape(layout)
    whole = jnp.stack(results)
    whole = lax.psum(whole, ("qa", "qb"))
    gate_grads = whole * rest_count ** (-0.5)
    return (amplitudes, adjoint, gate_grads)


def solution(mesh):
    in_specs = (P("qa", "qb", None, None, None), P("qa", "qb", None, None, None), P(), P())
    out_specs = (P("qa", "qb", None, None, None), P("qa", "qb", None, None, None), P())
    return jax.shard_map(shards, mesh=mesh, in_specs=in_specs, out_specs=out_specs, check_vma=False)
```

profile of v0, /device:TPU:0, one launch (start us, length us, event | category | flops | bytes accessed | tf_op | source)
XLA Modules:
  0.0 228.5 jit_solution(8593470169828072540)
XLA Ops:
  11.4 1.8 slice_bitcast_fusion
  17.6 4.4 %all-to-all-start.2 = ((f32[1,1,128,8,128]{4,3,1,0,2:T(8,128)}), f32[1,1,128,8,128]{4,3,1,0,2:T(8,128)S(1)}, u32[]{:S(2)}, u32[]{:S(2)}) async-start(f32[1,1,128,8,128]{4,3,1,0,2:T(8,128)} %bitcast.433), calls=%async_computation.2 | async-start | bytes 1048576 | tf_op jit(solution)/shard_map/all_to_all | solution.py:57
  26.2 2.5 %conditional.27 = (f32[1,1,128,8,128]{4,2,3,1,0:T(8,128)}) conditional(s32[]{:T(128)} %bitcast.160, (f32[1,1,128,8,128]{4,2,3,1,0:T(8,128)}, f32[128,128]{1,0:T(8,128)S(1)}) %tuple.187, (f32[1,1,128,8,128]{4,2,3,1,0:T(8,128)}, f32[128,128]{1,0:T(8,128)S(1)}) %tuple.187), branch_computations={%region_6.0_spmd, %region_7.0_spmd} | conditional | flops 201326592 | bytes 1114120 | solution.py:15
  26.2 2.5 %convolution_bitcast_fusion.6 = f32[1,1,128,8,128]{4,2,3,1,0:T(8,128)} fusion(f32[1,1,128,8,128]{4,2,3,1,0:T(8,128)} %get-tuple-element.291, f32[128,128]{1,0:T(8,128)S(1)} %get-tuple-element.442), kind=kOutput, calls=%fused_computation.20 | convolution fusion | flops 201326592 | bytes 1114112 | tf_op jit(solution)/shard_map/cond/branch_0_fun/abisl,ij->abjsl/dot_general | solution.py:13
  28.7 2.1 copy.47
  30.9 4.1 %all-to-all-start = ((f32[1,1,128,8,128]{4,3,1,0,2:T(8,128)}), f32[1,1,128,8,128]{4,3,1,0,2:T(8,128)}, u32[]{:S(2)}, u32[]{:S(2)}) async-start(f32[1,1,128,8,128]{4,3,1,0,2:T(8,128)} %copy.47), calls=%async_computation | async-start | bytes 1048576 | tf_op jit(solution)/shard_map/all_to_all | solution.py:56
  38.9 2.5 %conditional.37 = (f32[1,1,128,8,128]{4,2,3,1,0:T(8,128)}) conditional(s32[]{:T(128)} %bitcast.158, (f32[1,1,128,8,128]{4,2,3,1,0:T(8,128)}, f32[128,128]{1,0:T(8,128)S(1)}) %tuple.197, (f32[1,1,128,8,128]{4,2,3,1,0:T(8,128)}, f32[128,128]{1,0:T(8,128)S(1)}) %tuple.197), branch_computations={%region_26.0_spmd, %region_27.0_spmd} | conditional | flops 201326592 | bytes 1114120 | solution.py:15
  38.9 2.5 %convolution_bitcast_fusion.24 = f32[1,1,128,8,128]{4,2,3,1,0:T(8,128)} fusion(f32[1,1,128,8,128]{4,2,3,1,0:T(8,128)} %get-tuple-element.331, f32[128,128]{1,0:T(8,128)S(1)} %get-tuple-element.468), kind=kOutput, calls=%fused_computation.86 | convolution fusion | flops 201326592 | bytes 1114112 | tf_op jit(solution)/shard_map/cond/branch_0_fun/abisl,ij->abjsl/dot_general | solution.py:13
  41.4 2.4 %conditional.38 = (f32[1,1,128,8,128]{4,2,3,1,0:T(8,128)}) conditional(s32[]{:T(128)} %bitcast.157, (f32[1,1,128,8,128]{4,2,3,1,0:T(8,128)}, f32[128,128]{1,0:T(8,128)S(1)}) %tuple.198, (f32[1,1,128,8,128]{4,2,3,1,0:T(8,128)}, f32[128,128]{1,0:T(8,128)S(1)}) %tuple.198), branch_computations={%region_28.0_spmd, %region_29.0_spmd} | conditional | flops 201326592 | bytes 1114120 | solution.py:15
  41.4 2.4 %convolution_bitcast_fusion.27 = f32[1,1,128,8,128]{4,2,3,1,0:T(8,128)} fusion(f32[1,1,128,8,128]{4,2,3,1,0:T(8,128)} %get-tuple-element.336, f32[128,128]{1,0:T(8,128)S(1)} %get-tuple-element.337), kind=kOutput, calls=%fused_computation.95 | convolution fusion | flops 201326592 | bytes 1114112 | tf_op jit(solution)/shard_map/cond/branch_1_fun/abmsi,ij->abmsj/dot_general | solution.py:10
  43.8 2.5 %conditional.39 = (f32[128,8,128]{2,0,1:T(8,128)}) conditional(s32[]{:T(128)} %bitcast.156, (f32[1,1,128,8,128]{4,2,3,1,0:T(8,128)}, f32[128,128]{1,0:T(8,128)S(1)}) %tuple.199, (f32[1,1,128,8,128]{4,2,3,1,0:T(8,128)}, f32[128,128]{1,0:T(8,128)S(1)}) %tuple.199), branch_computations={%region_30.0_spmd, %region_31.0_spmd} | conditional | flops 201326592 | bytes 1114120 | solution.py:15
  43.8 2.5 %fusion.70 = f32[128,8,128]{2,0,1:T(8,128)} fusion(f32[1,1,128,8,128]{4,2,3,1,0:T(8,128)} %get-tuple-element.339, f32[128,128]{1,0:T(8,128)S(1)} %get-tuple-element.472), kind=kOutput, calls=%fused_computation.98 | convolution fusion | flops 201326592 | bytes 1114112 | tf_op jit(solution)/shard_map/cond/branch_0_fun/abisl,ij->abjsl/dot_general | solution.py:13
  46.3 2.2 copy.155
  48.5 6.5 %all-to-all-start.3 = ((f32[1,1,128,8,128]{4,3,1,0,2:T(8,128)}), f32[1,1,128,8,128]{4,3,1,0,2:T(8,128)}, u32[]{:S(2)}, u32[]{:S(2)}) async-start(f32[1,1,128,8,128]{4,3,1,0,2:T(8,128)} %bitcast.434), calls=%async_computation.3 | async-start | bytes 1048576 | tf_op jit(solution)/shard_map/all_to_all | solution.py:63
  55.0 2.4 %conditional.28 = (f32[1,1,128,8,128]{4,2,3,1,0:T(8,128)}) conditional(s32[]{:T(128)} %bitcast.159, (f32[1,1,128,8,128]{4,3,1,0,2:T(8,128)}, f32[128,128]{1,0:T(8,128)S(1)}) %tuple.188, (f32[1,1,128,8,128]{4,3,1,0,2:T(8,128)}, f32[128,128]{1,0:T(8,128)S(1)}) %tuple.188), branch_computations={%region_8.0_spmd, %region_9.0_spmd} | conditional | flops 201326592 | bytes 1114120 | solution.py:15
  55.0 2.4 %convolution_bitcast_fusion.9 = f32[1,1,128,8,128]{4,2,3,1,0:T(8,128)} fusion(f32[1,1,128,8,128]{4,3,1,0,2:T(8,128)} %get-tuple-element.445, f32[128,128]{1,0:T(8,128)S(1)} %get-tuple-element.297), kind=kOutput, calls=%fused_computation.30 | convolution fusion | flops 201326592 | bytes 1114112 | tf_op jit(solution)/shard_map/cond/branch_1_fun/abmsi,ij->abmsj/dot_general | solution.py:10
  57.4 2.5 %conditional.29 = (f32[1,1,128,8,128]{4,2,3,1,0:T(8,128)}) conditional(s32[]{:T(128)} %bitcast.158, (f32[1,1,128,8,128]{4,2,3,1,0:T(8,128)}, f32[128,128]{1,0:T(8,128)S(1)}) %tuple.189, (f32[1,1,128,8,128]{4,2,3,1,0:T(8,128)}, f32[128,128]{1,0:T(8,128)S(1)}) %tuple.189), branch_computations={%region_10.0_spmd, %region_11.0_spmd} | conditional | flops 201326592 | bytes 1114120 | solution.py:15
  57.4 2.5 %convolution_bitcast_fusion.10 = f32[1,1,128,8,128]{4,2,3,1,0:T(8,128)} fusion(f32[1,1,128,8,128]{4,2,3,1,0:T(8,128)} %get-tuple-element.299, f32[128,128]{1,0:T(8,128)S(1)} %get-tuple-element.448), kind=kOutput, calls=%fused_computation.34 | convolution fusion | flops 201326592 | bytes 1114112 | tf_op jit(solution)/shard_map/cond/branch_0_fun/abisl,ij->abjsl/dot_general | solution.py:13
  59.9 2.4 %conditional.30 = (f32[1,1,128,8,128]{4,2,3,1,0:T(8,128)}) conditional(s32[]{:T(128)} %bitcast.157, (f32[1,1,128,8,128]{4,2,3,1,0:T(8,128)}, f32[128,128]{1,0:T(8,128)S(1)}) %tuple.190, (f32[1,1,128,8,128]{4,2,3,1,0:T(8,128)}, f32[128,128]{1,0:T(8,128)S(1)}) %tuple.190), branch_computations={%region_12.0_spmd, %region_13.0_spmd} | conditional | flops 201326592 | bytes 1114120 | solution.py:15
  59.9 2.4 %convolution_bitcast_fusion.13 = f32[1,1,128,8,128]{4,2,3,1,0:T(8,128)} fusion(f32[1,1,128,8,128]{4,2,3,1,0:T(8,128)} %get-tuple-element.304, f32[128,128]{1,0:T(8,128)S(1)} %get-tuple-element.305), kind=kOutput, calls=%fused_computation.43 | convolution fusion | flops 201326592 | bytes 1114112 | tf_op jit(solution)/shard_map/cond/branch_1_fun/abmsi,ij->abmsj/dot_general | solution.py:10
  62.3 2.5 %conditional.31 = (f32[1,1,128,8,128]{4,2,3,1,0:T(8,128)}) conditional(s32[]{:T(128)} %bitcast.156, (f32[1,1,128,8,128]{4,2,3,1,0:T(8,128)}, f32[128,128]{1,0:T(8,128)S(1)}) %tuple.191, (f32[1,1,128,8,128]{4,2,3,1,0:T(8,128)}, f32[128,128]{1,0:T(8,128)S(1)}) %tuple.191), branch_computations={%region_14.0_spmd, %region_15.0_spmd} | conditional | flops 201326592 | bytes 1114120 | solution.py:15
  62.3 2.5 %convolution_bitcast_fusion.14 = f32[1,1,128,8,128]{4,2,3,1,0:T(8,128)} fusion(f32[1,1,128,8,128]{4,2,3,1,0:T(8,128)} %get-tuple-element.307, f32[128,128]{1,0:T(8,128)S(1)} %get-tuple-element.452), kind=kOutput, calls=%fused_computation.46 | convolution fusion | flops 201326592 | bytes 1114112 | tf_op jit(solution)/shard_map/cond/branch_0_fun/abisl,ij->abjsl/dot_general | solution.py:13
  64.7 2.2 copy.54
  66.9 3.3 %all-to-all-done.3 = f32[1,1,128,8,128]{4,3,1,0,2:T(8,128)} async-done(((f32[1,1,128,8,128]{4,3,1,0,2:T(8,128)}), f32[1,1,128,8,128]{4,3,1,0,2:T(8,128)}, u32[]{:S(2)}, u32[]{:S(2)}) %all-to-all-start.3) | async-done | bytes 524320 | tf_op jit(solution)/shard_map/all_to_all | solution.py:63
  70.2 4.1 %all-to-all-start.1 = ((f32[1,1,128,8,128]{4,3,1,0,2:T(8,128)}), f32[1,1,128,8,128]{4,3,1,0,2:T(8,128)}, u32[]{:S(2)}, u32[]{:S(2)}) async-start(f32[1,1,128,8,128]{4,3,1,0,2:T(8,128)} %copy.54), calls=%async_computation.1 | async-start | bytes 1048576 | tf_op jit(solution)/shard_map/all_to_all | solution.py:62
  74.4 3.8 %conditional.47 = (f32[1,128,128]{2,1,0:T(8,128)S(1)}) conditional(s32[]{:T(128)} %bitcast.163, (f32[1,1,128,8,128]{4,3,2,1,0:T(8,128)}, f32[1,1,128,8,128]{4,2,3,1,0:T(8,128)S(1)}) %tuple.207, (f32[1,1,128,8,128]{4,3,2,1,0:T(8,128)}, f32[1,1,128,8,128]{4,2,3,1,0:T(8,128)S(1)}) %tuple.207), branch_computations={%region_46.0_spmd, %region_47.0_spmd} | conditional | flops 201326592 | bytes 2162696 | solution.py:26
  74.4 2.1 copy.78
  76.5 1.7 convolution_bitcast_fusion.43
  86.6 129.4 %all-reduce.2.cloned.1.call-done = f32[2,4,128,128]{3,2,1,0:T(8,128)} async-done(((f32[2,4,128,128]{3,2,1,0:T(8,128)}), f32[2,4,128,128]{3,2,1,0:T(8,128)}) %all-reduce.2.cloned.1.call-update) | async-done | bytes 524304 | tf_op jit(solution)/shard_map/psum | solution.py:68
  216.0 1.9 broadcast_multiply_fusion
  217.9 1.9 copy.208
  219.8 1.9 copy.209
  (64 shorter events, 34.4 us)
Async XLA Ops:
  11.4 1.8 copy-start.7
  13.2 1.4 copy-start.11
  17.6 4.4 %copy-start.10 = (f32[1,1,128,8,128]{4,3,2,1,0:T(8,128)S(1)}, f32[1,1,128,8,128]{4,3,2,1,0:T(8,128)}, u32[]{:S(2)}) copy-start(f32[1,1,128,8,128]{4,3,2,1,0:T(8,128)} %param.52) | copy-start | bytes 1572868
  17.6 13.2 %all-to-all-start.2 = ((f32[1,1,128,8,128]{4,3,1,0,2:T(8,128)}), f32[1,1,128,8,128]{4,3,1,0,2:T(8,128)S(1)}, u32[]{:S(2)}, u32[]{:S(2)}) async-start(f32[1,1,128,8,128]{4,3,1,0,2:T(8,128)} %bitcast.433), calls=%async_computation.2 | async-start | bytes 1048576 | tf_op jit(solution)/shard_map/all_to_all | solution.py:57
  30.9 17.6 %all-to-all-start = ((f32[1,1,128,8,128]{4,3,1,0,2:T(8,128)}), f32[1,1,128,8,128]{4,3,1,0,2:T(8,128)}, u32[]{:S(2)}, u32[]{:S(2)}) async-start(f32[1,1,128,8,128]{4,3,1,0,2:T(8,128)} %copy.47), calls=%async_computation | async-start | bytes 1048576 | tf_op jit(solution)/shard_map/all_to_all | solution.py:56
  48.5 21.7 %all-to-all-start.3 = ((f32[1,1,128,8,128]{4,3,1,0,2:T(8,128)}), f32[1,1,128,8,128]{4,3,1,0,2:T(8,128)}, u32[]{:S(2)}, u32[]{:S(2)}) async-start(f32[1,1,128,8,128]{4,3,1,0,2:T(8,128)} %bitcast.434), calls=%async_computation.3 | async-start | bytes 1048576 | tf_op jit(solution)/shard_map/all_to_all | solution.py:63
  70.2 147.7 %all-to-all-start.1 = ((f32[1,1,128,8,128]{4,3,1,0,2:T(8,128)}), f32[1,1,128,8,128]{4,3,1,0,2:T(8,128)}, u32[]{:S(2)}, u32[]{:S(2)}) async-start(f32[1,1,128,8,128]{4,3,1,0,2:T(8,128)} %copy.54), calls=%async_computation.1 | async-start | bytes 1048576 | tf_op jit(solution)/shard_map/all_to_all | solution.py:62
  74.3 141.7 %all-reduce.2.cloned.1.call-start = ((), (), s32[]{:S(2)}) async-start(), calls=%async_computation.4 | async-start | bytes 1048576 | tf_op jit(solution)/shard_map/psum | solution.py:68
  78.2 1.0 copy-start
  79.2 1.3 copy-start.8
  80.5 1.0 copy-start.4
  81.5 1.0 copy-start.1
  81.5 1.2 copy-start.5
  82.7 1.0 copy-start.2
  82.7 1.2 copy-start.6
  83.9 1.0 copy-start.3
  83.9 1.2 copy-start.9
Sparse Core Ops, SparseCore 0:
  86.7 129.2 all-reduce.1
where the time goes:
time: 230 us; the launch traced here: 229 us
  waiting for transfers between devices  133 us (58%)
  matrix products  35.4 us (15%)
  between operations  19.3 us (8%)
  starting transfers between devices  19.2 us (8%)
  local copies, waits for them, and re-layouts  18.7 us (8%)
  other arithmetic  2.75 us (1%)
    psum x1, waiting for transfers between devices, shards(): whole = lax.psum(whole, ('qa', 'qb'))  129 us
    dot_general x10, matrix products, apply_low(): jnp.einsum('abmsi,ij->abmsj', inner, matrix, precision=lax.Precision.HIGH...  15.3 us
    dot_general x6, matrix products, apply_middle(): jnp.einsum('abisl,ij->abjsl', inner, matrix, precision=lax.Precision.HIGH...  13 us
    cond x4, local copies, waits for them, and re-layouts, unapply(): return lax.cond(target == 0, apply_low, apply_middle, values)  7.61 us
    all_to_all x1, starting transfers between devices, shards(): lax.all_to_all(adjoint, 'qa', split_axis=2, concat_axis=0, tiled=True)  6.51 us
    unnamed x26, local copies, waits for them, and re-layouts  5.32 us
    dot_general x5, matrix products, from_low(): jnp.einsum('abmsi,abmsj->ij', inner[0], inner[1], precision=lax.Precision...  5.31 us
  transfers between devices with their start and end apart: 5, of which 2 were waited for; matrix products, arithmetic and copies ran while one was open for 19% of the time, Pallas kernels for 0%

commit v1 on v0

v1 whole, which is shorter than its diff:
```python
import functools

import jax
import jax.numpy as jnp
from jax import lax
from jax.experimental import pallas as pl
from jax.experimental.pallas import tpu as pltpu
from jax.sharding import PartitionSpec as P

F32, BF16 = jnp.float32, jnp.bfloat16
VMEM_LIMIT = 32 * 1024 * 1024


def split(x):
    high = x.astype(BF16)
    return high, (x - high.astype(F32)).astype(BF16)


def dot(a, b, dims=((1,), (0,))):
    return lax.dot_general(a, b, (dims, ((), ())), preferred_element_type=F32)


def right_factor(u):
    high, low = split(u)
    row = jnp.concatenate([high, low], axis=1)
    return jnp.concatenate([row, row], axis=0)


def left_factor(u):
    high, low = split(jnp.transpose(u))
    return jnp.concatenate(
        [jnp.concatenate([high, high], axis=1), jnp.concatenate([low, low], axis=1)], axis=0
    )


def times_right(x, factor):
    d = x.shape[1]
    r = dot(jnp.concatenate(split(x), axis=1), factor)
    return r[:, :d] + r[:, d:]


def times_left(factor, x):
    d = x.shape[0]
    r = dot(factor, jnp.concatenate(split(x), axis=0))
    return r[:d] + r[d:]


def matmul(a, b):
    return times_right(a, right_factor(b))


def slab_of_native(ref, s):
    rows, slabs, lanes = ref.shape
    return ref.reshape(rows * slabs, lanes)[pl.ds(s, rows, stride=slabs), :]


def slab_of_parts(ref, a, s):
    n, _, _, r, lanes = ref.shape
    return ref[:, a, s].reshape(n * r, lanes)


def products(targets, gates, block):
    d = gates.shape[-1]
    eye = (
        lax.broadcasted_iota(jnp.int32, (d, d), 0) == lax.broadcasted_iota(jnp.int32, (d, d), 1)
    ).astype(F32)
    last = gates.shape[1] - 1
    u = gates[block, last]
    low_turn = targets[block, last] == 0
    low, mid = jnp.where(low_turn, u, eye), jnp.where(low_turn, eye, u)
    for g in range(last - 1, -1, -1):
        both = matmul(jnp.concatenate([low, mid], axis=0), gates[block, g])
        low_turn = targets[block, g] == 0
        low, mid = jnp.where(low_turn, both[:d], low), jnp.where(low_turn, mid, both[d:])
    return low, mid


def apply_kernel(block, native, targets, gates, *refs):
    out = refs[-1]
    n, _, slabs, r, d = out.shape
    low, mid = products(targets, gates, block)
    low, mid = right_factor(low), left_factor(mid)
    for s in range(slabs):
        if native:
            x, y = slab_of_native(refs[0], s), slab_of_native(refs[1], s)
        else:
            x, y = slab_of_parts(refs[0], 0, s), slab_of_parts(refs[0], 1, s)
        z = times_right(jnp.concatenate([x, y], axis=0), low)
        z = times_left(mid, jnp.concatenate([z[: n * r], z[n * r :]], axis=1))
        out[:, 0, s] = z[:, :d].reshape(n, r, d)
        out[:, 1, s] = z[:, d:].reshape(n, r, d)


def gradient_kernel(block, native, scale, targets, gates, *refs):
    out, held, inner = refs[-3:]
    slabs, d = held.shape[1], held.shape[3]
    for s in range(slabs):
        for a in range(2):
            held[a, s] = slab_of_native(refs[a], s) if native else slab_of_parts(refs[0], a, s)

    def contract_low():
        total = jnp.zeros((2 * d, 2 * d), F32)
        for s in range(slabs):
            y = jnp.concatenate(split(held[1, s]), axis=1)
            x = jnp.concatenate(split(held[0, s]), axis=1)
            total = total + dot(y, x, ((0,), (0,)))
        inner[...] = (total[:d, :d] + total[d:, d:]) + (total[:d, d:] + total[d:, :d])

    def contract_mid():
        total = jnp.zeros((2 * d, 2 * d), F32)
        for s in range(slabs):
            y = jnp.concatenate(split(held[1, s]), axis=0)
            x = jnp.concatenate(split(held[0, s]), axis=0)
            total = total + dot(y, x, ((1,), (1,)))
        inner[...] = (total[:d, :d] + total[d:, d:]) + (total[:d, d:] + total[d:, :d])

    def apply_low(u):
        factor = right_factor(u)
        for s in range(slabs):
            z = times_right(jnp.concatenate([held[0, s], held[1, s]], axis=0), factor)
            held[0, s], held[1, s] = z[:d], z[d:]

    def apply_mid(u):
        factor = left_factor(u)
        for s in range(slabs):
            z = times_left(factor, jnp.concatenate([held[0, s], held[1, s]], axis=1))
            held[0, s], held[1, s] = z[:, :d], z[:, d:]

    last = gates.shape[1] - 1
    pending = None
    for g in range(last, -1, -1):
        low_turn = targets[block, g] == 0
        fresh = True if g == last else targets[block, g] != targets[block, g + 1]
        pl.when(jnp.logical_and(fresh, low_turn))(contract_low)
        pl.when(jnp.logical_and(fresh, jnp.logical_not(low_turn)))(contract_mid)
        u = gates[block, g]
        grad = matmul(inner[...], u)
        out[g] = grad * scale
        if g == 0:
            break
        inner[...] = times_left(left_factor(u), grad)
        pending = u if g == last else jnp.where(fresh, u, matmul(pending, u))
        turn = targets[block, g - 1] != targets[block, g]
        pl.when(jnp.logical_and(turn, low_turn))(lambda p=pending: apply_low(p))
        pl.when(jnp.logical_and(turn, jnp.logical_not(low_turn)))(lambda p=pending: apply_mid(p))


def store_kernel(parts, first, second):
    n, _, slabs, r, d = parts.shape
    for a, out in enumerate((first, second)):
        flat = out.reshape(n * r * slabs, d)
        for s in range(slabs):
            flat[pl.ds(s, n * r, stride=slabs), :] = slab_of_parts(parts, a, s)


def call(kernel, out_shape, inputs, scratch=(), flops=0):
    specs = [
        pl.BlockSpec(memory_space=pltpu.SMEM if x.dtype == jnp.int32 else pltpu.VMEM)
        for x in inputs
    ]
    outs = jax.tree.map(lambda _: pl.BlockSpec(memory_space=pltpu.VMEM), out_shape)
    size = sum(x.size * 4 for x in inputs) + sum(x.size * 4 for x in jax.tree.leaves(out_shape))
    return pl.pallas_call(
        kernel,
        out_shape=out_shape,
        in_specs=specs,
        out_specs=outs,
        scratch_shapes=list(scratch),
        compiler_params=pltpu.CompilerParams(vmem_limit_bytes=VMEM_LIMIT),
        cost_estimate=pl.CostEstimate(flops=flops, bytes_accessed=size, transcendentals=0),
    )(*inputs)


def shards(state, costate, gates, targets):
    layout = state.shape
    rows, slabs, d = layout[2:]
    n_qa, n_qb = lax.axis_size("qa"), lax.axis_size("qb")
    scale = (n_qa * n_qb * rows * slabs) ** -0.5
    natives = [state.reshape(layout[2:]), costate.reshape(layout[2:])]
    parts_qb = jax.ShapeDtypeStruct((n_qb, 2, slabs, rows // n_qb, d), F32)
    parts_qa = jax.ShapeDtypeStruct((n_qa, 2, slabs, rows // n_qa, d), F32)
    grads = jax.ShapeDtypeStruct(gates.shape[1:], F32)
    scratch = [pltpu.VMEM((2, slabs, rows, d), F32), pltpu.VMEM((d, d), F32)]
    work = 2 * 2 * 2 * 4 * rows * slabs * d * d

    sent = call(functools.partial(apply_kernel, 1, True), parts_qb, [targets, gates, *natives], flops=work)
    parts = lax.all_to_all(sent, "qb", 0, 0, tiled=True)
    grads1 = call(
        functools.partial(gradient_kernel, 1, True, scale), grads, [targets, gates, *natives], scratch, 8 * work
    )
    sent = call(functools.partial(apply_kernel, 0, False), parts_qa, [targets, gates, parts], flops=work)
    last = lax.all_to_all(sent, "qa", 0, 0, tiled=True)
    grads0 = call(
        functools.partial(gradient_kernel, 0, False, scale), grads, [targets, gates, parts], scratch, 8 * work
    )
    both = jnp.stack([grads0, grads1])
    shares = both.reshape(n_qa * n_qb, -1, d)
    share = lax.all_to_all(shares, ("qa", "qb"), 0, 0, tiled=True).sum(0, keepdims=True)
    whole = lax.all_to_all(jnp.broadcast_to(share, shares.shape), ("qa", "qb"), 0, 0, tiled=True)
    native = jax.ShapeDtypeStruct(layout[2:], F32)
    first, second = call(store_kernel, (native, native), [last])
    return first.reshape(layout), second.reshape(layout), whole.reshape(gates.shape)


def solution(mesh):
    in_specs = (P("qa", "qb", None, None, None), P("qa", "qb", None, None, None), P(), P())
    out_specs = (P("qa", "qb", None, None, None), P("qa", "qb", None, None, None), P())
    return jax.shard_map(shards, mesh=mesh, in_specs=in_specs, out_specs=out_specs, check_vma=False)
```

time: 230 us -> 102 us (0.44)
  waiting for transfers between devices: 133 us -> 62.2 us
  matrix products: 35.4 us -> 0 us
  between operations: 19.3 us -> 0.7 us
  Pallas kernels: 0 us -> 15.5 us
  local copies, waits for them, and re-layouts: 18.7 us -> 5.45 us
    psum x1 -> x0, waiting for transfers between devices: 129 us -> none  [shards(): whole = lax.psum(whole, ('qa', 'qb'))]
    all_to_all x4, waiting for transfers between devices: 3.29 us -> 62.2 us  [the longest x1 26 us: shards(): last = lax.all_to_all(sent, 'qa', 0, 0, tiled=True)]
    dot_general x24 -> x0, matrix products: 35.4 us -> none  [the longest x10 15.3 us: apply_low(): jnp.einsum('abmsi,ij->abmsj', inner, matrix, precision=lax.Precision.HIGH...]
    pallas_call x0 -> x5, Pallas kernels: none -> 15.5 us  [call(): pl.pallas_call(kernel, out_shape=out_shape, in_specs=specs, out_specs=out...]
    cond x4 -> x0, local copies, waits for them, and re-layouts: 7.61 us -> none  [unapply(): return lax.cond(target == 0, apply_low, apply_middle, values)]
    unnamed x26 -> x15, local copies, waits for them, and re-layouts: 5.32 us -> 4.6 us
  transfers between devices with their start and end apart: 5 -> 4, of which waited for: 2 -> 4; matrix products, arithmetic and copies ran while one was open for 19% -> 0% of each run, Pallas kernels for 0% -> 9%
where the time goes in v1:
time: 102 us
  waiting for transfers between devices  62.2 us (61%)
  starting transfers between devices  17.1 us (17%)
  Pallas kernels  15.5 us (15%)
  local copies, waits for them, and re-layouts  5.45 us (5%)
    all_to_all x1, waiting for transfers between devices, shards(): last = lax.all_to_all(sent, 'qa', 0, 0, tiled=True)  26 us
    pallas_call x5, Pallas kernels, call(): pl.pallas_call(kernel, out_shape=out_shape, in_specs=specs, out_specs=out...  15.5 us
    all_to_all x1, waiting for transfers between devices, shards(): lax.all_to_all(jnp.broadcast_to(share, shares.shape), ('qa', 'qb'), 0, 0,...  14.3 us
    all_to_all x1, waiting for transfers between devices, shards(): lax.all_to_all(shares, ('qa', 'qb'), 0, 0, tiled=True).sum(0, keepdims=True)  12.7 us
    all_to_all x1, waiting for transfers between devices, shards(): parts = lax.all_to_all(sent, 'qb', 0, 0, tiled=True)  9.21 us
    all_to_all x1, starting transfers between devices, shards(): lax.all_to_all(shares, ('qa', 'qb'), 0, 0, tiled=True).sum(0, keepdims=True)  5.59 us
    unnamed x15, local copies, waits for them, and re-layouts  4.6 us
    all_to_all x1, starting transfers between devices, shards(): parts = lax.all_to_all(sent, 'qb', 0, 0, tiled=True)  4.37 us
  transfers between devices with their start and end apart: 4, of which 4 were waited for; matrix products, arithmetic and copies ran while one was open for 0% of the time, Pallas kernels for 9%

profile of v1, /device:TPU:0, one launch (start us, length us, event | category | flops | bytes accessed | tf_op | source)
XLA Modules:
  0.0 101.8 jit_solution(1282556627556169052)
XLA Ops:
  0.6 0.0 copy-start.6
  0.6 0.7 copy-done.6
  1.3 0.0 copy-start
  1.3 1.0 %copy-done = f32[2,4,128,128]{3,2,1,0:T(8,128)S(1)} copy-done((f32[2,4,128,128]{3,2,1,0:T(8,128)S(1)}, f32[2,4,128,128]{3,2,1,0:T(8,128)}, u32[]{:S(2)}) %copy-start) | copy-done | bytes 524312
  2.4 0.0 copy-start.2
  2.4 1.0 %copy-done.2 = f32[1,1,128,8,128]{4,3,2,1,0:T(8,128)S(1)} copy-done((f32[1,1,128,8,128]{4,3,2,1,0:T(8,128)S(1)}, f32[1,1,128,8,128]{4,3,2,1,0:T(8,128)}, u32[]{:S(2)}) %copy-start.2) | copy-done | bytes 524312
  3.4 0.0 copy-start.4
  3.4 1.0 %copy-done.4 = f32[1,1,128,8,128]{4,3,2,1,0:T(8,128)S(1)} copy-done((f32[1,1,128,8,128]{4,3,2,1,0:T(8,128)S(1)}, f32[1,1,128,8,128]{4,3,2,1,0:T(8,128)}, u32[]{:S(2)}) %copy-start.4) | copy-done | bytes 524312
  4.4 2.8 %shard_map.67 = f32[4,2,8,32,128]{4,3,2,1,0:T(8,128)} custom-call(s32[2,4]{1,0:T(2,128)S(1)} %copy-done.6, f32[2,4,128,128]{3,2,1,0:T(8,128)S(1)} %copy-done, f32[128,8,128]{2,1,0:T(8,128)S(1)} %bitcast.8, f32[128,8,128]{2,1,0:T(8,128)S(1)} %bitcast.10), custom_call_target="tpu_custom_call" | custom-call | flops 536870912 | bytes 2621472 | tf_op jit(solution)/shard_map/pallas_call | solution.py:163
  7.3 0.0 copy-start.1
  7.3 0.0 copy-start.3
  7.3 0.0 copy-start.5
  7.3 4.4 %all-to-all-start = ((f32[4,2,8,32,128]{4,3,2,1,0:T(8,128)}), f32[4,2,8,32,128]{4,3,2,1,0:T(8,128)S(1)}, u32[]{:S(2)}, u32[]{:S(2)}) async-start(f32[4,2,8,32,128]{4,3,2,1,0:T(8,128)} %shard_map.67), calls=%async_computation | async-start | bytes 2097152 | tf_op jit(solution)/shard_map/all_to_all | solution.py:187
  11.7 0.0 copy-done.1
  11.7 0.0 copy-done.3
  11.7 0.0 copy-done.5
  11.7 5.2 %shard_map.71 = f32[4,128,128]{2,1,0:T(8,128)S(1)} custom-call(s32[2,4]{1,0:T(2,128)S(1)} %copy-done.6, f32[2,4,128,128]{3,2,1,0:T(8,128)S(1)} %copy-done.1, f32[128,8,128]{2,1,0:T(8,128)S(1)} %bitcast.9, f32[128,8,128]{2,1,0:T(8,128)S(1)} %bitcast.11), custom_call_target="tpu_custom_call" | custom-call | flops 4294967296 | bytes 1835040 | tf_op jit(solution)/shard_map/pallas_call | solution.py:163
  16.9 9.2 %all-to-all-done.refs_0_ = f32[4,2,8,32,128]{4,3,2,1,0:T(8,128)S(1)} async-done(((f32[4,2,8,32,128]{4,3,2,1,0:T(8,128)}), f32[4,2,8,32,128]{4,3,2,1,0:T(8,128)S(1)}, u32[]{:S(2)}, u32[]{:S(2)}) %all-to-all-start) | async-done | bytes 1048608 | tf_op jit(solution)/shard_map/all_to_all | solution.py:187
  26.1 3.3 %shard_map.70 = f32[4,128,128]{2,1,0:T(8,128)S(1)} custom-call(s32[2,4]{1,0:T(2,128)S(1)} %copy-done.6, f32[2,4,128,128]{3,2,1,0:T(8,128)S(1)} %copy-done.1, f32[4,2,8,32,128]{4,3,2,1,0:T(8,128)S(1)} %all-to-all-done.refs_0_), custom_call_target="tpu_custom_call" | custom-call | flops 4294967296 | bytes 1835040 | tf_op jit(solution)/shard_map/pallas_call | solution.py:163
  29.4 0.8 pad_maximum_fusion
  30.3 5.6 %all-to-all-start.2 = ((f32[32,32,128]{2,1,0:T(8,128)}), f32[32,32,128]{2,1,0:T(8,128)S(1)}, u32[]{:S(2)}, u32[]{:S(2)}) async-start(f32[32,32,128]{2,1,0:T(8,128)} %bitcast.6), calls=%async_computation.2 | async-start | bytes 1048576 | tf_op jit(solution)/shard_map/all_to_all | solution.py:198
  35.9 2.8 %shard_map.68 = f32[8,2,8,16,128]{4,3,2,1,0:T(8,128)} custom-call(s32[2,4]{1,0:T(2,128)S(1)} %copy-done.6, f32[2,4,128,128]{3,2,1,0:T(8,128)S(1)} %copy-done.1, f32[4,2,8,32,128]{4,3,2,1,0:T(8,128)S(1)} %all-to-all-done.refs_0_), custom_call_target="tpu_custom_call" | custom-call | flops 536870912 | bytes 2621472 | tf_op jit(solution)/shard_map/pallas_call | solution.py:163
  38.7 12.7 %all-to-all-done.2 = f32[32,32,128]{2,1,0:T(8,128)S(1)} async-done(((f32[32,32,128]{2,1,0:T(8,128)}), f32[32,32,128]{2,1,0:T(8,128)S(1)}, u32[]{:S(2)}, u32[]{:S(2)}) %all-to-all-start.2) | async-done | bytes 524320 | tf_op jit(solution)/shard_map/all_to_all | solution.py:198
  51.4 3.6 %all-to-all-start.1 = ((f32[8,2,8,16,128]{4,3,2,1,0:T(8,128)}), f32[8,2,8,16,128]{4,3,2,1,0:T(8,128)S(1)}, u32[]{:S(2)}, u32[]{:S(2)}) async-start(f32[8,2,8,16,128]{4,3,2,1,0:T(8,128)} %shard_map.68), calls=%async_computation.1 | async-start | bytes 2097152 | tf_op jit(solution)/shard_map/all_to_all | solution.py:192
  55.0 26.0 %all-to-all-done.1.parts = f32[8,2,8,16,128]{4,3,2,1,0:T(8,128)S(1)} async-done(((f32[8,2,8,16,128]{4,3,2,1,0:T(8,128)}), f32[8,2,8,16,128]{4,3,2,1,0:T(8,128)S(1)}, u32[]{:S(2)}, u32[]{:S(2)}) %all-to-all-start.1) | async-done | bytes 1048608 | tf_op jit(solution)/shard_map/all_to_all | solution.py:192
  81.0 0.9 broadcast_in_dim.2
  81.8 3.6 %all-to-all-start.3 = ((f32[32,32,128]{2,1,0:T(8,128)}), f32[32,32,128]{2,1,0:T(8,128)S(1)}, u32[]{:S(2)}, u32[]{:S(2)}) async-start(f32[32,32,128]{2,1,0:T(8,128)} %broadcast_in_dim.2), calls=%async_computation.3 | async-start | bytes 1048576 | tf_op jit(solution)/shard_map/all_to_all | solution.py:199
  85.4 1.2 %shard_map.69 = (f32[128,8,128]{2,1,0:T(8,128)}, f32[128,8,128]{2,1,0:T(8,128)}) custom-call(f32[8,2,8,16,128]{4,3,2,1,0:T(8,128)S(1)} %all-to-all-done.1.parts), custom_call_target="tpu_custom_call" | custom-call | bytes 2097152 | tf_op jit(solution)/shard_map/pallas_call | solution.py:163
  86.7 14.3 %all-to-all-done.3 = f32[32,32,128]{2,1,0:T(8,128)S(1)} async-done(((f32[32,32,128]{2,1,0:T(8,128)}), f32[32,32,128]{2,1,0:T(8,128)S(1)}, u32[]{:S(2)}, u32[]{:S(2)}) %all-to-all-start.3) | async-done | bytes 524320 | tf_op jit(solution)/shard_map/all_to_all | solution.py:199
  101.0 0.8 copy.8
  (1 shorter events, 0.0 us)
Async XLA Ops:
  0.6 0.7 copy-start.6
  1.3 1.0 %copy-start = (f32[2,4,128,128]{3,2,1,0:T(8,128)S(1)}, f32[2,4,128,128]{3,2,1,0:T(8,128)}, u32[]{:S(2)}) copy-start(f32[2,4,128,128]{3,2,1,0:T(8,128)} %gates.7) | copy-start | bytes 1572868
  2.4 1.0 %copy-start.2 = (f32[1,1,128,8,128]{4,3,2,1,0:T(8,128)S(1)}, f32[1,1,128,8,128]{4,3,2,1,0:T(8,128)}, u32[]{:S(2)}) copy-start(f32[1,1,128,8,128]{4,3,2,1,0:T(8,128)} %param.4) | copy-start | bytes 1572868
  3.4 1.0 %copy-start.4 = (f32[1,1,128,8,128]{4,3,2,1,0:T(8,128)S(1)}, f32[1,1,128,8,128]{4,3,2,1,0:T(8,128)}, u32[]{:S(2)}) copy-start(f32[1,1,128,8,128]{4,3,2,1,0:T(8,128)} %param.5) | copy-start | bytes 1572868
  7.3 4.4 %copy-start.1 = (f32[2,4,128,128]{3,2,1,0:T(8,128)S(1)}, f32[2,4,128,128]{3,2,1,0:T(8,128)}, u32[]{:S(2)}) copy-start(f32[2,4,128,128]{3,2,1,0:T(8,128)} %gates.7) | copy-start | bytes 1572868
  7.3 4.4 %copy-start.3 = (f32[1,1,128,8,128]{4,3,2,1,0:T(8,128)S(1)}, f32[1,1,128,8,128]{4,3,2,1,0:T(8,128)}, u32[]{:S(2)}) copy-start(f32[1,1,128,8,128]{4,3,2,1,0:T(8,128)} %param.4) | copy-start | bytes 1572868
  7.3 4.4 %copy-start.5 = (f32[1,1,128,8,128]{4,3,2,1,0:T(8,128)S(1)}, f32[1,1,128,8,128]{4,3,2,1,0:T(8,128)}, u32[]{:S(2)}) copy-start(f32[1,1,128,8,128]{4,3,2,1,0:T(8,128)} %param.5) | copy-start | bytes 1572868
  7.3 18.8 %all-to-all-start = ((f32[4,2,8,32,128]{4,3,2,1,0:T(8,128)}), f32[4,2,8,32,128]{4,3,2,1,0:T(8,128)S(1)}, u32[]{:S(2)}, u32[]{:S(2)}) async-start(f32[4,2,8,32,128]{4,3,2,1,0:T(8,128)} %shard_map.67), calls=%async_computation | async-start | bytes 2097152 | tf_op jit(solution)/shard_map/all_to_all | solution.py:187
  30.3 21.1 %all-to-all-start.2 = ((f32[32,32,128]{2,1,0:T(8,128)}), f32[32,32,128]{2,1,0:T(8,128)S(1)}, u32[]{:S(2)}, u32[]{:S(2)}) async-start(f32[32,32,128]{2,1,0:T(8,128)} %bitcast.6), calls=%async_computation.2 | async-start | bytes 1048576 | tf_op jit(solution)/shard_map/all_to_all | solution.py:198
  51.4 29.6 %all-to-all-start.1 = ((f32[8,2,8,16,128]{4,3,2,1,0:T(8,128)}), f32[8,2,8,16,128]{4,3,2,1,0:T(8,128)S(1)}, u32[]{:S(2)}, u32[]{:S(2)}) async-start(f32[8,2,8,16,128]{4,3,2,1,0:T(8,128)} %shard_map.68), calls=%async_computation.1 | async-start | bytes 2097152 | tf_op jit(solution)/shard_map/all_to_all | solution.py:192
  81.8 19.1 %all-to-all-start.3 = ((f32[32,32,128]{2,1,0:T(8,128)}), f32[32,32,128]{2,1,0:T(8,128)S(1)}, u32[]{:S(2)}, u32[]{:S(2)}) async-start(f32[32,32,128]{2,1,0:T(8,128)} %broadcast_in_dim.2), calls=%async_computation.3 | async-start | bytes 1048576 | tf_op jit(solution)/shard_map/all_to_all | solution.py:199

commit v2 on v1

v2 whole, which is shorter than its diff:
```python
import functools

import jax
import jax.numpy as jnp
from jax import lax
from jax.experimental import pallas as pl
from jax.experimental.pallas import tpu as pltpu
from jax.sharding import PartitionSpec as P

F32, BF16 = jnp.float32, jnp.bfloat16
VMEM_LIMIT = 32 * 1024 * 1024


def split(x):
    high = x.astype(BF16)
    return high, (x - high.astype(F32)).astype(BF16)


def dot(a, b, dims=((1,), (0,))):
    return lax.dot_general(a, b, (dims, ((), ())), preferred_element_type=F32)


def right_factor(u):
    high, low = split(u)
    row = jnp.concatenate([high, low], axis=1)
    return jnp.concatenate([row, row], axis=0)


def left_factor(u):
    return stack_factor(jnp.transpose(u))


def stack_factor(u):
    high, low = split(u)
    return jnp.concatenate(
        [jnp.concatenate([high, high], axis=1), jnp.concatenate([low, low], axis=1)], axis=0
    )


def times_right(x, factor):
    d = x.shape[1]
    r = dot(jnp.concatenate(split(x), axis=1), factor)
    return r[:, :d] + r[:, d:]


def times_left(factor, x):
    d = x.shape[0]
    r = dot(factor, jnp.concatenate(split(x), axis=0))
    return r[:d] + r[d:]


def matmul(a, b):
    return times_right(a, right_factor(b))


def slab_of_native(ref, s):
    rows, slabs, lanes = ref.shape
    return ref.reshape(rows * slabs, lanes)[pl.ds(s, rows, stride=slabs), :]


def slab_of_parts(ref, a, s):
    n, _, _, r, lanes = ref.shape
    return ref[:, a, s].reshape(n * r, lanes)


def products(targets, gates, block, at):
    d = gates.shape[-1]
    eye = (
        lax.broadcasted_iota(jnp.int32, (d, d), 0) == lax.broadcasted_iota(jnp.int32, (d, d), 1)
    ).astype(F32)
    last = gates.shape[1] - 1
    u = gates[at, last]
    low_turn = targets[block, last] == 0
    low, mid = jnp.where(low_turn, u, eye), jnp.where(low_turn, eye, u)
    for g in range(last - 1, -1, -1):
        both = matmul(jnp.concatenate([low, mid], axis=0), gates[at, g])
        low_turn = targets[block, g] == 0
        low, mid = jnp.where(low_turn, both[:d], low), jnp.where(low_turn, mid, both[d:])
    return low, mid


def apply_kernel(block, native, targets, gates, *refs):
    out = refs[-1]
    n, _, slabs, r, d = out.shape
    low, mid = products(targets, gates, block, block)
    low, mid = right_factor(low), left_factor(mid)
    for s in range(slabs):
        if native:
            x, y = slab_of_native(refs[0], s), slab_of_native(refs[1], s)
        else:
            x, y = slab_of_parts(refs[0], 0, s), slab_of_parts(refs[0], 1, s)
        z = times_right(jnp.concatenate([x, y], axis=0), low)
        z = times_left(mid, jnp.concatenate([z[: n * r], z[n * r :]], axis=1))
        out[:, 0, s] = z[:, :d].reshape(n, r, d)
        out[:, 1, s] = z[:, d:].reshape(n, r, d)


def block_kernel(block, load, store, emit, scale, targets, gates, held, inner, grads):
    slabs, d = held.shape[1], held.shape[3]
    load(held)

    def contract_low():
        total = jnp.zeros((2 * d, 2 * d), F32)
        for s in range(slabs):
            y = jnp.concatenate(split(held[1, s]), axis=1)
            x = jnp.concatenate(split(held[0, s]), axis=1)
            total = total + dot(y, x, ((0,), (0,)))
        inner[...] = (total[:d, :d] + total[d:, d:]) + (total[:d, d:] + total[d:, :d])

    def contract_mid():
        total = jnp.zeros((2 * d, 2 * d), F32)
        for s in range(slabs):
            y = jnp.concatenate(split(held[1, s]), axis=0)
            x = jnp.concatenate(split(held[0, s]), axis=0)
            total = total + dot(y, x, ((1,), (1,)))
        inner[...] = (total[:d, :d] + total[d:, d:]) + (total[:d, d:] + total[d:, :d])

    def put(s, x, y):
        held[0, s], held[1, s] = x, y

    def apply_low(u, put):
        factor = right_factor(u)
        for s in range(slabs):
            z = times_right(jnp.concatenate([held[0, s], held[1, s]], axis=0), factor)
            put(s, z[:d], z[d:])

    def apply_mid(u, put):
        factor = left_factor(u)
        for s in range(slabs):
            z = times_left(factor, jnp.concatenate([held[0, s], held[1, s]], axis=1))
            put(s, z[:, :d], z[:, d:])

    last = gates.shape[1] - 1
    pending = None
    for g in range(last, -1, -1):
        low_turn = targets[block, g] == 0
        fresh = True if g == last else targets[block, g] != targets[block, g + 1]
        pl.when(jnp.logical_and(fresh, low_turn))(contract_low)
        pl.when(jnp.logical_and(fresh, jnp.logical_not(low_turn)))(contract_mid)
        u = gates[block, g]
        grad = matmul(inner[...], u)
        grads[g] = grad * scale
        pending = u if g == last else jnp.where(fresh, u, matmul(pending, u))
        if g == 0:
            break
        inner[...] = times_left(left_factor(u), grad)
        turn = targets[block, g - 1] != targets[block, g]
        pl.when(jnp.logical_and(turn, low_turn))(lambda p=pending: apply_low(p, put))
        pl.when(jnp.logical_and(turn, jnp.logical_not(low_turn)))(lambda p=pending: apply_mid(p, put))
    if store is not None:
        pl.when(low_turn)(lambda: apply_low(pending, store))
        pl.when(jnp.logical_not(low_turn))(lambda: apply_mid(pending, store))
    emit(grads)


def gradient_kernel(block, scale, targets, gates, *refs):
    out, held, inner = refs[-3:]

    def load(held):
        for s in range(held.shape[1]):
            for a in range(2):
                held[a, s] = slab_of_native(refs[a], s)

    block_kernel(block, load, None, lambda grads: None, scale, targets, gates, held, inner, out)


def slabs_gradient_kernel(block, scale, targets, gates, parts, out, held, inner):
    def load(held):
        for s in range(held.shape[1]):
            for a in range(2):
                held[a, s] = slab_of_parts(parts, a, s)

    block_kernel(block, load, None, lambda grads: None, scale, targets, gates, held, inner, out)


def second_kernel(block, n_qb, scale, targets, gates, *refs):
    blocks, (out, keep, send, held, inner, grads) = refs[:n_qb], refs[n_qb:]
    n, _, slabs, r, d = out.shape
    mine = lax.axis_index("qb")

    def load(held):
        for k, ref in enumerate(blocks):
            count = ref.shape[2]
            rows = pl.ds(pl.multiple_of((mine ^ k) * count, count), count)
            held[:, :, rows] = ref[...]

    def store(s, x, y):
        out[:, 0, s] = x.reshape(n, r, d)
        out[:, 1, s] = y.reshape(n, r, d)

    def emit(grads):
        half = grads.shape[0] // 2
        core = mine % 2
        keep[...] = grads[pl.ds(core * half, half)].reshape(keep.shape)
        send[...] = grads[pl.ds((1 - core) * half, half)].reshape(send.shape)

    block_kernel(block, load, store, emit, scale, targets, gates, held, inner, grads)


def first_kernel(block, n_qb, targets, gates, state, costate, *refs):
    outs, (mats, x_ref, y_ref, turned, sems) = refs[:n_qb], refs[n_qb:]
    copies = [
        pltpu.make_async_copy(gates.at[pl.ds(block, 1)], mats, sems.at[0]),
        pltpu.make_async_copy(state, x_ref, sems.at[1]),
        pltpu.make_async_copy(costate, y_ref, sems.at[2]),
    ]
    for copy in copies:
        copy.start()
    _, slabs, r, d = outs[0].shape
    mine = lax.axis_index("qb")
    copies[0].wait()
    low, mid = products(targets, mats, block, 0)
    low = right_factor(low)
    turned[...] = jnp.transpose(mid)
    mid = jnp.concatenate(
        [turned[pl.ds(pl.multiple_of((mine ^ k) * r, r), r), :] for k in range(n_qb)], axis=0
    )
    mid = stack_factor(mid)
    copies[1].wait()
    copies[2].wait()
    for s in range(slabs):
        x, y = slab_of_native(x_ref, s), slab_of_native(y_ref, s)
        z = times_right(jnp.concatenate([x, y], axis=0), low)
        z = times_left(mid, jnp.concatenate([z[:d], z[d:]], axis=1))
        for k, out in enumerate(outs):
            out[0, s] = z[k * r : (k + 1) * r, :d]
            out[1, s] = z[k * r : (k + 1) * r, d:]


def halve_kernel(parts, keep, send, total):
    total[...] = functools.reduce(lambda a, b: a + b, [parts[i] for i in range(parts.shape[0])])
    core = lax.axis_index("qb") % 2
    half = keep.shape[0]
    keep[...] = total[pl.ds(pl.multiple_of(core * half, half), half), :]
    send[...] = total[pl.ds(pl.multiple_of((1 - core) * half, half), half), :]


def plane_partners(n_qb):
    return [(dx, dy) for dx in range(2) for dy in range(n_qb // 2)]


def share_kernel(n_qb, keep0, got0, keep1, got1, *refs):
    outs, (sum0, sum1) = refs[:-2], refs[-2:]
    sum0[...] = keep0[...] + got0[...]
    sum1[...] = keep1[...] + got1[...]
    x, y = lax.axis_index("qa") % 2, lax.axis_index("qb") // 2
    size0, size1 = sum0.shape[0] // n_qb, sum1.shape[0] // (n_qb // 2)
    for (dx, dy), out in zip(plane_partners(n_qb), outs):
        place = (x ^ dx) * (n_qb // 2) + (y ^ dy)
        out[:size0] = sum0[pl.ds(pl.multiple_of(place * size0, size0), size0), :]
        if dx == 0:
            out[size0:] = sum1[pl.ds(pl.multiple_of((y ^ dy) * size1, size1), size1), :]


def plane_sum_kernel(n_qb, *refs):
    ins, out = refs[:-1], refs[-1]
    size0 = ins[-1].shape[0]
    out[:size0] = functools.reduce(lambda a, b: a + b, [ref[:size0] for ref in ins])
    out[size0:] = functools.reduce(lambda a, b: a + b, [ref[size0:] for ref in ins[: n_qb // 2]])


def line_sum_kernel(size0, *refs):
    ins, out, held = refs[:-2], refs[-2], refs[-1]
    line = lax.axis_index("qa") // 2
    size1 = ins[0].shape[0] - size0
    for k, ref in enumerate(ins):
        held[line ^ k] = ref[:size0]
        out[pl.ds(size0 + k * size1, size1), :] = ref[size0:]
    out[:size0] = functools.reduce(lambda a, b: a + b, [held[i] for i in range(len(ins))])


def collect_kernel(n_qa, n_qb, size0, *refs):
    ins, out = refs[:-1], refs[-1]
    rows = out.shape[1]
    size1 = rows // (n_qa * n_qb)
    a, b = lax.axis_index("qa"), lax.axis_index("qb")
    for i, ref in enumerate(ins):
        dc, (dx, dy) = i // n_qb, plane_partners(n_qb)[i % n_qb]
        x, y, core = (a % 2) ^ dx, (b // 2) ^ dy, (b % 2) ^ dc
        row = core * (rows // 2) + (x * (n_qb // 2) + y) * size0
        out[0, pl.ds(pl.multiple_of(row, size0), size0), :] = ref[:size0]
        for dz in range(n_qa // 2):
            row = ((((a // 2) ^ dz) * 2 + x) * 2 + core) * (n_qb // 2) + y
            row = pl.multiple_of(row * size1, size1)
            out[1, pl.ds(row, size1), :] = ref[size0 + dz * size1 : size0 + (dz + 1) * size1]


def store_kernel(parts, first, second):
    n, _, slabs, r, d = parts.shape
    for a, out in enumerate((first, second)):
        flat = out.reshape(n * r * slabs, d)
        for s in range(slabs):
            flat[pl.ds(s, n * r, stride=slabs), :] = slab_of_parts(parts, a, s)


def call(kernel, out_shape, inputs, scratch=(), flops=0, far=()):
    def spec(i, x):
        if x.dtype == jnp.int32:
            return pl.BlockSpec(memory_space=pltpu.SMEM)
        return pl.BlockSpec(memory_space=pl.ANY if i in far else pltpu.VMEM)

    outs = jax.tree.map(lambda _: pl.BlockSpec(memory_space=pltpu.VMEM), out_shape)
    size = sum(x.size * 4 for x in inputs) + sum(x.size * 4 for x in jax.tree.leaves(out_shape))
    return pl.pallas_call(
        kernel,
        out_shape=out_shape,
        in_specs=[spec(i, x) for i, x in enumerate(inputs)],
        out_specs=outs,
        scratch_shapes=list(scratch),
        compiler_params=pltpu.CompilerParams(vmem_limit_bytes=VMEM_LIMIT),
        cost_estimate=pl.CostEstimate(flops=flops, bytes_accessed=size, transcendentals=0),
    )(*inputs)


def shape(*dims):
    return jax.ShapeDtypeStruct(dims, F32)


def exchange(x, da, db):
    n_qa, n_qb = lax.axis_size("qa"), lax.axis_size("qb")
    pairs = [(a * n_qb + b, (a ^ da) * n_qb + (b ^ db)) for a in range(n_qa) for b in range(n_qb)]
    return lax.ppermute(x, ("qa", "qb"), pairs)


def summed(grads0, grads1):
    both = jnp.stack([grads0, grads1])
    shares = both.reshape(lax.axis_size("qa") * lax.axis_size("qb"), -1, both.shape[-1])
    share = lax.all_to_all(shares, ("qa", "qb"), 0, 0, tiled=True).sum(0, keepdims=True)
    return lax.all_to_all(jnp.broadcast_to(share, shares.shape), ("qa", "qb"), 0, 0, tiled=True)


def shards(state, costate, gates, targets):
    layout = state.shape
    rows, slabs, d = layout[2:]
    n_qa, n_qb = lax.axis_size("qa"), lax.axis_size("qb")
    scale = (n_qa * n_qb * rows * slabs) ** -0.5
    native = shape(*layout[2:])
    natives = [state.reshape(native.shape), costate.reshape(native.shape)]
    r = rows // n_qb
    parts_qa = shape(n_qa, 2, slabs, rows // n_qa, d)
    held, square = pltpu.VMEM((2, slabs, rows, d), F32), pltpu.VMEM((d, d), F32)
    work = 2 * 2 * 2 * 4 * rows * slabs * d * d
    count = gates.shape[1]
    every = count * d

    if every % (8 * n_qa * n_qb) or r % 8 or n_qa % 2 or n_qb % 2:
        parts_qb = shape(n_qb, 2, slabs, r, d)
        sent = call(functools.partial(apply_kernel, 1, True), parts_qb, [targets, gates, *natives], flops=work)
        parts = lax.all_to_all(sent, "qb", 0, 0, tiled=True)
        grads1 = call(
            functools.partial(gradient_kernel, 1, scale),
            shape(count, d, d), [targets, gates, *natives], [held, square], 8 * work,
        )
        sent = call(functools.partial(apply_kernel, 0, False), parts_qa, [targets, gates, parts], flops=work)
        last = lax.all_to_all(sent, "qa", 0, 0, tiled=True)
        grads0 = call(
            functools.partial(slabs_gradient_kernel, 0, scale),
            shape(count, d, d), [targets, gates, parts], [held, square], 8 * work,
        )
        whole = summed(grads0, grads1)
    else:
        blocks = call(
            functools.partial(first_kernel, 1, n_qb),
            [shape(2, slabs, r, d)] * n_qb,
            [targets, gates, *natives],
            [
                pltpu.VMEM((1, *gates.shape[1:]), F32),
                pltpu.VMEM(native.shape, F32),
                pltpu.VMEM(native.shape, F32),
                square,
                pltpu.SemaphoreType.DMA((3,)),
            ],
            work,
            far=(1, 2, 3),
        )
        blocks = [blocks[0]] + [exchange(blocks[k], 0, k) for k in range(1, n_qb)]
        grads1 = call(
            functools.partial(gradient_kernel, 1, scale),
            shape(count, d, d), [targets, gates, *natives], [held, square], 4 * work,
        )
        part1 = lax.all_to_all(grads1.reshape(n_qa, -1, d), "qa", 0, 0, tiled=True)

        half = shape(every // 2, d)
        sent, keep0, send0 = call(
            functools.partial(second_kernel, 0, n_qb, scale),
            (parts_qa, half, half),
            [targets, gates, *blocks],
            [held, square, pltpu.VMEM((count, d, d), F32)],
            6 * work,
        )
        last = lax.all_to_all(sent, "qa", 0, 0, tiled=True)

        whole1 = every // n_qa
        keep1, send1 = call(
            halve_kernel, (shape(whole1 // 2, d),) * 2, [part1], [pltpu.VMEM((whole1, d), F32)]
        )
        size0, size1 = every // 2 // n_qb, every // (n_qa * n_qb)
        partners = plane_partners(n_qb)
        shares = call(
            functools.partial(share_kernel, n_qb),
            [shape(size0 + (size1 if dx == 0 else 0), d) for dx, _ in partners],
            [keep0, exchange(send0, 0, 1), keep1, exchange(send1, 0, 1)],
            [pltpu.VMEM(half.shape, F32), pltpu.VMEM((whole1 // 2, d), F32)],
        )
        shares = [shares[0]] + [exchange(x, dx, 2 * dy) for x, (dx, dy) in zip(shares[1:], partners[1:])]
        mine = call(functools.partial(plane_sum_kernel, n_qb), shape(size0 + size1, d), shares)
        lines = [mine] + [exchange(mine, 2 * dz, 0) for dz in range(1, n_qa // 2)]
        mine = call(
            functools.partial(line_sum_kernel, size0),
            shape(size0 + size1 * (n_qa // 2), d),
            lines,
            [pltpu.VMEM((n_qa // 2, size0, d), F32)],
        )
        found = [mine] + [exchange(mine, dx, 2 * dy) for dx, dy in partners[1:]]
        found = found + [exchange(x, 0, 1) for x in found]
        whole = call(
            functools.partial(collect_kernel, n_qa, n_qb, size0), shape(gates.shape[0], every, d), found
        )
    first, second = call(store_kernel, (native, native), [last])
    return first.reshape(layout), second.reshape(layout), whole.reshape(gates.shape)


def solution(mesh):
    in_specs = (P("qa", "qb", None, None, None), P("qa", "qb", None, None, None), P(), P())
    out_specs = (P("qa", "qb", None, None, None), P("qa", "qb", None, None, None), P())
    return jax.shard_map(shards, mesh=mesh, in_specs=in_specs, out_specs=out_specs, check_vma=False)
```

time: 102 us -> 75.7 us (0.74)
  waiting for transfers between devices: 62.2 us -> 30.3 us
  starting transfers between devices: 17.1 us -> 25.6 us
  local copies, waits for them, and re-layouts: 5.45 us -> 3.8 us
  Pallas kernels: 15.5 us -> 14.3 us
    all_to_all x3 -> x1, waiting for transfers between devices: 36.2 us -> 1.67 us  [shards(): part1 = lax.all_to_all(grads1.reshape(n_qa, -1, d), 'qa', 0, 0, tiled=True)]
    ppermute x0 -> x18, waiting for transfers between devices: none -> 28.7 us  [exchange(): return lax.ppermute(x, ('qa', 'qb'), pairs)]
    all_to_all x1, waiting for transfers between devices: 26 us -> 0.01 us  [shards(): last = lax.all_to_all(sent, 'qa', 0, 0, tiled=True)]
    ppermute x0 -> x18, starting transfers between devices: none -> 15.3 us  [exchange(): return lax.ppermute(x, ('qa', 'qb'), pairs)]
    all_to_all x3 -> x1, starting transfers between devices: 13.5 us -> 6.14 us  [shards(): part1 = lax.all_to_all(grads1.reshape(n_qa, -1, d), 'qa', 0, 0, tiled=True)]
    pallas_call x5 -> x9, Pallas kernels: 15.5 us -> 14.3 us  [call(): pl.pallas_call(kernel, out_shape=out_shape, in_specs=[spec(i, x) for i, x...]
    unnamed x15 -> x10, local copies, waits for them, and re-layouts: 4.6 us -> 3.8 us
  transfers between devices with their start and end apart: 4 -> 20, of which waited for: 4 -> 12; matrix products, arithmetic and copies ran while one was open for 0% -> 0% of each run, Pallas kernels for 9% -> 15%
where the time goes in v2:
time: 75.7 us; the launch traced here: 74.8 us
  waiting for transfers between devices  30.3 us (40%)
  starting transfers between devices  25.6 us (34%)
  Pallas kernels  14.3 us (19%)
  local copies, waits for them, and re-layouts  3.8 us (5%)
    ppermute x18, waiting for transfers between devices, exchange(): return lax.ppermute(x, ('qa', 'qb'), pairs)  28.7 us
    ppermute x18, starting transfers between devices, exchange(): return lax.ppermute(x, ('qa', 'qb'), pairs)  15.3 us
    pallas_call x9, Pallas kernels, call(): pl.pallas_call(kernel, out_shape=out_shape, in_specs=[spec(i, x) for i, x...  14.3 us
    all_to_all x1, starting transfers between devices, shards(): part1 = lax.all_to_all(grads1.reshape(n_qa, -1, d), 'qa', 0, 0, tiled=True)  6.14 us
    all_to_all x1, starting transfers between devices, shards(): last = lax.all_to_all(sent, 'qa', 0, 0, tiled=True)  4.17 us
    unnamed x10, local copies, waits for them, and re-layouts  3.8 us
    all_to_all x1, waiting for transfers between devices, shards(): part1 = lax.all_to_all(grads1.reshape(n_qa, -1, d), 'qa', 0, 0, tiled=True)  1.67 us
  transfers between devices with their start and end apart: 20, of which 12 were waited for; matrix products, arithmetic and copies ran while one was open for 0% of the time, Pallas kernels for 15%

profile of v2, /device:TPU:0, one launch (start us, length us, event | category | flops | bytes accessed | tf_op | source)
XLA Modules:
  0.0 74.8 jit_solution(12542398973548754692)
XLA Ops:
  0.6 0.7 copy-done.4
  1.3 1.0 %copy-done = f32[1,1,128,8,128]{4,3,2,1,0:T(8,128)S(1)} copy-done((f32[1,1,128,8,128]{4,3,2,1,0:T(8,128)S(1)}, f32[1,1,128,8,128]{4,3,2,1,0:T(8,128)}, u32[]{:S(2)}) %copy-start) | copy-done | bytes 524312
  2.4 1.0 %copy-done.1 = f32[1,1,128,8,128]{4,3,2,1,0:T(8,128)S(1)} copy-done((f32[1,1,128,8,128]{4,3,2,1,0:T(8,128)S(1)}, f32[1,1,128,8,128]{4,3,2,1,0:T(8,128)}, u32[]{:S(2)}) %copy-start.1) | copy-done | bytes 524312
  3.4 1.0 %copy-done.2 = f32[2,4,128,128]{3,2,1,0:T(8,128)S(1)} copy-done((f32[2,4,128,128]{3,2,1,0:T(8,128)S(1)}, f32[2,4,128,128]{3,2,1,0:T(8,128)}, u32[]{:S(2)}) %copy-start.2) | copy-done | bytes 524312
  4.4 2.1 %shard_map.67 = (f32[2,8,32,128]{3,2,1,0:T(8,128)S(1)}, f32[2,8,32,128]{3,2,1,0:T(8,128)S(1)}, f32[2,8,32,128]{3,2,1,0:T(8,128)S(1)}, f32[2,8,32,128]{3,2,1,0:T(8,128)S(1)}) custom-call(s32[2,4]{1,0:T(2,128)S(1)} %copy-done.4, f32[2,4,128,128]{3,2,1,0:T(8,128)S(1)} %copy-done.2, f32[128,8,128]{2,1,0:T(8,128)S(1)} %bitcast.6, f32[128,8,128]{2,1,0:T(8,128)S(1)} %bitcast.8), custom_call_target="tpu_custom_call" | custom-call | flops 536870912 | bytes 2621472 | tf_op jit(solution)/shard_map/pallas_call | solution.py:304
  6.6 0.5 collective-permute-start
  7.1 2.6 %collective-permute-start.1 = (f32[2,8,32,128]{3,2,1,0:T(8,128)S(1)}, f32[2,8,32,128]{3,2,1,0:T(8,128)S(1)}, u32[]{:S(2)}, u32[]{:S(2)}) collective-permute-start(f32[2,8,32,128]{3,2,1,0:T(8,128)S(1)} %get-tuple-element.20), channel_id=1, source_target_pairs={{0,2},{1,3},{2,0},{3,1},{4,6},{5,7},{6,4},{7,5},{8,10},{9,11},{10,... | collective-permute-start | bytes 786440 | tf_op jit(solution)/shard_map/ppermute | solution.py:322
  9.8 4.1 %shard_map.70 = f32[4,128,128]{2,1,0:T(8,128)} custom-call(s32[2,4]{1,0:T(2,128)S(1)} %copy-done.4, f32[2,4,128,128]{3,2,1,0:T(8,128)S(1)} %copy-done.2, f32[128,8,128]{2,1,0:T(8,128)S(1)} %bitcast.7, f32[128,8,128]{2,1,0:T(8,128)S(1)} %bitcast.9), custom_call_target="tpu_custom_call" | custom-call | flops 2147483648 | bytes 1835040 | tf_op jit(solution)/shard_map/pallas_call | solution.py:304
  13.9 6.1 %all-to-all-start.1 = ((f32[8,64,128]{2,1,0:T(8,128)}), f32[8,64,128]{2,1,0:T(8,128)S(1)}, u32[]{:S(2)}, u32[]{:S(2)}) async-start(f32[8,64,128]{2,1,0:T(8,128)} %bitcast.4), calls=%async_computation.1 | async-start | bytes 524288 | tf_op jit(solution)/shard_map/all_to_all | solution.py:381
  20.0 1.9 %collective-permute-done.2.refs_3_ = f32[2,8,32,128]{3,2,1,0:T(8,128)S(1)} collective-permute-done((f32[2,8,32,128]{3,2,1,0:T(8,128)S(1)}, f32[2,8,32,128]{3,2,1,0:T(8,128)S(1)}, u32[]{:S(2)}, u32[]{:S(2)}) %collective-permute-start.2) | collective-permute-done | bytes 262176 | tf_op jit(solution)/shard_map/ppermute | solution.py:322
  21.9 5.9 %shard_map.68 = (f32[8,2,8,16,128]{4,3,2,1,0:T(8,128)}, f32[256,128]{1,0:T(8,128)S(1)}, f32[256,128]{1,0:T(8,128)S(1)}) custom-call(s32[2,4]{1,0:T(2,128)S(1)} %copy-done.4, f32[2,4,128,128]{3,2,1,0:T(8,128)S(1)} %copy-done.3, f32[2,8,32,128]{3,2,1,0:T(8,128)S(1)} %get-tuple-element.18.refs_0_, f32[2,8,32,128]{3,2,1,0:T(8,128)S(1)} %collective-permute-done.refs_1_, ...), custom_call_target="tpu_custom_call" | custom-call | flops 3221225472 | bytes 2883616 | tf_op jit(solution)/shard_map/pallas_call | solution.py:304
  27.8 1.7 %all-to-all-done.1.parts = f32[8,64,128]{2,1,0:T(8,128)S(1)} async-done(((f32[8,64,128]{2,1,0:T(8,128)}), f32[8,64,128]{2,1,0:T(8,128)S(1)}, u32[]{:S(2)}, u32[]{:S(2)}) %all-to-all-start.1) | async-done | bytes 262176 | tf_op jit(solution)/shard_map/all_to_all | solution.py:381
  29.5 4.2 %all-to-all-start = ((f32[8,2,8,16,128]{4,3,2,1,0:T(8,128)}), f32[8,2,8,16,128]{4,3,2,1,0:T(8,128)S(1)}, u32[]{:S(2)}, u32[]{:S(2)}) async-start(f32[8,2,8,16,128]{4,3,2,1,0:T(8,128)} %get-tuple-element.22), calls=%async_computation | async-start | bytes 2097152 | tf_op jit(solution)/shard_map/all_to_all | solution.py:391
  33.9 0.3 collective-permute-start.4
  34.2 0.8 %collective-permute-done.3.got0 = f32[256,128]{1,0:T(8,128)S(1)} collective-permute-done((f32[256,128]{1,0:T(8,128)S(1)}, f32[256,128]{1,0:T(8,128)S(1)}, u32[]{:S(2)}, u32[]{:S(2)}) %collective-permute-start.3) | collective-permute-done | bytes 131104 | tf_op jit(solution)/shard_map/ppermute | solution.py:322
  35.2 1.6 %collective-permute-start.5 = (f32[80,128]{1,0:T(8,128)S(1)}, f32[80,128]{1,0:T(8,128)S(1)}, u32[]{:S(2)}, u32[]{:S(2)}) collective-permute-start(f32[80,128]{1,0:T(8,128)S(1)} %get-tuple-element.30), channel_id=1, source_target_pairs={{0,2},{1,3},{2,0},{3,1},{4,6},{5,7},{6,4},{7,5},{8,10},{9,11},{10,... | collective-permute-start | bytes 122888 | tf_op jit(solution)/shard_map/ppermute | solution.py:322
  36.8 1.9 %collective-permute-start.6 = (f32[64,128]{1,0:T(8,128)S(1)}, f32[64,128]{1,0:T(8,128)S(1)}, u32[]{:S(2)}, u32[]{:S(2)}) collective-permute-start(f32[64,128]{1,0:T(8,128)S(1)} %get-tuple-element.31), channel_id=1, source_target_pairs={{0,4},{1,5},{2,6},{3,7},{4,0},{5,1},{6,2},{7,3},{8,12},{9,13},{10,... | collective-permute-start | bytes 98312 | tf_op jit(solution)/shard_map/ppermute | solution.py:322
  38.8 5.8 %collective-permute-done.6.refs_2_ = f32[64,128]{1,0:T(8,128)S(1)} collective-permute-done((f32[64,128]{1,0:T(8,128)S(1)}, f32[64,128]{1,0:T(8,128)S(1)}, u32[]{:S(2)}, u32[]{:S(2)}) %collective-permute-start.6) | collective-permute-done | bytes 32800 | tf_op jit(solution)/shard_map/ppermute | solution.py:322
  44.5 1.9 %collective-permute-done.7.refs_3_ = f32[64,128]{1,0:T(8,128)S(1)} collective-permute-done((f32[64,128]{1,0:T(8,128)S(1)}, f32[64,128]{1,0:T(8,128)S(1)}, u32[]{:S(2)}, u32[]{:S(2)}) %collective-permute-start.7) | collective-permute-done | bytes 32800 | tf_op jit(solution)/shard_map/ppermute | solution.py:322
  46.5 1.7 %collective-permute-start.9 = (f32[80,128]{1,0:T(8,128)S(1)}, f32[80,128]{1,0:T(8,128)S(1)}, u32[]{:S(2)}, u32[]{:S(2)}) collective-permute-start(f32[80,128]{1,0:T(8,128)S(1)} %shard_map.73.refs_0_), channel_id=1, source_target_pairs={{0,16},{1,17},{2,18},{3,19},{4,20},{5,21},{6,22},{7,23},{8,24},{9,... | collective-permute-start | bytes 122888 | tf_op jit(solution)/shard_map/ppermute | solution.py:322
  48.3 2.6 %collective-permute-start.10 = (f32[80,128]{1,0:T(8,128)S(1)}, f32[80,128]{1,0:T(8,128)S(1)}, u32[]{:S(2)}, u32[]{:S(2)}) collective-permute-start(f32[80,128]{1,0:T(8,128)S(1)} %shard_map.73.refs_0_), channel_id=1, source_target_pairs={{0,24},{1,25},{2,26},{3,27},{4,28},{5,29},{6,30},{7,31},{8,16},{9,... | collective-permute-start | bytes 122888 | tf_op jit(solution)/shard_map/ppermute | solution.py:322
  50.9 3.0 %collective-permute-done.8.refs_1_ = f32[80,128]{1,0:T(8,128)S(1)} collective-permute-done((f32[80,128]{1,0:T(8,128)S(1)}, f32[80,128]{1,0:T(8,128)S(1)}, u32[]{:S(2)}, u32[]{:S(2)}) %collective-permute-start.8) | collective-permute-done | bytes 40992 | tf_op jit(solution)/shard_map/ppermute | solution.py:322
  53.9 9.4 %collective-permute-done.9.refs_2_ = f32[80,128]{1,0:T(8,128)S(1)} collective-permute-done((f32[80,128]{1,0:T(8,128)S(1)}, f32[80,128]{1,0:T(8,128)S(1)}, u32[]{:S(2)}, u32[]{:S(2)}) %collective-permute-start.9) | collective-permute-done | bytes 40992 | tf_op jit(solution)/shard_map/ppermute | solution.py:322
  63.3 1.6 %collective-permute-start.11 = (f32[128,128]{1,0:T(8,128)S(1)}, f32[128,128]{1,0:T(8,128)S(1)}, u32[]{:S(2)}, u32[]{:S(2)}) collective-permute-start(f32[128,128]{1,0:T(8,128)S(1)} %shard_map.74.refs_0_), channel_id=1, source_target_pairs={{0,2},{1,3},{2,0},{3,1},{4,6},{5,7},{6,4},{7,5},{8,10},{9,11},{10,... | collective-permute-start | bytes 196616 | tf_op jit(solution)/shard_map/ppermute | solution.py:322
  64.9 1.4 %collective-permute-start.12 = (f32[128,128]{1,0:T(8,128)S(1)}, f32[128,128]{1,0:T(8,128)S(1)}, u32[]{:S(2)}, u32[]{:S(2)}) collective-permute-start(f32[128,128]{1,0:T(8,128)S(1)} %shard_map.74.refs_0_), channel_id=1, source_target_pairs={{0,4},{1,5},{2,6},{3,7},{4,0},{5,1},{6,2},{7,3},{8,12},{9,13},{10,... | collective-permute-start | bytes 196616 | tf_op jit(solution)/shard_map/ppermute | solution.py:322
  66.3 0.5 collective-permute-start.13
  66.8 0.8 %collective-permute-done.11.refs_1_ = f32[128,128]{1,0:T(8,128)S(1)} collective-permute-done((f32[128,128]{1,0:T(8,128)S(1)}, f32[128,128]{1,0:T(8,128)S(1)}, u32[]{:S(2)}, u32[]{:S(2)}) %collective-permute-start.11) | collective-permute-done | bytes 65568 | tf_op jit(solution)/shard_map/ppermute | solution.py:322
  67.6 1.6 %collective-permute-done.12.refs_2_ = f32[128,128]{1,0:T(8,128)S(1)} collective-permute-done((f32[128,128]{1,0:T(8,128)S(1)}, f32[128,128]{1,0:T(8,128)S(1)}, u32[]{:S(2)}, u32[]{:S(2)}) %collective-permute-start.12) | collective-permute-done | bytes 65568 | tf_op jit(solution)/shard_map/ppermute | solution.py:322
  69.2 2.3 %collective-permute-done.13.refs_3_ = f32[128,128]{1,0:T(8,128)S(1)} collective-permute-done((f32[128,128]{1,0:T(8,128)S(1)}, f32[128,128]{1,0:T(8,128)S(1)}, u32[]{:S(2)}, u32[]{:S(2)}) %collective-permute-start.13) | collective-permute-done | bytes 65568 | tf_op jit(solution)/shard_map/ppermute | solution.py:322
  71.5 1.2 %collective-permute-done.17.refs_7_ = f32[128,128]{1,0:T(8,128)S(1)} collective-permute-done((f32[128,128]{1,0:T(8,128)S(1)}, f32[128,128]{1,0:T(8,128)S(1)}, u32[]{:S(2)}, u32[]{:S(2)}) %collective-permute-start.17) | collective-permute-done | bytes 65568 | tf_op jit(solution)/shard_map/ppermute | solution.py:322
  72.7 0.9 %shard_map.75 = f32[2,512,128]{2,1,0:T(8,128)} custom-call(f32[128,128]{1,0:T(8,128)S(1)} %shard_map.74.refs_0_, f32[128,128]{1,0:T(8,128)S(1)} %collective-permute-done.11.refs_1_, f32[128,128]{1,0:T(8,128)S(1)} %collective-permute-done.12.refs_2_, f32[128,128]{1,0:T(8,128)S(1)} %collective-permute-done.13.refs_3_, ...), custom_call_target="tpu_custom_call" | custom-call | bytes 1048576 | tf_op jit(solution)/shard_map/pallas_call | solution.py:304
  73.6 1.2 %shard_map.69 = (f32[128,8,128]{2,1,0:T(8,128)}, f32[128,8,128]{2,1,0:T(8,128)}) custom-call(f32[8,2,8,16,128]{4,3,2,1,0:T(8,128)S(1)} %all-to-all-done.parts), custom_call_target="tpu_custom_call" | custom-call | bytes 2097152 | tf_op jit(solution)/shard_map/pallas_call | solution.py:304
  (27 shorter events, 0.8 us)
Async XLA Ops:
  0.6 0.7 copy-start.4
  1.3 1.0 %copy-start = (f32[1,1,128,8,128]{4,3,2,1,0:T(8,128)S(1)}, f32[1,1,128,8,128]{4,3,2,1,0:T(8,128)}, u32[]{:S(2)}) copy-start(f32[1,1,128,8,128]{4,3,2,1,0:T(8,128)} %param.4) | copy-start | bytes 1572868
  2.4 1.0 %copy-start.1 = (f32[1,1,128,8,128]{4,3,2,1,0:T(8,128)S(1)}, f32[1,1,128,8,128]{4,3,2,1,0:T(8,128)}, u32[]{:S(2)}) copy-start(f32[1,1,128,8,128]{4,3,2,1,0:T(8,128)} %param.5) | copy-start | bytes 1572868
  3.4 1.0 %copy-start.2 = (f32[2,4,128,128]{3,2,1,0:T(8,128)S(1)}, f32[2,4,128,128]{3,2,1,0:T(8,128)}, u32[]{:S(2)}) copy-start(f32[2,4,128,128]{3,2,1,0:T(8,128)} %gates.5) | copy-start | bytes 1572868
  6.6 13.5 %collective-permute-start = (f32[2,8,32,128]{3,2,1,0:T(8,128)S(1)}, f32[2,8,32,128]{3,2,1,0:T(8,128)S(1)}, u32[]{:S(2)}, u32[]{:S(2)}) collective-permute-start(f32[2,8,32,128]{3,2,1,0:T(8,128)S(1)} %get-tuple-element.19), channel_id=1, source_target_pairs={{0,1},{1,0},{2,3},{3,2},{4,5},{5,4},{6,7},{7,6},{8,9},{9,8},{10,11... | collective-permute-start | bytes 786440 | tf_op jit(solution)/shard_map/ppermute | solution.py:322
  7.1 12.9 %collective-permute-start.1 = (f32[2,8,32,128]{3,2,1,0:T(8,128)S(1)}, f32[2,8,32,128]{3,2,1,0:T(8,128)S(1)}, u32[]{:S(2)}, u32[]{:S(2)}) collective-permute-start(f32[2,8,32,128]{3,2,1,0:T(8,128)S(1)} %get-tuple-element.20), channel_id=1, source_target_pairs={{0,2},{1,3},{2,0},{3,1},{4,6},{5,7},{6,4},{7,5},{8,10},{9,11},{10,... | collective-permute-start | bytes 786440 | tf_op jit(solution)/shard_map/ppermute | solution.py:322
  9.7 12.3 %collective-permute-start.2 = (f32[2,8,32,128]{3,2,1,0:T(8,128)S(1)}, f32[2,8,32,128]{3,2,1,0:T(8,128)S(1)}, u32[]{:S(2)}, u32[]{:S(2)}) collective-permute-start(f32[2,8,32,128]{3,2,1,0:T(8,128)S(1)} %get-tuple-element.21), channel_id=1, source_target_pairs={{0,3},{1,2},{2,1},{3,0},{4,7},{5,6},{6,5},{7,4},{8,11},{9,10},{10,... | collective-permute-start | bytes 786440 | tf_op jit(solution)/shard_map/ppermute | solution.py:322
  13.9 8.1 %copy-start.3 = (f32[2,4,128,128]{3,2,1,0:T(8,128)S(1)}, f32[2,4,128,128]{3,2,1,0:T(8,128)}, u32[]{:S(2)}) copy-start(f32[2,4,128,128]{3,2,1,0:T(8,128)} %gates.5) | copy-start | bytes 1572868
  13.9 15.6 %all-to-all-start.1 = ((f32[8,64,128]{2,1,0:T(8,128)}), f32[8,64,128]{2,1,0:T(8,128)S(1)}, u32[]{:S(2)}, u32[]{:S(2)}) async-start(f32[8,64,128]{2,1,0:T(8,128)} %bitcast.4), calls=%async_computation.1 | async-start | bytes 524288 | tf_op jit(solution)/shard_map/all_to_all | solution.py:381
  29.5 44.1 %all-to-all-start = ((f32[8,2,8,16,128]{4,3,2,1,0:T(8,128)}), f32[8,2,8,16,128]{4,3,2,1,0:T(8,128)S(1)}, u32[]{:S(2)}, u32[]{:S(2)}) async-start(f32[8,2,8,16,128]{4,3,2,1,0:T(8,128)} %get-tuple-element.22), calls=%async_computation | async-start | bytes 2097152 | tf_op jit(solution)/shard_map/all_to_all | solution.py:391
  33.6 1.3 %collective-permute-start.3 = (f32[256,128]{1,0:T(8,128)S(1)}, f32[256,128]{1,0:T(8,128)S(1)}, u32[]{:S(2)}, u32[]{:S(2)}) collective-permute-start(f32[256,128]{1,0:T(8,128)S(1)} %get-tuple-element.26), channel_id=1, source_target_pairs={{0,1},{1,0},{2,3},{3,2},{4,5},{5,4},{6,7},{7,6},{8,9},{9,8},{10,11... | collective-permute-start | bytes 393224 | tf_op jit(solution)/shard_map/ppermute | solution.py:322
  33.9 1.2 %collective-permute-start.4 = (f32[32,128]{1,0:T(8,128)S(1)}, f32[32,128]{1,0:T(8,128)S(1)}, u32[]{:S(2)}, u32[]{:S(2)}) collective-permute-start(f32[32,128]{1,0:T(8,128)S(1)} %get-tuple-element.28), channel_id=1, source_target_pairs={{0,1},{1,0},{2,3},{3,2},{4,5},{5,4},{6,7},{7,6},{8,9},{9,8},{10,11... | collective-permute-start | bytes 49160 | tf_op jit(solution)/shard_map/ppermute | solution.py:322
  35.2 11.2 %collective-permute-start.5 = (f32[80,128]{1,0:T(8,128)S(1)}, f32[80,128]{1,0:T(8,128)S(1)}, u32[]{:S(2)}, u32[]{:S(2)}) collective-permute-start(f32[80,128]{1,0:T(8,128)S(1)} %get-tuple-element.30), channel_id=1, source_target_pairs={{0,2},{1,3},{2,0},{3,1},{4,6},{5,7},{6,4},{7,5},{8,10},{9,11},{10,... | collective-permute-start | bytes 122888 | tf_op jit(solution)/shard_map/ppermute | solution.py:322
  36.8 7.7 %collective-permute-start.6 = (f32[64,128]{1,0:T(8,128)S(1)}, f32[64,128]{1,0:T(8,128)S(1)}, u32[]{:S(2)}, u32[]{:S(2)}) collective-permute-start(f32[64,128]{1,0:T(8,128)S(1)} %get-tuple-element.31), channel_id=1, source_target_pairs={{0,4},{1,5},{2,6},{3,7},{4,0},{5,1},{6,2},{7,3},{8,12},{9,13},{10,... | collective-permute-start | bytes 98312 | tf_op jit(solution)/shard_map/ppermute | solution.py:322
  38.7 7.7 %collective-permute-start.7 = (f32[64,128]{1,0:T(8,128)S(1)}, f32[64,128]{1,0:T(8,128)S(1)}, u32[]{:S(2)}, u32[]{:S(2)}) collective-permute-start(f32[64,128]{1,0:T(8,128)S(1)} %get-tuple-element.32), channel_id=1, source_target_pairs={{0,6},{1,7},{2,4},{3,5},{4,2},{5,3},{6,0},{7,1},{8,14},{9,15},{10,... | collective-permute-start | bytes 98312 | tf_op jit(solution)/shard_map/ppermute | solution.py:322
  46.5 7.4 %collective-permute-start.8 = (f32[80,128]{1,0:T(8,128)S(1)}, f32[80,128]{1,0:T(8,128)S(1)}, u32[]{:S(2)}, u32[]{:S(2)}) collective-permute-start(f32[80,128]{1,0:T(8,128)S(1)} %shard_map.73.refs_0_), channel_id=1, source_target_pairs={{0,8},{1,9},{2,10},{3,11},{4,12},{5,13},{6,14},{7,15},{8,0},{9,1},... | collective-permute-start | bytes 122888 | tf_op jit(solution)/shard_map/ppermute | solution.py:322
  46.5 16.7 %collective-permute-start.9 = (f32[80,128]{1,0:T(8,128)S(1)}, f32[80,128]{1,0:T(8,128)S(1)}, u32[]{:S(2)}, u32[]{:S(2)}) collective-permute-start(f32[80,128]{1,0:T(8,128)S(1)} %shard_map.73.refs_0_), channel_id=1, source_target_pairs={{0,16},{1,17},{2,18},{3,19},{4,20},{5,21},{6,22},{7,23},{8,24},{9,... | collective-permute-start | bytes 122888 | tf_op jit(solution)/shard_map/ppermute | solution.py:322
  48.3 14.9 %collective-permute-start.10 = (f32[80,128]{1,0:T(8,128)S(1)}, f32[80,128]{1,0:T(8,128)S(1)}, u32[]{:S(2)}, u32[]{:S(2)}) collective-permute-start(f32[80,128]{1,0:T(8,128)S(1)} %shard_map.73.refs_0_), channel_id=1, source_target_pairs={{0,24},{1,25},{2,26},{3,27},{4,28},{5,29},{6,30},{7,31},{8,16},{9,... | collective-permute-start | bytes 122888 | tf_op jit(solution)/shard_map/ppermute | solution.py:322
  63.3 4.3 %collective-permute-start.11 = (f32[128,128]{1,0:T(8,128)S(1)}, f32[128,128]{1,0:T(8,128)S(1)}, u32[]{:S(2)}, u32[]{:S(2)}) collective-permute-start(f32[128,128]{1,0:T(8,128)S(1)} %shard_map.74.refs_0_), channel_id=1, source_target_pairs={{0,2},{1,3},{2,0},{3,1},{4,6},{5,7},{6,4},{7,5},{8,10},{9,11},{10,... | collective-permute-start | bytes 196616 | tf_op jit(solution)/shard_map/ppermute | solution.py:322
  64.9 4.3 %collective-permute-start.12 = (f32[128,128]{1,0:T(8,128)S(1)}, f32[128,128]{1,0:T(8,128)S(1)}, u32[]{:S(2)}, u32[]{:S(2)}) collective-permute-start(f32[128,128]{1,0:T(8,128)S(1)} %shard_map.74.refs_0_), channel_id=1, source_target_pairs={{0,4},{1,5},{2,6},{3,7},{4,0},{5,1},{6,2},{7,3},{8,12},{9,13},{10,... | collective-permute-start | bytes 196616 | tf_op jit(solution)/shard_map/ppermute | solution.py:322
  66.3 5.2 %collective-permute-start.13 = (f32[128,128]{1,0:T(8,128)S(1)}, f32[128,128]{1,0:T(8,128)S(1)}, u32[]{:S(2)}, u32[]{:S(2)}) collective-permute-start(f32[128,128]{1,0:T(8,128)S(1)} %shard_map.74.refs_0_), channel_id=1, source_target_pairs={{0,6},{1,7},{2,4},{3,5},{4,2},{5,3},{6,0},{7,1},{8,14},{9,15},{10,... | collective-permute-start | bytes 196616 | tf_op jit(solution)/shard_map/ppermute | solution.py:322
  66.8 4.6 %collective-permute-start.14 = (f32[128,128]{1,0:T(8,128)S(1)}, f32[128,128]{1,0:T(8,128)S(1)}, u32[]{:S(2)}, u32[]{:S(2)}) collective-permute-start(f32[128,128]{1,0:T(8,128)S(1)} %shard_map.74.refs_0_), channel_id=1, source_target_pairs={{0,1},{1,0},{2,3},{3,2},{4,5},{5,4},{6,7},{7,6},{8,9},{9,8},{10,11... | collective-permute-start | bytes 196616 | tf_op jit(solution)/shard_map/ppermute | solution.py:322
  67.6 3.9 %collective-permute-start.15 = (f32[128,128]{1,0:T(8,128)S(1)}, f32[128,128]{1,0:T(8,128)S(1)}, u32[]{:S(2)}, u32[]{:S(2)}) collective-permute-start(f32[128,128]{1,0:T(8,128)S(1)} %collective-permute-done.11.refs_1_), channel_id=1, source_target_pairs={{0,1},{1,0},{2,3},{3,2},{4,5},{5,4},{6,7},{7,6},{8,9},{9,8},{10,11... | collective-permute-start | bytes 196616 | tf_op jit(solution)/shard_map/ppermute | solution.py:322
  69.1 2.3 %collective-permute-start.16 = (f32[128,128]{1,0:T(8,128)S(1)}, f32[128,128]{1,0:T(8,128)S(1)}, u32[]{:S(2)}, u32[]{:S(2)}) collective-permute-start(f32[128,128]{1,0:T(8,128)S(1)} %collective-permute-done.12.refs_2_), channel_id=1, source_target_pairs={{0,1},{1,0},{2,3},{3,2},{4,5},{5,4},{6,7},{7,6},{8,9},{9,8},{10,11... | collective-permute-start | bytes 196616 | tf_op jit(solution)/shard_map/ppermute | solution.py:322
  71.4 1.3 %collective-permute-start.17 = (f32[128,128]{1,0:T(8,128)S(1)}, f32[128,128]{1,0:T(8,128)S(1)}, u32[]{:S(2)}, u32[]{:S(2)}) collective-permute-start(f32[128,128]{1,0:T(8,128)S(1)} %collective-permute-done.13.refs_3_), channel_id=1, source_target_pairs={{0,1},{1,0},{2,3},{3,2},{4,5},{5,4},{6,7},{7,6},{8,9},{9,8},{10,11... | collective-permute-start | bytes 196616 | tf_op jit(solution)/shard_map/ppermute | solution.py:322

commit v3 on v1

v3 whole, which is shorter than its diff:
```python
import functools

import jax
import jax.numpy as jnp
from jax import lax
from jax.experimental import pallas as pl
from jax.experimental.pallas import tpu as pltpu
from jax.sharding import PartitionSpec as P

F32, BF16 = jnp.float32, jnp.bfloat16
K0COST = 50
PARTS_DUE = 'plane'
WINDOWS = [(0, 'plane'), (1, ('line', 1)), (1, ('line', 2)), ('plane', ('back', 0)), (('line', 1), ('back', 1)), (0, ('line', 1)), (1, ('line', 2))]
VMEM_LIMIT = 16 * 1024 * 1024


def split(x):
    high = x.astype(BF16)
    return high, (x - high.astype(F32)).astype(BF16)


def dot(a, b, dims=((1,), (0,))):
    return lax.dot_general(a, b, (dims, ((), ())), preferred_element_type=F32)


def right_factor(u):
    high, low = split(u)
    row = jnp.concatenate([high, low], axis=1)
    return jnp.concatenate([row, row], axis=0)


def left_factor(u):
    return stack_factor(jnp.transpose(u))


def stack_factor(u):
    high, low = split(u)
    return jnp.concatenate(
        [jnp.concatenate([high, high], axis=1), jnp.concatenate([low, low], axis=1)], axis=0
    )


def times_right(x, factor):
    d = x.shape[1]
    r = dot(jnp.concatenate(split(x), axis=1), factor)
    return r[:, :d] + r[:, d:]


def times_left(factor, x):
    d = x.shape[0]
    r = dot(factor, jnp.concatenate(split(x), axis=0))
    return r[:d] + r[d:]


def matmul(a, b):
    return times_right(a, right_factor(b))


def slab_of_native(ref, s):
    rows, slabs, lanes = ref.shape
    return ref.reshape(rows * slabs, lanes)[pl.ds(s, rows, stride=slabs), :]


def slab_of_parts(ref, a, s):
    n, _, _, r, lanes = ref.shape
    return ref[:, a, s].reshape(n * r, lanes)


def products(targets, gates, block, at):
    d = gates.shape[-1]
    eye = (
        lax.broadcasted_iota(jnp.int32, (d, d), 0) == lax.broadcasted_iota(jnp.int32, (d, d), 1)
    ).astype(F32)
    last = gates.shape[1] - 1
    u = gates[at, last]
    low_turn = targets[block, last] == 0
    low, mid = jnp.where(low_turn, u, eye), jnp.where(low_turn, eye, u)
    for g in range(last - 1, -1, -1):
        both = matmul(jnp.concatenate([low, mid], axis=0), gates[at, g])
        low_turn = targets[block, g] == 0
        low, mid = jnp.where(low_turn, both[:d], low), jnp.where(low_turn, mid, both[d:])
    return low, mid


def apply_kernel(block, native, targets, gates, *refs):
    out = refs[-1]
    n, _, slabs, r, d = out.shape
    low, mid = products(targets, gates, block, block)
    low, mid = right_factor(low), left_factor(mid)
    for s in range(slabs):
        if native:
            x, y = slab_of_native(refs[0], s), slab_of_native(refs[1], s)
        else:
            x, y = slab_of_parts(refs[0], 0, s), slab_of_parts(refs[0], 1, s)
        z = times_right(jnp.concatenate([x, y], axis=0), low)
        z = times_left(mid, jnp.concatenate([z[: n * r], z[n * r :]], axis=1))
        out[:, 0, s] = z[:, :d].reshape(n, r, d)
        out[:, 1, s] = z[:, d:].reshape(n, r, d)


def fuse(x):
    return jnp.concatenate(split(x), axis=-1)


def stacked(x):
    d = x.shape[-1] // 2
    return jnp.concatenate([x[:, :d], x[:, d:]], axis=0)


def same_run(targets, block, g):
    return targets[block, g] == targets[block, g + 1]


def identity(d):
    rows, columns = (lax.broadcasted_iota(jnp.int32, (d, d), i) for i in range(2))
    return (rows == columns).astype(F32)


def chains(targets, gates, right, left, made, kept):
    blocks, count, d, _ = gates.shape
    eye = identity(d)
    for block in range(blocks):
        left[block, count] = left_factor(eye)
        made[block] = eye
    made[blocks] = eye
    made[blocks + 1] = eye

    def step(i, _):
        g = count - 1 - i
        for block in range(blocks):
            u = gates[block, g]
            after = jnp.minimum(g + 1, count - 1)
            going = jnp.logical_and(i > 0, targets[block, g] == targets[block, after])
            p = jnp.where(going, matmul(made[block], u), u)
            made[block] = p
            if block:
                right[block, g] = right_factor(p)
                left[block, g] = left_factor(p)
            else:
                kept[g] = p
        both = made[pl.ds(blocks, 2)].reshape(2 * d, d)
        both = matmul(both, gates[0, g])
        low_turn = targets[0, g] == 0
        made[blocks] = jnp.where(low_turn, both[:d], made[blocks])
        made[blocks + 1] = jnp.where(low_turn, made[blocks + 1], both[d:])
        return _

    lax.fori_loop(0, count, step, 0)


def block_kernel(block, at, finish_from, scale, targets, right, left, held, inner, grads, ready=None):
    _, slabs, rows, d = held.shape
    d = d // 2
    count = grads.shape[0]

    def contract_low():
        y, x = (held[a].reshape(slabs * rows, 2 * d) for a in (1, 0))
        return dot(y, x, ((0,), (0,)))

    def contract_mid():
        y, x = (
            jnp.concatenate([stacked(held[a, s]) for s in range(slabs)], axis=1) for a in (1, 0)
        )
        return dot(y, x, ((1,), (1,)))

    def contract(g, how):
        total = how()
        inner[g] = (total[:d, :d] + total[d:, d:]) + (total[:d, d:] + total[d:, :d])

    def apply_low(g, begin=0):
        step = slabs // 2
        for a in range(2):
            for s in range(begin, slabs, step):
                r = dot(held[a, pl.ds(s, step)].reshape(step * rows, 2 * d), right[at, g])
                held[a, pl.ds(s, step)] = fuse((r[:, :d] + r[:, d:]).reshape(step, rows, d))

    def apply_mid(g, begin=0):
        for s in range(begin, slabs, 2):
            pairs = [(a, s + j) for a in range(2) for j in range(2)]
            x = jnp.concatenate([stacked(held[pair]) for pair in pairs], axis=1)
            r = dot(left[at, g], x)
            r = r[:d] + r[d:]
            for j, pair in enumerate(pairs):
                held[pair] = fuse(r[:, j * d : (j + 1) * d])

    def step(i, _):
        g = count - 1 - i
        low_turn = targets[block, g] == 0
        mid_turn = jnp.logical_not(low_turn)
        fresh = jnp.logical_or(i == 0, targets[block, g] != targets[block, jnp.minimum(g + 1, count - 1)])
        pl.when(jnp.logical_and(fresh, low_turn))(lambda: contract(g, contract_low))
        pl.when(jnp.logical_and(fresh, mid_turn))(lambda: contract(g, contract_mid))
        if ready is not None:
            pl.when(i == 0)(ready)
        turn = targets[block, g] != targets[block, jnp.maximum(g - 1, 0)]
        pl.when(jnp.logical_and(turn, low_turn))(lambda: apply_low(g))
        pl.when(jnp.logical_and(turn, mid_turn))(lambda: apply_mid(g))
        return _

    lax.fori_loop(0, count, step, 0)
    if finish_from < slabs:
        low_turn = targets[block, 0] == 0
        pl.when(low_turn)(lambda: apply_low(0, finish_from))
        pl.when(jnp.logical_not(low_turn))(lambda: apply_mid(0, finish_from))
    first = [count - 1] * count
    before = [count] * count
    for g in range(count - 2, -1, -1):
        going = same_run(targets, block, g)
        first[g] = jnp.where(going, first[g + 1], g)
        before[g] = jnp.where(going, g + 1, count)
    moved = [times_right(inner[first[g]], right[at, g]) for g in range(count)]
    for g in range(count):
        grads[g] = times_left(left[at, before[g]], moved[g]) * scale


def halves(grads, keep, send):
    half = grads.shape[0] // 2
    core = lax.axis_index("qb") % 2
    keep[...] = grads[pl.ds(core * half, half)].reshape(keep.shape)
    send[...] = grads[pl.ds((1 - core) * half, half)].reshape(send.shape)


def first_gradient_kernel(block, scale, *refs):
    refs, (keep, send, far0, low0, mid0, held, inner, right, left, made, grads, near0, sem) = refs[:4], refs[4:]
    gradient_kernel(block, scale, *refs, grads, near0, held, inner, right, left, made)
    copy = pltpu.make_async_copy(near0, far0, sem)
    copy.start()
    low0[...] = right_factor(made[made.shape[0] - 2])
    mid0[...] = left_factor(made[made.shape[0] - 1])
    halves(grads, keep, send)
    copy.wait()


def build(products, right, left):
    count, d, _ = products.shape
    for g in range(count):
        right[0, g] = right_factor(products[g])
        left[0, g] = left_factor(products[g])
    left[0, count] = left_factor(identity(d))


def gradient_kernel(block, scale, targets, gates, state, costate, out, factors0, held, inner, right, left, made):
    chains(targets, gates, right, left, made, factors0)
    for s in range(held.shape[1]):
        for a, ref in enumerate((state, costate)):
            held[a, s] = fuse(slab_of_native(ref, s))
    block_kernel(block, block, held.shape[1], scale, targets, right, left, held, inner, out)


def slabs_gradient_kernel(block, scale, targets, products, parts, out, held, inner, right, left):
    build(products, right, left)
    for s in range(held.shape[1]):
        for a in range(2):
            held[a, s] = fuse(slab_of_parts(parts, a, s))
    block_kernel(block, 0, held.shape[1], scale, targets, right, left, held, inner, out)


def early_kernel(n_qb, low, mid, *refs):
    blocks, (out, held) = refs[:n_qb], refs[n_qb:]
    n, _, slabs, r, d = out.shape
    gather(blocks, lambda rows, x: held.__setitem__((slice(None), slice(None), rows), x))
    for s in range(slabs):
        z = times_right(jnp.concatenate([held[0, s], held[1, s]], axis=0), low[...])
        z = times_left(mid[...], jnp.concatenate([z[: n * r], z[n * r :]], axis=1))
        for a in range(2):
            out[:, a, s] = z[:, a * d : (a + 1) * d].reshape(n, r, d)


def gather(blocks, put):
    mine = lax.axis_index("qb")
    for k, ref in enumerate(blocks):
        count = ref.shape[2]
        put(pl.ds(pl.multiple_of((mine ^ k) * count, count), count), ref[...])


def second_kernel(block, n_qa, n_qb, early, scale, targets, products, *refs):
    blocks, outs = (refs[:n_qb], refs[n_qb : 2 * n_qb]), refs[2 * n_qb : 2 * n_qb + n_qa]
    keep, send, held, inner, grads, here, right, left, sem = refs[2 * n_qb + n_qa :]
    copy = pltpu.make_async_copy(products, here, sem)
    copy.start()

    def ready():
        copy.wait()
        build(here, right, left)

    d = inner.shape[-1]
    for slabs, part in zip((slice(0, early), slice(early, None)), blocks):
        gather(part, lambda rows, x: held.__setitem__((slice(None), slabs, rows), fuse(x)))
    block_kernel(block, 0, early, scale, targets, right, left, held, inner, grads, ready)
    for k, ref in enumerate(outs):
        count = ref.shape[2]
        rows = pl.ds(pl.multiple_of((lax.axis_index("qa") ^ k) * count, count), count)
        part = held[:, early:, rows].astype(F32)
        ref[...] = part[..., :d] + part[..., d:]
    halves(grads, keep, send)


def first_kernel(block, n_qb, far_targets, gates, state, costate, *refs):
    outs, (targets, mats, x_ref, y_ref, turned, sems) = refs[: 2 * n_qb], refs[2 * n_qb :]
    copies = [
        pltpu.make_async_copy(far_targets, targets, sems.at[3]),
        pltpu.make_async_copy(gates.at[pl.ds(block, 1)], mats, sems.at[0]),
        pltpu.make_async_copy(state, x_ref, sems.at[1]),
        pltpu.make_async_copy(costate, y_ref, sems.at[2]),
    ]
    for copy in copies:
        copy.start()
    slabs = x_ref.shape[1]
    _, early, r, d = outs[0].shape
    mine = lax.axis_index("qb")
    copies[0].wait()
    copies[1].wait()
    low, mid = products(targets, mats, block, 0)
    low = right_factor(low)
    turned[...] = jnp.transpose(mid)
    mid = jnp.concatenate(
        [turned[pl.ds(pl.multiple_of((mine ^ k) * r, r), r), :] for k in range(n_qb)], axis=0
    )
    mid = stack_factor(mid)
    copies[2].wait()
    copies[3].wait()
    for s in range(slabs):
        x, y = slab_of_native(x_ref, s), slab_of_native(y_ref, s)
        z = times_right(jnp.concatenate([x, y], axis=0), low)
        z = times_left(mid, jnp.concatenate([z[:d], z[d:]], axis=1))
        late, i = (0, s) if s < early else (1, s - early)
        for k, out in enumerate(outs[late * n_qb : (late + 1) * n_qb]):
            out[0, i] = z[k * r : (k + 1) * r, :d]
            out[1, i] = z[k * r : (k + 1) * r, d:]


def split_sum_kernel(bit, shared, keep, got, *refs):
    outs, total = refs[:-1], refs[-1]
    total[...] = keep[...] + got[...]
    split_total(bit, shared, outs, total)


def split_total(bit, shared, outs, total):
    axis, weight = bit
    mine = (lax.axis_index(axis) // weight) % 2
    first = total.shape[0] - shared
    for which, out in enumerate(outs):
        half = first // 2
        start = (mine ^ which) * half
        out[:half] = total[pl.ds(pl.multiple_of(start, half), half), :]
        rest = out.shape[0] - half
        if rest and rest == shared:
            out[half:] = total[first:]
        elif rest:
            start = pl.multiple_of(first + (mine ^ which) * rest, rest)
            out[half:] = total[pl.ds(start, rest), :]


def join_split_kernel(bit, keep0, got0, keep1, got1, *refs):
    outs, total = refs[:-1], refs[-1]
    shared = keep1.shape[0]
    total[:-shared] = keep0[...] + got0[...]
    total[-shared:] = keep1[...] + got1[...]
    split_total(bit, shared, outs, total)


def sum_kernel(keep, got, out):
    out[...] = keep[...] + got[...]


def collect_kernel(orders, back, *refs):
    ins, out = refs[:-1], refs[-1]
    size = ins[0].shape[0] // 2
    for i, ref in enumerate(ins):
        for block, order in enumerate(orders):
            row = 0
            for axis, weight in order:
                delta = (i >> back.index((axis, weight))) & 1
                row = row * 2 + ((lax.axis_index(axis) // weight) % 2) ^ delta
            row = pl.multiple_of(row * size, size)
            out[block, pl.ds(row, size), :] = ref[block * size : (block + 1) * size]


def store_kernel(parts, first, second):
    n, _, slabs, r, d = parts.shape
    for a, out in enumerate((first, second)):
        flat = out.reshape(n * r * slabs, d)
        for s in range(slabs):
            flat[pl.ds(s, n * r, stride=slabs), :] = slab_of_parts(parts, a, s)


def place_kernel(n_qa, parts, *refs):
    blocks, outs = refs[:n_qa], refs[n_qa:]
    rows, slabs, d = outs[0].shape
    r, early = rows // n_qa, parts.shape[2]
    for a, out in enumerate(outs):
        flat = out.reshape(rows * slabs, d)
        for s in range(early):
            flat[pl.ds(s, rows, stride=slabs), :] = slab_of_parts(parts, a, s)
    for k, ref in enumerate(blocks):
        start = pl.multiple_of((lax.axis_index("qa") ^ k) * (r * slabs), r * slabs)
        for a, out in enumerate(outs):
            flat = out.reshape(rows * slabs, d)
            for s in range(early, slabs):
                flat[pl.ds(start + s, r, stride=slabs), :] = ref[a, s - early]


def call(kernel, out_shape, inputs, scratch=(), flops=0, far=(), far_out=(), ride=()):
    def spec(i, x):
        near = pltpu.SMEM if x.dtype == jnp.int32 else pltpu.VMEM
        return pl.BlockSpec(memory_space=pl.ANY if i in far else near)

    outs, tree = jax.tree.flatten(out_shape)
    n_in, n_out, n_ride = len(inputs), len(outs), len(ride)
    passing = [pl.BlockSpec(memory_space=pl.ANY)] * n_ride

    def body(*refs):
        rest = refs[n_in + n_ride :]
        kernel(*refs[:n_in], *rest[:n_out], *rest[n_out + n_ride :])

    size = sum(x.size * 4 for x in inputs) + sum(x.size * 4 for x in outs)
    got = pl.pallas_call(
        body,
        out_shape=outs + [shape(*x.shape) for x in ride],
        in_specs=[spec(i, x) for i, x in enumerate(inputs)] + passing,
        out_specs=[pl.BlockSpec(memory_space=pltpu.HBM if i in far_out else pltpu.VMEM) for i in range(n_out)] + passing,
        scratch_shapes=list(scratch),
        input_output_aliases={n_in + i: n_out + i for i in range(n_ride)},
        compiler_params=pltpu.CompilerParams(vmem_limit_bytes=VMEM_LIMIT),
        cost_estimate=pl.CostEstimate(flops=flops, bytes_accessed=size, transcendentals=0),
    )(*inputs, *ride)
    result = jax.tree.unflatten(tree, got[:n_out])
    return (result, list(got[n_out:])) if n_ride else result


def shape(*dims):
    return jax.ShapeDtypeStruct(dims, F32)


def exchange(x, da, db):
    n_qa, n_qb = lax.axis_size("qa"), lax.axis_size("qb")
    pairs = [(a * n_qb + b, (a ^ da) * n_qb + (b ^ db)) for a in range(n_qa) for b in range(n_qb)]
    return lax.ppermute(x, ("qa", "qb"), pairs)


def summed(grads0, grads1):
    both = jnp.stack([grads0, grads1])
    shares = both.reshape(lax.axis_size("qa") * lax.axis_size("qb"), -1, both.shape[-1])
    share = lax.all_to_all(shares, ("qa", "qb"), 0, 0, tiled=True).sum(0, keepdims=True)
    return lax.all_to_all(jnp.broadcast_to(share, shares.shape), ("qa", "qb"), 0, 0, tiled=True)


def nothing(*refs):
    pass


def windows(n_qa):
    ks = sorted(range(1, n_qa), reverse=True)
    stages = WINDOWS
    return {k: stages[min(i, len(stages) - 1)] for i, k in enumerate(ks)}


def shards(state, costate, gates, targets):
    layout = state.shape
    rows, slabs, d = layout[2:]
    n_qa, n_qb = lax.axis_size("qa"), lax.axis_size("qb")
    scale = (n_qa * n_qb * rows * slabs) ** -0.5
    native = shape(*layout[2:])
    natives = [state.reshape(native.shape), costate.reshape(native.shape)]
    r = rows // n_qb
    parts_qa = shape(n_qa, 2, slabs, rows // n_qa, d)
    count = gates.shape[1]
    held, inner = pltpu.VMEM((2, slabs, rows, 2 * d), BF16), pltpu.VMEM((count, d, d), F32)
    def factors(blocks):
        return [(blocks, count, 2 * d, 2 * d), (blocks, count + 1, 2 * d, 2 * d)]

    products0 = shape(count, d, d)
    chain = [pltpu.VMEM(x, BF16) for x in factors(2)] + [pltpu.VMEM((4, d, d), F32)]
    early = slabs // 2
    work = 2 * 2 * 2 * 4 * rows * slabs * d * d
    every = count * d

    if every % (16 * n_qb) or r % 16 or n_qa % 2 or n_qb % 2:
        parts_qb = shape(n_qb, 2, slabs, r, d)
        sent = call(functools.partial(apply_kernel, 1, True), parts_qb, [targets, gates, *natives], flops=work)
        parts = lax.all_to_all(sent, "qb", 0, 0, tiled=True)
        grads1, products = call(
            functools.partial(gradient_kernel, 1, scale),
            [shape(count, d, d), products0], [targets, gates, *natives], [held, inner, *chain], 8 * work,
        )
        sent = call(functools.partial(apply_kernel, 0, False), parts_qa, [targets, gates, parts], flops=work)
        last = lax.all_to_all(sent, "qa", 0, 0, tiled=True)
        first, second = call(store_kernel, (native, native), [last])
        grads0 = call(
            functools.partial(slabs_gradient_kernel, 0, scale),
            shape(count, d, d), [targets, products, parts], [held, inner, *(pltpu.VMEM(x, BF16) for x in factors(1))], 8 * work,
        )
        whole = summed(grads0, grads1)
    else:
        blocks = call(
            functools.partial(first_kernel, 1, n_qb),
            [shape(2, n, r, d) for n in (early, slabs - early) for _ in range(n_qb)],
            [pltpu.with_memory_space_constraint(x, pltpu.HBM) for x in (targets, gates, *natives)],
            [
                pltpu.SMEM(targets.shape, jnp.int32),
                pltpu.VMEM((1, *gates.shape[1:]), F32),
                pltpu.VMEM(native.shape, F32),
                pltpu.VMEM(native.shape, F32),
                pltpu.VMEM((d, d), F32),
                pltpu.SemaphoreType.DMA((4,)),
            ],
            work,
            far=(0, 1, 2, 3),
        )
        front, rear = blocks[:n_qb], blocks[n_qb:]
        front = front[:1] + [exchange(x, 0, k) for k, x in enumerate(front) if k]
        rear = rear[:1] + [exchange(x, 0, k) for k, x in enumerate(rear) if k]
        bits = [("qb", 1 << i) for i in range(n_qb.bit_length() - 1)]
        across_x = ("qa", 1)

        def across(x, bit):
            return exchange(x, bit[1], 0) if bit[0] == "qa" else exchange(x, 0, bit[1])

        half = shape(every // 2, d)
        square = jax.ShapeDtypeStruct((2 * d, 2 * d), BF16)
        keep1, send1, products, low, mid = call(
            functools.partial(first_gradient_kernel, 1, scale),
            [half, half, products0, square, square],
            [targets, gates, *natives],
            [held, inner, *chain, inner, inner, pltpu.SemaphoreType.DMA],
            10 * work,
            far_out=(2,),
        )
        got1 = across(send1, bits[0])
        sent = call(
            functools.partial(early_kernel, n_qb),
            shape(n_qa, 2, early, rows // n_qa, d),
            [low, mid, *front],
            [pltpu.VMEM((2, early, rows, d), F32)],
            3 * work,
        )
        parts = lax.all_to_all(sent, "qa", 0, 0, tiled=True)
        *moved, keep0, send0 = call(
            functools.partial(second_kernel, 0, n_qa, n_qb, early, scale),
            [shape(2, slabs - early, rows // n_qa, d)] * n_qa + [half, half],
            [targets, products, *front, *rear],
            [held, inner, inner, inner, *(pltpu.VMEM(x, BF16) for x in factors(1)), pltpu.SemaphoreType.DMA],
            K0COST * work,
            far=(1,),
        )
        came = {0: moved[0], "parts": parts}
        moved = dict(enumerate(moved))
        window = windows(n_qa)

        def after(stage, kernel, out_shape, inputs, scratch=(), far=()):
            due = [k for k in window if window[k][1] == stage]
            opens = [k for k in window if window[k][0] == stage]
            ride = [came[k] for k in due] + [moved[k] for k in opens]
            if stage == PARTS_DUE:
                ride, due = [came["parts"], *ride], ["parts", *due]
            if not ride:
                return call(kernel, out_shape, inputs, scratch, far=far) if out_shape else None
            result, rode = call(kernel, out_shape, inputs, scratch, far=far, ride=ride)
            came.update(zip(due, rode))
            moved.update(zip(opens, rode[len(due) :]))
            start(stage)
            return result

        def start(stage):
            for k in window:
                if window[k][0] == stage:
                    came[k] = exchange(moved[k], k, 0)

        start(0)
        keep, got = (keep0, keep1), (across(send0, bits[0]), got1)
        bits = bits + [across_x]
        size = every // 2
        for i, bit in enumerate(bits[1:]):
            if i == 0:
                kernel, inputs = functools.partial(join_split_kernel, bit), [keep[0], got[0], keep[1], got[1]]
            else:
                kernel, inputs = functools.partial(split_sum_kernel, bit, size), [keep, got]
            scratch = [pltpu.VMEM((2 * size, d), F32)]
            keep, send = after(i + 1, kernel, [shape(size, d)] * 2, inputs, scratch)
            got = across(send, bit)
            size = size // 2
        mine = after("plane", sum_kernel, shape(*keep.shape), [keep, got])
        for i in range(1, n_qa.bit_length() - 1):
            got = exchange(mine, 1 << i, 0)
            mine = after(("line", i), sum_kernel, shape(*mine.shape), [mine, got])
        back = list(reversed(bits))
        found = [mine]
        for i, bit in enumerate(back):
            found = found + [across(x, bit) for x in found]
            after(("back", i), nothing, [], [found[-1]], far=(0,))
        whole = call(
            functools.partial(collect_kernel, [bits, bits], back), shape(gates.shape[0], every, d), found
        )
        first, second = call(
            functools.partial(place_kernel, n_qa),
            (native, native),
            [came["parts"], *(came[k] for k in range(n_qa))],
        )
    return first.reshape(layout), second.reshape(layout), whole.reshape(gates.shape)


def solution(mesh):
    in_specs = (P("qa", "qb", None, None, None), P("qa", "qb", None, None, None), P(), P())
    out_specs = (P("qa", "qb", None, None, None), P("qa", "qb", None, None, None), P())
    return jax.shard_map(shards, mesh=mesh, in_specs=in_specs, out_specs=out_specs, check_vma=False)
```

time: 102 us -> 63.3 us (0.62)
  waiting for transfers between devices: 62.2 us -> 9.44 us
  starting transfers between devices: 17.1 us -> 38.2 us
  local copies, waits for them, and re-layouts: 5.45 us -> 0.02 us
    all_to_all x4 -> x1, waiting for transfers between devices: 62.2 us -> 0.46 us  [shards(): parts = lax.all_to_all(sent, 'qa', 0, 0, tiled=True)]
    ppermute x0 -> x26, starting transfers between devices: none -> 32.2 us  [exchange(): return lax.ppermute(x, ('qa', 'qb'), pairs)]
    all_to_all x4 -> x1, starting transfers between devices: 17.1 us -> 5.95 us  [shards(): parts = lax.all_to_all(sent, 'qa', 0, 0, tiled=True)]
    ppermute x0 -> x26, waiting for transfers between devices: none -> 8.99 us  [exchange(): return lax.ppermute(x, ('qa', 'qb'), pairs)]
    unnamed x15 -> x8, local copies, waits for them, and re-layouts: 4.6 us -> 0.02 us
    pallas_call x5 -> x13, Pallas kernels: 15.5 us -> 14.7 us  [call(): pl.pallas_call(body, out_shape=outs + [shape(*x.shape) for x in ride], in...]
  transfers between devices with their start and end apart: 4 -> 27, of which waited for: 4 -> 7; matrix products, arithmetic and copies ran while one was open for 0% -> 0% of each run, Pallas kernels for 9% -> 18%
where the time goes in v3:
time: 63.3 us; the launch traced here: 63.1 us
  starting transfers between devices  38.2 us (60%)
  Pallas kernels  14.7 us (23%)
  waiting for transfers between devices  9.44 us (15%)
  between operations  0.77 us (1%)
    ppermute x26, starting transfers between devices, exchange(): return lax.ppermute(x, ('qa', 'qb'), pairs)  32.2 us
    pallas_call x13, Pallas kernels, call(): pl.pallas_call(body, out_shape=outs + [shape(*x.shape) for x in ride], in...  14.7 us
    ppermute x26, waiting for transfers between devices, exchange(): return lax.ppermute(x, ('qa', 'qb'), pairs)  8.99 us
    all_to_all x1, starting transfers between devices, shards(): parts = lax.all_to_all(sent, 'qa', 0, 0, tiled=True)  5.95 us
  transfers between devices with their start and end apart: 27, of which 7 were waited for; matrix products, arithmetic and copies ran while one was open for 0% of the time, Pallas kernels for 18%

profile of v3, /device:TPU:0, one launch (start us, length us, event | category | flops | bytes accessed | tf_op | source)
XLA Modules:
  0.0 63.1 jit_solution(16458176110163141741)
XLA Ops:
  0.7 2.6 %shard_map.68 = (f32[2,4,32,128]{3,2,1,0:T(8,128)S(1)}, f32[2,4,32,128]{3,2,1,0:T(8,128)S(1)}, f32[2,4,32,128]{3,2,1,0:T(8,128)S(1)}, f32[2,4,32,128]{3,2,1,0:T(...) custom-call(s32[2,4]{1,0:T(2,128)} %refs_0_.5, ...), custom_call_target="tpu_custom_call" | custom-call | flops 536870912 | bytes 2621472 | tf_op jit(solution)/shard_map/pallas_call | solution.py:417
  3.2 0.5 collective-permute-start
  3.7 2.6 %collective-permute-start.1 = (f32[2,4,32,128]{3,2,1,0:T(8,128)S(1)}, f32[2,4,32,128]{3,2,1,0:T(8,128)S(1)}, u32[]{:S(2)}, u32[]{:S(2)}) collective-permute-start(f32[2,4,32,128]{3,2,1,0:T(8,128)S(1)} %get-tuple-element.49), channel_id=1, source_target_pairs={{0,2},{1,3},{2,0},{3,1},{4,6},{5,7},{6,4},{7,5},{8,10},{9,11},{10,... | collective-permute-start | bytes 393224 | tf_op jit(solution)/shard_map/ppermute | solution.py:438
  6.4 4.8 %shard_map.67 = (f32[256,128]{1,0:T(8,128)S(1)}, f32[256,128]{1,0:T(8,128)S(1)}, f32[4,128,128]{2,1,0:T(8,128)S(1)}, bf16[256,256]{1,0:T(8,128)(2,1)S(1)}, bf16[256,256]{1,0:T(8,128)(2,1)S(1)}) custom-call(s32[2,4]{1,0:T(2,128)S(1)} %copy-done.3, f32[2,4,128,128]{3,2,1,0:T(8,128)S(1)} %copy-done, f32[128,8,128]{2,1,0:T(8,128)S(1)} %bitcast.6, ...), custom_call_target="tpu_custom_call" | custom-call | flops 5368709120 | bytes 2621472 | tf_op jit(solution)/shard_map/pallas_call | solution.py:417
  11.4 0.4 collective-permute-start.3
  11.8 1.7 %collective-permute-start.4 = (f32[2,4,32,128]{3,2,1,0:T(8,128)S(1)}, f32[2,4,32,128]{3,2,1,0:T(8,128)S(1)}, u32[]{:S(2)}, u32[]{:S(2)}) collective-permute-start(f32[2,4,32,128]{3,2,1,0:T(8,128)S(1)} %get-tuple-element.53), channel_id=1, source_target_pairs={{0,2},{1,3},{2,0},{3,1},{4,6},{5,7},{6,4},{7,5},{8,10},{9,11},{10,... | collective-permute-start | bytes 393224 | tf_op jit(solution)/shard_map/ppermute | solution.py:438
  13.6 1.4 %shard_map.72 = f32[8,2,4,16,128]{4,3,2,1,0:T(8,128)} custom-call(bf16[256,256]{1,0:T(8,128)(2,1)S(1)} %get-tuple-element.66.refs_0_, bf16[256,256]{1,0:T(8,128)(2,1)S(1)} %get-tuple-element.67.refs_1_, f32[2,4,32,128]{3,2,1,0:T(8,128)S(1)} %get-tuple-element.47.refs_2_, f32[2,4,32,128]{3,2,1,0:T(8,128)S(1)} %collective-permute-done.refs_3_, ...), custom_call_target="tpu_custom_call" | custom-call | flops 1610612736 | bytes 1572864 | tf_op jit(solution)/shard_map/pallas_call | solution.py:417
  15.0 6.0 %all-to-all-start = ((f32[8,2,4,16,128]{4,3,2,1,0:T(8,128)}), f32[8,2,4,16,128]{4,3,2,1,0:T(8,128)S(1)}, u32[]{:S(2)}, u32[]{:S(2)}) async-start(f32[8,2,4,16,128]{4,3,2,1,0:T(8,128)} %shard_map.72), calls=%async_computation | async-start | bytes 1048576 | tf_op jit(solution)/shard_map/all_to_all | solution.py:537
  21.0 3.8 %shard_map.69 = (f32[2,4,16,128]{3,2,1,0:T(8,128)S(1)}, f32[2,4,16,128]{3,2,1,0:T(8,128)S(1)}, f32[2,4,16,128]{3,2,1,0:T(8,128)S(1)}, f32[2,4,16,128]{3,2,1,0:T(...) custom-call(s32[2,4]{1,0:T(2,128)S(1)} %copy-done.3, ...), custom_call_target="tpu_custom_call" | custom-call | flops 26843545600 | bytes 2097184 | tf_op jit(solution)/shard_map/pallas_call | solution.py:417
  24.8 0.2 collective-permute-start.6
  25.0 1.2 %collective-permute-done.6.refs_1_ = f32[256,128]{1,0:T(8,128)S(1)} collective-permute-done((f32[256,128]{1,0:T(8,128)S(1)}, f32[256,128]{1,0:T(8,128)S(1)}, u32[]{:S(2)}, u32[]{:S(2)}) %collective-permute-start.6) | collective-permute-done | bytes 131104 | tf_op jit(solution)/shard_map/ppermute | solution.py:438
  26.2 1.6 %collective-permute-start.8 = (f32[256,128]{1,0:T(8,128)S(1)}, f32[256,128]{1,0:T(8,128)S(1)}, u32[]{:S(2)}, u32[]{:S(2)}) collective-permute-start(f32[256,128]{1,0:T(8,128)S(1)} %get-tuple-element.63), channel_id=1, source_target_pairs={{0,2},{1,3},{2,0},{3,1},{4,6},{5,7},{6,4},{7,5},{8,10},{9,11},{10,... | collective-permute-start | bytes 393224 | tf_op jit(solution)/shard_map/ppermute | solution.py:438
  27.8 4.7 %collective-permute-start.10 = (f32[2,4,16,128]{3,2,1,0:T(8,128)S(1)}, f32[2,4,16,128]{3,2,1,0:T(8,128)S(1)}, u32[]{:S(2)}, u32[]{:S(2)}) collective-permute-start(f32[2,4,16,128]{3,2,1,0:T(8,128)S(1)} %get-tuple-element.68), channel_id=1, source_target_pairs={{0,28},{1,29},{2,30},{3,31},{4,24},{5,25},{6,26},{7,27},{8,20},{9,... | collective-permute-start | bytes 196616 | tf_op jit(solution)/shard_map/ppermute | solution.py:438
  32.5 1.4 %collective-permute-start.9 = (f32[128,128]{1,0:T(8,128)S(1)}, f32[128,128]{1,0:T(8,128)S(1)}, u32[]{:S(2)}, u32[]{:S(2)}) collective-permute-start(f32[128,128]{1,0:T(8,128)S(1)} %get-tuple-element.65), channel_id=1, source_target_pairs={{0,4},{1,5},{2,6},{3,7},{4,0},{5,1},{6,2},{7,3},{8,12},{9,13},{10,... | collective-permute-start | bytes 196616 | tf_op jit(solution)/shard_map/ppermute | solution.py:438
  33.9 1.5 %collective-permute-start.13 = (f32[2,4,16,128]{3,2,1,0:T(8,128)S(1)}, f32[2,4,16,128]{3,2,1,0:T(8,128)S(1)}, u32[]{:S(2)}, u32[]{:S(2)}) collective-permute-start(f32[2,4,16,128]{3,2,1,0:T(8,128)S(1)} %get-tuple-element.74), channel_id=1, source_target_pairs={{0,8},{1,9},{2,10},{3,11},{4,12},{5,13},{6,14},{7,15},{8,0},{9,1},... | collective-permute-start | bytes 196616 | tf_op jit(solution)/shard_map/ppermute | solution.py:438
  35.4 2.4 %collective-permute-start.12 = (f32[2,4,16,128]{3,2,1,0:T(8,128)S(1)}, f32[2,4,16,128]{3,2,1,0:T(8,128)S(1)}, u32[]{:S(2)}, u32[]{:S(2)}) collective-permute-start(f32[2,4,16,128]{3,2,1,0:T(8,128)S(1)} %get-tuple-element.73), channel_id=1, source_target_pairs={{0,24},{1,25},{2,26},{3,27},{4,28},{5,29},{6,30},{7,31},{8,16},{9,... | collective-permute-start | bytes 196616 | tf_op jit(solution)/shard_map/ppermute | solution.py:438
  37.8 0.5 all-to-all-done.refs_2_
  38.2 4.3 %collective-permute-start.11 = (f32[128,128]{1,0:T(8,128)S(1)}, f32[128,128]{1,0:T(8,128)S(1)}, u32[]{:S(2)}, u32[]{:S(2)}) collective-permute-start(f32[128,128]{1,0:T(8,128)S(1)} %get-tuple-element.72.refs_0_), channel_id=1, source_target_pairs={{0,8},{1,9},{2,10},{3,11},{4,12},{5,13},{6,14},{7,15},{8,0},{9,1},... | collective-permute-start | bytes 196616 | tf_op jit(solution)/shard_map/ppermute | solution.py:438
  42.5 2.2 %collective-permute-done.11.refs_1_ = f32[128,128]{1,0:T(8,128)S(1)} collective-permute-done((f32[128,128]{1,0:T(8,128)S(1)}, f32[128,128]{1,0:T(8,128)S(1)}, u32[]{:S(2)}, u32[]{:S(2)}) %collective-permute-start.11) | collective-permute-done | bytes 65568 | tf_op jit(solution)/shard_map/ppermute | solution.py:438
  44.8 2.2 %collective-permute-start.14 = (f32[128,128]{1,0:T(8,128)S(1)}, f32[128,128]{1,0:T(8,128)S(1)}, u32[]{:S(2)}, u32[]{:S(2)}) collective-permute-start(f32[128,128]{1,0:T(8,128)S(1)} %get-tuple-element.76.refs_0_), channel_id=1, source_target_pairs={{0,16},{1,17},{2,18},{3,19},{4,20},{5,21},{6,22},{7,23},{8,24},{9,... | collective-permute-start | bytes 196616 | tf_op jit(solution)/shard_map/ppermute | solution.py:438
  47.0 1.8 %collective-permute-done.15.refs_2_ = f32[2,4,16,128]{3,2,1,0:T(8,128)S(1)} collective-permute-done((f32[2,4,16,128]{3,2,1,0:T(8,128)S(1)}, f32[2,4,16,128]{3,2,1,0:T(8,128)S(1)}, u32[]{:S(2)}, u32[]{:S(2)}) %collective-permute-start.15) | collective-permute-done | bytes 65568 | tf_op jit(solution)/shard_map/ppermute | solution.py:438
  48.8 1.2 %collective-permute-done.14.refs_1_ = f32[128,128]{1,0:T(8,128)S(1)} collective-permute-done((f32[128,128]{1,0:T(8,128)S(1)}, f32[128,128]{1,0:T(8,128)S(1)}, u32[]{:S(2)}, u32[]{:S(2)}) %collective-permute-start.14) | collective-permute-done | bytes 65568 | tf_op jit(solution)/shard_map/ppermute | solution.py:438
  50.1 2.2 %collective-permute-start.20 = (f32[2,4,16,128]{3,2,1,0:T(8,128)S(1)}, f32[2,4,16,128]{3,2,1,0:T(8,128)S(1)}, u32[]{:S(2)}, u32[]{:S(2)}) collective-permute-start(f32[2,4,16,128]{3,2,1,0:T(8,128)S(1)} %get-tuple-element.83), channel_id=1, source_target_pairs={{0,16},{1,17},{2,18},{3,19},{4,20},{5,21},{6,22},{7,23},{8,24},{9,... | collective-permute-start | bytes 196616 | tf_op jit(solution)/shard_map/ppermute | solution.py:438
  52.3 1.5 %collective-permute-start.21 = (f32[128,128]{1,0:T(8,128)S(1)}, f32[128,128]{1,0:T(8,128)S(1)}, u32[]{:S(2)}, u32[]{:S(2)}) collective-permute-start(f32[128,128]{1,0:T(8,128)S(1)} %get-tuple-element.81.refs_0_), channel_id=1, source_target_pairs={{0,2},{1,3},{2,0},{3,1},{4,6},{5,7},{6,4},{7,5},{8,10},{9,11},{10,... | collective-permute-start | bytes 196616 | tf_op jit(solution)/shard_map/ppermute | solution.py:438
  53.8 0.5 collective-permute-done.17.refs_0_.refs_1_
  54.4 1.5 %collective-permute-start.18 = (f32[128,128]{1,0:T(8,128)S(1)}, f32[128,128]{1,0:T(8,128)S(1)}, u32[]{:S(2)}, u32[]{:S(2)}) collective-permute-start(f32[128,128]{1,0:T(8,128)S(1)} %collective-permute-done.17.refs_0_.refs_1_), channel_id=1, source_target_pairs={{0,2},{1,3},{2,0},{3,1},{4,6},{5,7},{6,4},{7,5},{8,10},{9,11},{10,... | collective-permute-start | bytes 196616 | tf_op jit(solution)/shard_map/ppermute | solution.py:438
  55.9 2.1 %collective-permute-start.19 = (f32[2,4,16,128]{3,2,1,0:T(8,128)S(1)}, f32[2,4,16,128]{3,2,1,0:T(8,128)S(1)}, u32[]{:S(2)}, u32[]{:S(2)}) collective-permute-start(f32[2,4,16,128]{3,2,1,0:T(8,128)S(1)} %get-tuple-element.82), channel_id=1, source_target_pairs={{0,12},{1,13},{2,14},{3,15},{4,8},{5,9},{6,10},{7,11},{8,4},{9,5},... | collective-permute-start | bytes 196616 | tf_op jit(solution)/shard_map/ppermute | solution.py:438
  58.0 0.5 collective-permute-start.23
  58.6 0.4 collective-permute-start.25
  59.0 2.0 %collective-permute-done.19.refs_1_ = f32[2,4,16,128]{3,2,1,0:T(8,128)S(1)} collective-permute-done((f32[2,4,16,128]{3,2,1,0:T(8,128)S(1)}, f32[2,4,16,128]{3,2,1,0:T(8,128)S(1)}, u32[]{:S(2)}, u32[]{:S(2)}) %collective-permute-start.19) | collective-permute-done | bytes 65568 | tf_op jit(solution)/shard_map/ppermute | solution.py:438
  61.0 1.2 %shard_map.78 = (f32[128,8,128]{2,1,0:T(8,128)}, f32[128,8,128]{2,1,0:T(8,128)}) custom-call(f32[8,2,4,16,128]{4,3,2,1,0:T(8,128)S(1)} %get-tuple-element.70.refs_0_, f32[2,4,16,128]{3,2,1,0:T(8,128)S(1)} %get-tuple-element.71.refs_1_, f32[2,4,16,128]{3,2,1,0:T(8,128)S(1)} %get-tuple-element.79.refs_2_, f32[2,4,16,128]{3,2,1,0:T(8,128)S(1)} %get-tuple-element.80.refs_3_, ...), custom_call_target="tpu_custom_call" | custom-call | bytes 2097152 | tf_op jit(solution)/shard_map/pallas_call | solution.py:417
  62.2 0.9 %shard_map.79 = f32[2,512,128]{2,1,0:T(8,128)} custom-call(f32[128,128]{1,0:T(8,128)S(1)} %get-tuple-element.81.refs_0_, f32[128,128]{1,0:T(8,128)S(1)} %collective-permute-done.17.refs_0_.refs_1_, f32[128,128]{1,0:T(8,128)S(1)} %collective-permute-done.21.refs_2_, f32[128,128]{1,0:T(8,128)S(1)} %collective-permute-done.18.refs_0_.refs_3_, ...), custom_call_target="tpu_custom_call" | custom-call | bytes 1048576 | tf_op jit(solution)/shard_map/pallas_call | solution.py:417
  (43 shorter events, 0.7 us)
Async XLA Ops:
  0.6 5.8 %copy-start = (f32[2,4,128,128]{3,2,1,0:T(8,128)S(1)}, f32[2,4,128,128]{3,2,1,0:T(8,128)}, u32[]{:S(2)}) copy-start(f32[2,4,128,128]{3,2,1,0:T(8,128)} %refs_1_.3) | copy-start | bytes 1572868
  0.6 5.8 %copy-start.1 = (f32[1,1,128,8,128]{4,3,2,1,0:T(8,128)S(1)}, f32[1,1,128,8,128]{4,3,2,1,0:T(8,128)}, u32[]{:S(2)}) copy-start(f32[1,1,128,8,128]{4,3,2,1,0:T(8,128)} %param.4) | copy-start | bytes 1572868
  0.7 5.8 %copy-start.2 = (f32[1,1,128,8,128]{4,3,2,1,0:T(8,128)S(1)}, f32[1,1,128,8,128]{4,3,2,1,0:T(8,128)}, u32[]{:S(2)}) copy-start(f32[1,1,128,8,128]{4,3,2,1,0:T(8,128)} %param.5) | copy-start | bytes 1572868
  3.2 8.6 %collective-permute-start = (f32[2,4,32,128]{3,2,1,0:T(8,128)S(1)}, f32[2,4,32,128]{3,2,1,0:T(8,128)S(1)}, u32[]{:S(2)}, u32[]{:S(2)}) collective-permute-start(f32[2,4,32,128]{3,2,1,0:T(8,128)S(1)} %get-tuple-element.48), channel_id=1, source_target_pairs={{0,1},{1,0},{2,3},{3,2},{4,5},{5,4},{6,7},{7,6},{8,9},{9,8},{10,11... | collective-permute-start | bytes 393224 | tf_op jit(solution)/shard_map/ppermute | solution.py:438
  3.7 2.7 %copy-start.3 = (s32[2,4]{1,0:T(2,128)S(1)}, s32[2,4]{1,0:T(2,128)}, u32[]{:S(2)}) copy-start(s32[2,4]{1,0:T(2,128)} %refs_0_.5) | copy-start | bytes 100
  3.7 9.8 %collective-permute-start.1 = (f32[2,4,32,128]{3,2,1,0:T(8,128)S(1)}, f32[2,4,32,128]{3,2,1,0:T(8,128)S(1)}, u32[]{:S(2)}, u32[]{:S(2)}) collective-permute-start(f32[2,4,32,128]{3,2,1,0:T(8,128)S(1)} %get-tuple-element.49), channel_id=1, source_target_pairs={{0,2},{1,3},{2,0},{3,1},{4,6},{5,7},{6,4},{7,5},{8,10},{9,11},{10,... | collective-permute-start | bytes 393224 | tf_op jit(solution)/shard_map/ppermute | solution.py:438
  6.3 7.2 %collective-permute-start.2 = (f32[2,4,32,128]{3,2,1,0:T(8,128)S(1)}, f32[2,4,32,128]{3,2,1,0:T(8,128)S(1)}, u32[]{:S(2)}, u32[]{:S(2)}) collective-permute-start(f32[2,4,32,128]{3,2,1,0:T(8,128)S(1)} %get-tuple-element.50), channel_id=1, source_target_pairs={{0,3},{1,2},{2,1},{3,0},{4,7},{5,6},{6,5},{7,4},{8,11},{9,10},{10,... | collective-permute-start | bytes 393224 | tf_op jit(solution)/shard_map/ppermute | solution.py:438
  11.2 13.8 %collective-permute-start.7 = (f32[256,128]{1,0:T(8,128)S(1)}, f32[256,128]{1,0:T(8,128)S(1)}, u32[]{:S(2)}, u32[]{:S(2)}) collective-permute-start(f32[256,128]{1,0:T(8,128)S(1)} %get-tuple-element.58), channel_id=1, source_target_pairs={{0,1},{1,0},{2,3},{3,2},{4,5},{5,4},{6,7},{7,6},{8,9},{9,8},{10,11... | collective-permute-start | bytes 393224 | tf_op jit(solution)/shard_map/ppermute | solution.py:438
  11.4 9.5 %collective-permute-start.3 = (f32[2,4,32,128]{3,2,1,0:T(8,128)S(1)}, f32[2,4,32,128]{3,2,1,0:T(8,128)S(1)}, u32[]{:S(2)}, u32[]{:S(2)}) collective-permute-start(f32[2,4,32,128]{3,2,1,0:T(8,128)S(1)} %get-tuple-element.52), channel_id=1, source_target_pairs={{0,1},{1,0},{2,3},{3,2},{4,5},{5,4},{6,7},{7,6},{8,9},{9,8},{10,11... | collective-permute-start | bytes 393224 | tf_op jit(solution)/shard_map/ppermute | solution.py:438
  11.8 9.2 %collective-permute-start.4 = (f32[2,4,32,128]{3,2,1,0:T(8,128)S(1)}, f32[2,4,32,128]{3,2,1,0:T(8,128)S(1)}, u32[]{:S(2)}, u32[]{:S(2)}) collective-permute-start(f32[2,4,32,128]{3,2,1,0:T(8,128)S(1)} %get-tuple-element.53), channel_id=1, source_target_pairs={{0,2},{1,3},{2,0},{3,1},{4,6},{5,7},{6,4},{7,5},{8,10},{9,11},{10,... | collective-permute-start | bytes 393224 | tf_op jit(solution)/shard_map/ppermute | solution.py:438
  13.5 7.4 %collective-permute-start.5 = (f32[2,4,32,128]{3,2,1,0:T(8,128)S(1)}, f32[2,4,32,128]{3,2,1,0:T(8,128)S(1)}, u32[]{:S(2)}, u32[]{:S(2)}) collective-permute-start(f32[2,4,32,128]{3,2,1,0:T(8,128)S(1)} %get-tuple-element.54), channel_id=1, source_target_pairs={{0,3},{1,2},{2,1},{3,0},{4,7},{5,6},{6,5},{7,4},{8,11},{9,10},{10,... | collective-permute-start | bytes 393224 | tf_op jit(solution)/shard_map/ppermute | solution.py:438
  15.0 23.2 %all-to-all-start = ((f32[8,2,4,16,128]{4,3,2,1,0:T(8,128)}), f32[8,2,4,16,128]{4,3,2,1,0:T(8,128)S(1)}, u32[]{:S(2)}, u32[]{:S(2)}) async-start(f32[8,2,4,16,128]{4,3,2,1,0:T(8,128)} %shard_map.72), calls=%async_computation | async-start | bytes 1048576 | tf_op jit(solution)/shard_map/all_to_all | solution.py:537
  24.8 1.4 %collective-permute-start.6 = (f32[256,128]{1,0:T(8,128)S(1)}, f32[256,128]{1,0:T(8,128)S(1)}, u32[]{:S(2)}, u32[]{:S(2)}) collective-permute-start(f32[256,128]{1,0:T(8,128)S(1)} %get-tuple-element.56), channel_id=1, source_target_pairs={{0,1},{1,0},{2,3},{3,2},{4,5},{5,4},{6,7},{7,6},{8,9},{9,8},{10,11... | collective-permute-start | bytes 393224 | tf_op jit(solution)/shard_map/ppermute | solution.py:438
  26.2 6.3 %collective-permute-start.8 = (f32[256,128]{1,0:T(8,128)S(1)}, f32[256,128]{1,0:T(8,128)S(1)}, u32[]{:S(2)}, u32[]{:S(2)}) collective-permute-start(f32[256,128]{1,0:T(8,128)S(1)} %get-tuple-element.63), channel_id=1, source_target_pairs={{0,2},{1,3},{2,0},{3,1},{4,6},{5,7},{6,4},{7,5},{8,10},{9,11},{10,... | collective-permute-start | bytes 393224 | tf_op jit(solution)/shard_map/ppermute | solution.py:438
  27.8 10.0 %collective-permute-start.10 = (f32[2,4,16,128]{3,2,1,0:T(8,128)S(1)}, f32[2,4,16,128]{3,2,1,0:T(8,128)S(1)}, u32[]{:S(2)}, u32[]{:S(2)}) collective-permute-start(f32[2,4,16,128]{3,2,1,0:T(8,128)S(1)} %get-tuple-element.68), channel_id=1, source_target_pairs={{0,28},{1,29},{2,30},{3,31},{4,24},{5,25},{6,26},{7,27},{8,20},{9,... | collective-permute-start | bytes 196616 | tf_op jit(solution)/shard_map/ppermute | solution.py:438
  32.5 5.2 %collective-permute-start.9 = (f32[128,128]{1,0:T(8,128)S(1)}, f32[128,128]{1,0:T(8,128)S(1)}, u32[]{:S(2)}, u32[]{:S(2)}) collective-permute-start(f32[128,128]{1,0:T(8,128)S(1)} %get-tuple-element.65), channel_id=1, source_target_pairs={{0,4},{1,5},{2,6},{3,7},{4,0},{5,1},{6,2},{7,3},{8,12},{9,13},{10,... | collective-permute-start | bytes 196616 | tf_op jit(solution)/shard_map/ppermute | solution.py:438
  33.9 8.6 %collective-permute-start.13 = (f32[2,4,16,128]{3,2,1,0:T(8,128)S(1)}, f32[2,4,16,128]{3,2,1,0:T(8,128)S(1)}, u32[]{:S(2)}, u32[]{:S(2)}) collective-permute-start(f32[2,4,16,128]{3,2,1,0:T(8,128)S(1)} %get-tuple-element.74), channel_id=1, source_target_pairs={{0,8},{1,9},{2,10},{3,11},{4,12},{5,13},{6,14},{7,15},{8,0},{9,1},... | collective-permute-start | bytes 196616 | tf_op jit(solution)/shard_map/ppermute | solution.py:438
  35.4 7.1 %collective-permute-start.12 = (f32[2,4,16,128]{3,2,1,0:T(8,128)S(1)}, f32[2,4,16,128]{3,2,1,0:T(8,128)S(1)}, u32[]{:S(2)}, u32[]{:S(2)}) collective-permute-start(f32[2,4,16,128]{3,2,1,0:T(8,128)S(1)} %get-tuple-element.73), channel_id=1, source_target_pairs={{0,24},{1,25},{2,26},{3,27},{4,28},{5,29},{6,30},{7,31},{8,16},{9,... | collective-permute-start | bytes 196616 | tf_op jit(solution)/shard_map/ppermute | solution.py:438
  38.2 6.5 %collective-permute-start.11 = (f32[128,128]{1,0:T(8,128)S(1)}, f32[128,128]{1,0:T(8,128)S(1)}, u32[]{:S(2)}, u32[]{:S(2)}) collective-permute-start(f32[128,128]{1,0:T(8,128)S(1)} %get-tuple-element.72.refs_0_), channel_id=1, source_target_pairs={{0,8},{1,9},{2,10},{3,11},{4,12},{5,13},{6,14},{7,15},{8,0},{9,1},... | collective-permute-start | bytes 196616 | tf_op jit(solution)/shard_map/ppermute | solution.py:438
  42.5 6.3 %collective-permute-start.15 = (f32[2,4,16,128]{3,2,1,0:T(8,128)S(1)}, f32[2,4,16,128]{3,2,1,0:T(8,128)S(1)}, u32[]{:S(2)}, u32[]{:S(2)}) collective-permute-start(f32[2,4,16,128]{3,2,1,0:T(8,128)S(1)} %get-tuple-element.77), channel_id=1, source_target_pairs={{0,20},{1,21},{2,22},{3,23},{4,16},{5,17},{6,18},{7,19},{8,28},{9,... | collective-permute-start | bytes 196616 | tf_op jit(solution)/shard_map/ppermute | solution.py:438
  42.5 6.3 %collective-permute-start.16 = (f32[2,4,16,128]{3,2,1,0:T(8,128)S(1)}, f32[2,4,16,128]{3,2,1,0:T(8,128)S(1)}, u32[]{:S(2)}, u32[]{:S(2)}) collective-permute-start(f32[2,4,16,128]{3,2,1,0:T(8,128)S(1)} %get-tuple-element.78), channel_id=1, source_target_pairs={{0,4},{1,5},{2,6},{3,7},{4,0},{5,1},{6,2},{7,3},{8,12},{9,13},{10,... | collective-permute-start | bytes 196616 | tf_op jit(solution)/shard_map/ppermute | solution.py:438
  44.8 5.2 %collective-permute-start.14 = (f32[128,128]{1,0:T(8,128)S(1)}, f32[128,128]{1,0:T(8,128)S(1)}, u32[]{:S(2)}, u32[]{:S(2)}) collective-permute-start(f32[128,128]{1,0:T(8,128)S(1)} %get-tuple-element.76.refs_0_), channel_id=1, source_target_pairs={{0,16},{1,17},{2,18},{3,19},{4,20},{5,21},{6,22},{7,23},{8,24},{9,... | collective-permute-start | bytes 196616 | tf_op jit(solution)/shard_map/ppermute | solution.py:438
  50.0 4.3 %collective-permute-start.17 = (f32[128,128]{1,0:T(8,128)S(1)}, f32[128,128]{1,0:T(8,128)S(1)}, u32[]{:S(2)}, u32[]{:S(2)}) collective-permute-start(f32[128,128]{1,0:T(8,128)S(1)} %get-tuple-element.81.refs_0_), channel_id=1, source_target_pairs={{0,4},{1,5},{2,6},{3,7},{4,0},{5,1},{6,2},{7,3},{8,12},{9,13},{10,... | collective-permute-start | bytes 196616 | tf_op jit(solution)/shard_map/ppermute | solution.py:438
  50.1 7.9 %collective-permute-start.20 = (f32[2,4,16,128]{3,2,1,0:T(8,128)S(1)}, f32[2,4,16,128]{3,2,1,0:T(8,128)S(1)}, u32[]{:S(2)}, u32[]{:S(2)}) collective-permute-start(f32[2,4,16,128]{3,2,1,0:T(8,128)S(1)} %get-tuple-element.83), channel_id=1, source_target_pairs={{0,16},{1,17},{2,18},{3,19},{4,20},{5,21},{6,22},{7,23},{8,24},{9,... | collective-permute-start | bytes 196616 | tf_op jit(solution)/shard_map/ppermute | solution.py:438
  52.3 6.2 %collective-permute-start.21 = (f32[128,128]{1,0:T(8,128)S(1)}, f32[128,128]{1,0:T(8,128)S(1)}, u32[]{:S(2)}, u32[]{:S(2)}) collective-permute-start(f32[128,128]{1,0:T(8,128)S(1)} %get-tuple-element.81.refs_0_), channel_id=1, source_target_pairs={{0,2},{1,3},{2,0},{3,1},{4,6},{5,7},{6,4},{7,5},{8,10},{9,11},{10,... | collective-permute-start | bytes 196616 | tf_op jit(solution)/shard_map/ppermute | solution.py:438
  54.4 4.3 %collective-permute-start.18 = (f32[128,128]{1,0:T(8,128)S(1)}, f32[128,128]{1,0:T(8,128)S(1)}, u32[]{:S(2)}, u32[]{:S(2)}) collective-permute-start(f32[128,128]{1,0:T(8,128)S(1)} %collective-permute-done.17.refs_0_.refs_1_), channel_id=1, source_target_pairs={{0,2},{1,3},{2,0},{3,1},{4,6},{5,7},{6,4},{7,5},{8,10},{9,11},{10,... | collective-permute-start | bytes 196616 | tf_op jit(solution)/shard_map/ppermute | solution.py:438
  55.9 5.2 %collective-permute-start.19 = (f32[2,4,16,128]{3,2,1,0:T(8,128)S(1)}, f32[2,4,16,128]{3,2,1,0:T(8,128)S(1)}, u32[]{:S(2)}, u32[]{:S(2)}) collective-permute-start(f32[2,4,16,128]{3,2,1,0:T(8,128)S(1)} %get-tuple-element.82), channel_id=1, source_target_pairs={{0,12},{1,13},{2,14},{3,15},{4,8},{5,9},{6,10},{7,11},{8,4},{9,5},... | collective-permute-start | bytes 196616 | tf_op jit(solution)/shard_map/ppermute | solution.py:438
  58.0 4.2 %collective-permute-start.22 = (f32[128,128]{1,0:T(8,128)S(1)}, f32[128,128]{1,0:T(8,128)S(1)}, u32[]{:S(2)}, u32[]{:S(2)}) collective-permute-start(f32[128,128]{1,0:T(8,128)S(1)} %get-tuple-element.81.refs_0_), channel_id=1, source_target_pairs={{0,1},{1,0},{2,3},{3,2},{4,5},{5,4},{6,7},{7,6},{8,9},{9,8},{10,11... | collective-permute-start | bytes 196616 | tf_op jit(solution)/shard_map/ppermute | solution.py:438
  58.0 4.2 %collective-permute-start.23 = (f32[128,128]{1,0:T(8,128)S(1)}, f32[128,128]{1,0:T(8,128)S(1)}, u32[]{:S(2)}, u32[]{:S(2)}) collective-permute-start(f32[128,128]{1,0:T(8,128)S(1)} %collective-permute-done.17.refs_0_.refs_1_), channel_id=1, source_target_pairs={{0,1},{1,0},{2,3},{3,2},{4,5},{5,4},{6,7},{7,6},{8,9},{9,8},{10,11... | collective-permute-start | bytes 196616 | tf_op jit(solution)/shard_map/ppermute | solution.py:438
  58.5 3.7 %collective-permute-start.24 = (f32[128,128]{1,0:T(8,128)S(1)}, f32[128,128]{1,0:T(8,128)S(1)}, u32[]{:S(2)}, u32[]{:S(2)}) collective-permute-start(f32[128,128]{1,0:T(8,128)S(1)} %collective-permute-done.21.refs_2_), channel_id=1, source_target_pairs={{0,1},{1,0},{2,3},{3,2},{4,5},{5,4},{6,7},{7,6},{8,9},{9,8},{10,11... | collective-permute-start | bytes 196616 | tf_op jit(solution)/shard_map/ppermute | solution.py:438
  58.6 3.6 %collective-permute-start.25 = (f32[128,128]{1,0:T(8,128)S(1)}, f32[128,128]{1,0:T(8,128)S(1)}, u32[]{:S(2)}, u32[]{:S(2)}) collective-permute-start(f32[128,128]{1,0:T(8,128)S(1)} %collective-permute-done.18.refs_0_.refs_3_), channel_id=1, source_target_pairs={{0,1},{1,0},{2,3},{3,2},{4,5},{5,4},{6,7},{7,6},{8,9},{9,8},{10,11... | collective-permute-start | bytes 196616 | tf_op jit(solution)/shard_map/ppermute | solution.py:438

commit v4 on v3

--- a/solution.py
+++ b/solution.py
@@ -9,8 +9,7 @@
 
 F32, BF16 = jnp.float32, jnp.bfloat16
 K0COST = 50
-PARTS_DUE = 'plane'
-WINDOWS = [(0, 'plane'), (1, ('line', 1)), (1, ('line', 2)), ('plane', ('back', 0)), (('line', 1), ('back', 1)), (0, ('line', 1)), (1, ('line', 2))]
+WINDOWS = [(0, ('line', 1)), (1, ('line', 1)), ('plane', ('line', 2)), (('line', 1), None), (('line', 1), None), ('plane', ('line', 2)), ('plane', ('back', 0))]
 VMEM_LIMIT = 16 * 1024 * 1024
 
 
@@ -119,25 +118,28 @@
 def chains(targets, gates, right, left, made, kept):
     blocks, count, d, _ = gates.shape
     eye = identity(d)
+    left[1, count] = left_factor(eye)
+
+    def keep(block, g, p):
+        made[block] = p
+        if block:
+            right[block, g] = right_factor(p)
+            left[block, g] = left_factor(p)
+        else:
+            kept[g] = p
+
     for block in range(blocks):
-        left[block, count] = left_factor(eye)
-        made[block] = eye
-    made[blocks] = eye
-    made[blocks + 1] = eye
+        keep(block, count - 1, gates[block, count - 1])
+    low_turn = targets[0, count - 1] == 0
+    made[blocks] = jnp.where(low_turn, gates[0, count - 1], eye)
+    made[blocks + 1] = jnp.where(low_turn, eye, gates[0, count - 1])
 
     def step(i, _):
         g = count - 1 - i
         for block in range(blocks):
             u = gates[block, g]
-            after = jnp.minimum(g + 1, count - 1)
-            going = jnp.logical_and(i > 0, targets[block, g] == targets[block, after])
-            p = jnp.where(going, matmul(made[block], u), u)
-            made[block] = p
-            if block:
-                right[block, g] = right_factor(p)
-                left[block, g] = left_factor(p)
-            else:
-                kept[g] = p
+            going = targets[block, g] == targets[block, g + 1]
+            keep(block, g, jnp.where(going, matmul(made[block], u), u))
         both = made[pl.ds(blocks, 2)].reshape(2 * d, d)
         both = matmul(both, gates[0, g])
         low_turn = targets[0, g] == 0
@@ -145,10 +147,10 @@
         made[blocks + 1] = jnp.where(low_turn, made[blocks + 1], both[d:])
         return _
 
-    lax.fori_loop(0, count, step, 0)
-
-
-def block_kernel(block, at, finish_from, scale, targets, right, left, held, inner, grads, ready=None):
+    lax.fori_loop(1, count, step, 0)
+
+
+def block_kernel(block, at, scale, targets, right, left, held, inner, grads):
     _, slabs, rows, d = held.shape
     d = d // 2
     count = grads.shape[0]
@@ -174,8 +176,8 @@
                 r = dot(held[a, pl.ds(s, step)].reshape(step * rows, 2 * d), right[at, g])
                 held[a, pl.ds(s, step)] = fuse((r[:, :d] + r[:, d:]).reshape(step, rows, d))
 
-    def apply_mid(g, begin=0):
-        for s in range(begin, slabs, 2):
+    def apply_mid(g):
+        for s in range(0, slabs, 2):
             pairs = [(a, s + j) for a in range(2) for j in range(2)]
             x = jnp.concatenate([stacked(held[pair]) for pair in pairs], axis=1)
             r = dot(left[at, g], x)
@@ -190,18 +192,12 @@
         fresh = jnp.logical_or(i == 0, targets[block, g] != targets[block, jnp.minimum(g + 1, count - 1)])
         pl.when(jnp.logical_and(fresh, low_turn))(lambda: contract(g, contract_low))
         pl.when(jnp.logical_and(fresh, mid_turn))(lambda: contract(g, contract_mid))
-        if ready is not None:
-            pl.when(i == 0)(ready)
         turn = targets[block, g] != targets[block, jnp.maximum(g - 1, 0)]
         pl.when(jnp.logical_and(turn, low_turn))(lambda: apply_low(g))
         pl.when(jnp.logical_and(turn, mid_turn))(lambda: apply_mid(g))
         return _
 
     lax.fori_loop(0, count, step, 0)
-    if finish_from < slabs:
-        low_turn = targets[block, 0] == 0
-        pl.when(low_turn)(lambda: apply_low(0, finish_from))
-        pl.when(jnp.logical_not(low_turn))(lambda: apply_mid(0, finish_from))
     first = [count - 1] * count
     before = [count] * count
     for g in range(count - 2, -1, -1):
@@ -221,14 +217,12 @@
 
 
 def first_gradient_kernel(block, scale, *refs):
-    refs, (keep, send, far0, low0, mid0, held, inner, right, left, made, grads, near0, sem) = refs[:4], refs[4:]
-    gradient_kernel(block, scale, *refs, grads, near0, held, inner, right, left, made)
-    copy = pltpu.make_async_copy(near0, far0, sem)
-    copy.start()
+    refs, (keep, send, right0, left0, low0, mid0, held, inner, right, left, made, grads, products) = refs[:4], refs[4:]
+    gradient_kernel(block, scale, *refs, grads, products, held, inner, right, left, made)
+    build(products, right0, left0)
     low0[...] = right_factor(made[made.shape[0] - 2])
     mid0[...] = left_factor(made[made.shape[0] - 1])
     halves(grads, keep, send)
-    copy.wait()
 
 
 def build(products, right, left):
@@ -244,7 +238,7 @@
     for s in range(held.shape[1]):
         for a, ref in enumerate((state, costate)):
             held[a, s] = fuse(slab_of_native(ref, s))
-    block_kernel(block, block, held.shape[1], scale, targets, right, left, held, inner, out)
+    block_kernel(block, block, scale, targets, right, left, held, inner, out)
 
 
 def slabs_gradient_kernel(block, scale, targets, products, parts, out, held, inner, right, left):
@@ -252,18 +246,22 @@
     for s in range(held.shape[1]):
         for a in range(2):
             held[a, s] = fuse(slab_of_parts(parts, a, s))
-    block_kernel(block, 0, held.shape[1], scale, targets, right, left, held, inner, out)
-
-
-def early_kernel(n_qb, low, mid, *refs):
-    blocks, (out, held) = refs[:n_qb], refs[n_qb:]
-    n, _, slabs, r, d = out.shape
+    block_kernel(block, 0, scale, targets, right, left, held, inner, out)
+
+
+def end_kernel(n_qb, low, mid, *refs):
+    blocks, outs, held = refs[:n_qb], refs[n_qb:-1], refs[-1]
     gather(blocks, lambda rows, x: held.__setitem__((slice(None), slice(None), rows), x))
+    _, slabs, rows, d = held.shape
     for s in range(slabs):
         z = times_right(jnp.concatenate([held[0, s], held[1, s]], axis=0), low[...])
-        z = times_left(mid[...], jnp.concatenate([z[: n * r], z[n * r :]], axis=1))
-        for a in range(2):
-            out[:, a, s] = z[:, a * d : (a + 1) * d].reshape(n, r, d)
+        z = times_left(mid[...], jnp.concatenate([z[:rows], z[rows:]], axis=1))
+        held[0, s] = z[:, :d]
+        held[1, s] = z[:, d:]
+    for k, ref in enumerate(outs):
+        count = ref.shape[2]
+        start = (lax.axis_index("qa") ^ k) * count
+        ref[...] = held[:, :, pl.ds(pl.multiple_of(start, count), count)]
 
 
 def gather(blocks, put):
@@ -273,30 +271,16 @@
         put(pl.ds(pl.multiple_of((mine ^ k) * count, count), count), ref[...])
 
 
-def second_kernel(block, n_qa, n_qb, early, scale, targets, products, *refs):
-    blocks, outs = (refs[:n_qb], refs[n_qb : 2 * n_qb]), refs[2 * n_qb : 2 * n_qb + n_qa]
-    keep, send, held, inner, grads, here, right, left, sem = refs[2 * n_qb + n_qa :]
-    copy = pltpu.make_async_copy(products, here, sem)
-    copy.start()
-
-    def ready():
-        copy.wait()
-        build(here, right, left)
-
-    d = inner.shape[-1]
-    for slabs, part in zip((slice(0, early), slice(early, None)), blocks):
-        gather(part, lambda rows, x: held.__setitem__((slice(None), slabs, rows), fuse(x)))
-    block_kernel(block, 0, early, scale, targets, right, left, held, inner, grads, ready)
-    for k, ref in enumerate(outs):
-        count = ref.shape[2]
-        rows = pl.ds(pl.multiple_of((lax.axis_index("qa") ^ k) * count, count), count)
-        part = held[:, early:, rows].astype(F32)
-        ref[...] = part[..., :d] + part[..., d:]
+def second_kernel(block, n_qb, scale, targets, right, left, *refs):
+    blocks = refs[:n_qb]
+    keep, send, held, inner, grads = refs[n_qb:]
+    gather(blocks, lambda rows, x: held.__setitem__((slice(None), slice(None), rows), fuse(x)))
+    block_kernel(block, 0, scale, targets, right, left, held, inner, grads)
     halves(grads, keep, send)
 
 
 def first_kernel(block, n_qb, far_targets, gates, state, costate, *refs):
-    outs, (targets, mats, x_ref, y_ref, turned, sems) = refs[: 2 * n_qb], refs[2 * n_qb :]
+    outs, (targets, mats, x_ref, y_ref, turned, sems) = refs[:n_qb], refs[n_qb:]
     copies = [
         pltpu.make_async_copy(far_targets, targets, sems.at[3]),
         pltpu.make_async_copy(gates.at[pl.ds(block, 1)], mats, sems.at[0]),
@@ -305,8 +289,7 @@
     ]
     for copy in copies:
         copy.start()
-    slabs = x_ref.shape[1]
-    _, early, r, d = outs[0].shape
+    _, slabs, r, d = outs[0].shape
     mine = lax.axis_index("qb")
     copies[0].wait()
     copies[1].wait()
@@ -323,57 +306,53 @@
         x, y = slab_of_native(x_ref, s), slab_of_native(y_ref, s)
         z = times_right(jnp.concatenate([x, y], axis=0), low)
         z = times_left(mid, jnp.concatenate([z[:d], z[d:]], axis=1))
-        late, i = (0, s) if s < early else (1, s - early)
-        for k, out in enumerate(outs[late * n_qb : (late + 1) * n_qb]):
-            out[0, i] = z[k * r : (k + 1) * r, :d]
-            out[1, i] = z[k * r : (k + 1) * r, d:]
-
-
-def split_sum_kernel(bit, shared, keep, got, *refs):
-    outs, total = refs[:-1], refs[-1]
-    total[...] = keep[...] + got[...]
-    split_total(bit, shared, outs, total)
-
-
-def split_total(bit, shared, outs, total):
-    axis, weight = bit
-    mine = (lax.axis_index(axis) // weight) % 2
-    first = total.shape[0] - shared
-    for which, out in enumerate(outs):
-        half = first // 2
-        start = (mine ^ which) * half
-        out[:half] = total[pl.ds(pl.multiple_of(start, half), half), :]
-        rest = out.shape[0] - half
-        if rest and rest == shared:
-            out[half:] = total[first:]
-        elif rest:
-            start = pl.multiple_of(first + (mine ^ which) * rest, rest)
-            out[half:] = total[pl.ds(start, rest), :]
-
-
-def join_split_kernel(bit, keep0, got0, keep1, got1, *refs):
-    outs, total = refs[:-1], refs[-1]
-    shared = keep1.shape[0]
-    total[:-shared] = keep0[...] + got0[...]
-    total[-shared:] = keep1[...] + got1[...]
-    split_total(bit, shared, outs, total)
+        for k, out in enumerate(outs):
+            out[0, s] = z[k * r : (k + 1) * r, :d]
+            out[1, s] = z[k * r : (k + 1) * r, d:]
+
+
+def plane_partners(n_qb):
+    return [(dx, dy) for dx in range(2) for dy in range(n_qb // 2)]
+
+
+def place_of(n_qb, dx, dy):
+    x, y = lax.axis_index("qa") % 2, lax.axis_index("qb") // 2
+    return (x ^ dx) * (n_qb // 2) + (y ^ dy)
+
+
+def spread_kernel(n_qb, *refs):
+    pairs, (*outs, total) = refs[:4], refs[4:]
+    for block in range(2):
+        total[block] = pairs[2 * block][...] + pairs[2 * block + 1][...]
+    size = total.shape[1] // n_qb
+    for (dx, dy), out in zip(plane_partners(n_qb), outs):
+        rows = pl.ds(pl.multiple_of(place_of(n_qb, dx, dy) * size, size), size)
+        for block in range(2):
+            out[block * size : (block + 1) * size] = total[block, rows]
+
+
+def plane_sum_kernel(*refs):
+    refs[-1][...] = functools.reduce(lambda a, b: a + b, [ref[...] for ref in refs[:-1]])
 
 
 def sum_kernel(keep, got, out):
     out[...] = keep[...] + got[...]
 
 
-def collect_kernel(orders, back, *refs):
-    ins, out = refs[:-1], refs[-1]
+def collect_kernel(n_qb, *refs):
+    ins, (out, held, sem) = refs[:-3], refs[-3:]
     size = ins[0].shape[0] // 2
-    for i, ref in enumerate(ins):
-        for block, order in enumerate(orders):
-            row = 0
-            for axis, weight in order:
-                delta = (i >> back.index((axis, weight))) & 1
-                row = row * 2 + ((lax.axis_index(axis) // weight) % 2) ^ delta
-            row = pl.multiple_of(row * size, size)
-            out[block, pl.ds(row, size), :] = ref[block * size : (block + 1) * size]
+    copies = []
+    for block in range(2):
+        for i, ref in enumerate(ins):
+            core = (lax.axis_index("qb") % 2) ^ (i // n_qb)
+            row = core * n_qb + place_of(n_qb, *plane_partners(n_qb)[i % n_qb])
+            rows = pl.ds(pl.multiple_of(row * size, size), size)
+            held[block, rows] = ref[block * size : (block + 1) * size]
+        copies.append(pltpu.make_async_copy(held.at[block], out.at[block], sem.at[block]))
+        copies[-1].start()
+    for copy in copies:
+        copy.wait()
 
 
 def store_kernel(parts, first, second):
@@ -384,20 +363,21 @@
             flat[pl.ds(s, n * r, stride=slabs), :] = slab_of_parts(parts, a, s)
 
 
-def place_kernel(n_qa, parts, *refs):
-    blocks, outs = refs[:n_qa], refs[n_qa:]
-    rows, slabs, d = outs[0].shape
-    r, early = rows // n_qa, parts.shape[2]
+def place_kernel(n_qa, *refs):
+    blocks, (*outs, held, sem) = refs[:n_qa], refs[n_qa:]
+    _, rows, slabs, d = held.shape
+    r = rows // n_qa
+    copies = []
     for a, out in enumerate(outs):
-        flat = out.reshape(rows * slabs, d)
-        for s in range(early):
-            flat[pl.ds(s, rows, stride=slabs), :] = slab_of_parts(parts, a, s)
-    for k, ref in enumerate(blocks):
-        start = pl.multiple_of((lax.axis_index("qa") ^ k) * (r * slabs), r * slabs)
-        for a, out in enumerate(outs):
-            flat = out.reshape(rows * slabs, d)
-            for s in range(early, slabs):
-                flat[pl.ds(start + s, r, stride=slabs), :] = ref[a, s - early]
+        flat = held.at[a].reshape(rows * slabs, d)
+        for k, ref in enumerate(blocks):
+            start = pl.multiple_of((lax.axis_index("qa") ^ k) * (r * slabs), r * slabs)
+            for s in range(slabs):
+                flat[pl.ds(start + s, r, stride=slabs), :] = ref[a, s]
+        copies.append(pltpu.make_async_copy(held.at[a], out, sem.at[a]))
+        copies[-1].start()
+    for copy in copies:
+        copy.wait()
 
 
 def call(kernel, out_shape, inputs, scratch=(), flops=0, far=(), far_out=(), ride=()):
@@ -471,7 +451,6 @@
 
     products0 = shape(count, d, d)
     chain = [pltpu.VMEM(x, BF16) for x in factors(2)] + [pltpu.VMEM((4, d, d), F32)]
-    early = slabs // 2
     work = 2 * 2 * 2 * 4 * rows * slabs * d * d
     every = count * d
 
@@ -494,7 +473,7 @@
     else:
         blocks = call(
             functools.partial(first_kernel, 1, n_qb),
-            [shape(2, n, r, d) for n in (early, slabs - early) for _ in range(n_qb)],
+            [shape(2, slabs, r, d)] * n_qb,
             [pltpu.with_memory_space_constraint(x, pltpu.HBM) for x in (targets, gates, *natives)],
             [
                 pltpu.SMEM(targets.shape, jnp.int32),
@@ -507,43 +486,34 @@
             work,
             far=(0, 1, 2, 3),
         )
-        front, rear = blocks[:n_qb], blocks[n_qb:]
-        front = front[:1] + [exchange(x, 0, k) for k, x in enumerate(front) if k]
-        rear = rear[:1] + [exchange(x, 0, k) for k, x in enumerate(rear) if k]
-        bits = [("qb", 1 << i) for i in range(n_qb.bit_length() - 1)]
-        across_x = ("qa", 1)
-
-        def across(x, bit):
-            return exchange(x, bit[1], 0) if bit[0] == "qa" else exchange(x, 0, bit[1])
-
+        blocks = blocks[:1] + [exchange(x, 0, k) for k, x in enumerate(blocks) if k]
         half = shape(every // 2, d)
         square = jax.ShapeDtypeStruct((2 * d, 2 * d), BF16)
-        keep1, send1, products, low, mid = call(
+        keep1, send1, right0, left0, low, mid = call(
             functools.partial(first_gradient_kernel, 1, scale),
-            [half, half, products0, square, square],
+            [half, half, *(jax.ShapeDtypeStruct(x, BF16) for x in factors(1)), square, square],
             [targets, gates, *natives],
-            [held, inner, *chain, inner, inner, pltpu.SemaphoreType.DMA],
+            [held, inner, *chain, inner, inner],
             10 * work,
-            far_out=(2,),
-        )
-        got1 = across(send1, bits[0])
-        sent = call(
-            functools.partial(early_kernel, n_qb),
-            shape(n_qa, 2, early, rows // n_qa, d),
-            [low, mid, *front],
-            [pltpu.VMEM((2, early, rows, d), F32)],
+        )
+        got1 = exchange(send1, 0, 1)
+        keep0, send0 = call(
+            functools.partial(second_kernel, 0, n_qb, scale),
+            [half, half],
+            [targets, right0, left0, *blocks],
+            [held, inner, inner],
+            K0COST * work,
+        )
+        got0 = exchange(send0, 0, 1)
+        moved, _ = call(
+            functools.partial(end_kernel, n_qb),
+            [shape(2, slabs, rows // n_qa, d)] * n_qa,
+            [low, mid, *blocks],
+            [pltpu.VMEM((2, slabs, rows, d), F32)],
             3 * work,
-        )
-        parts = lax.all_to_all(sent, "qa", 0, 0, tiled=True)
-        *moved, keep0, send0 = call(
-            functools.partial(second_kernel, 0, n_qa, n_qb, early, scale),
-            [shape(2, slabs - early, rows // n_qa, d)] * n_qa + [half, half],
-            [targets, products, *front, *rear],
-            [held, inner, inner, inner, *(pltpu.VMEM(x, BF16) for x in factors(1)), pltpu.SemaphoreType.DMA],
-            K0COST * work,
-            far=(1,),
-        )
-        came = {0: moved[0], "parts": parts}
+            ride=[keep0],
+        )
+        came = {0: moved[0]}
         moved = dict(enumerate(moved))
         window = windows(n_qa)
 
@@ -551,8 +521,6 @@
             due = [k for k in window if window[k][1] == stage]
             opens = [k for k in window if window[k][0] == stage]
             ride = [came[k] for k in due] + [moved[k] for k in opens]
-            if stage == PARTS_DUE:
-                ride, due = [came["parts"], *ride], ["parts", *due]
             if not ride:
                 return call(kernel, out_shape, inputs, scratch, far=far) if out_shape else None
             result, rode = call(kernel, out_shape, inputs, scratch, far=far, ride=ride)
@@ -567,34 +535,37 @@
                     came[k] = exchange(moved[k], k, 0)
 
         start(0)
-        keep, got = (keep0, keep1), (across(send0, bits[0]), got1)
-        bits = bits + [across_x]
-        size = every // 2
-        for i, bit in enumerate(bits[1:]):
-            if i == 0:
-                kernel, inputs = functools.partial(join_split_kernel, bit), [keep[0], got[0], keep[1], got[1]]
-            else:
-                kernel, inputs = functools.partial(split_sum_kernel, bit, size), [keep, got]
-            scratch = [pltpu.VMEM((2 * size, d), F32)]
-            keep, send = after(i + 1, kernel, [shape(size, d)] * 2, inputs, scratch)
-            got = across(send, bit)
-            size = size // 2
-        mine = after("plane", sum_kernel, shape(*keep.shape), [keep, got])
+        partners = plane_partners(n_qb)
+        size = every // n_qb
+        pieces = after(
+            1,
+            functools.partial(spread_kernel, n_qb),
+            [shape(size, d)] * n_qb,
+            [keep0, got0, keep1, got1],
+            [pltpu.VMEM((2, every // 2, d), F32)],
+        )
+        pieces = pieces[:1] + [exchange(x, dx, 2 * dy) for x, (dx, dy) in zip(pieces[1:], partners[1:])]
+        mine = after("plane", plane_sum_kernel, shape(size, d), pieces)
         for i in range(1, n_qa.bit_length() - 1):
             got = exchange(mine, 1 << i, 0)
             mine = after(("line", i), sum_kernel, shape(*mine.shape), [mine, got])
-        back = list(reversed(bits))
-        found = [mine]
-        for i, bit in enumerate(back):
-            found = found + [across(x, bit) for x in found]
-            after(("back", i), nothing, [], [found[-1]], far=(0,))
+        found = [mine] + [exchange(mine, dx, 2 * dy) for dx, dy in partners[1:]]
+        after(("back", 0), nothing, [], [found[1]], far=(0,))
+        after(("back", 1), nothing, [], [found[-1]], far=(0,))
+        found = found + [exchange(x, 0, 1) for x in found]
         whole = call(
-            functools.partial(collect_kernel, [bits, bits], back), shape(gates.shape[0], every, d), found
+            functools.partial(collect_kernel, n_qb),
+            shape(gates.shape[0], every, d),
+            found,
+            [pltpu.VMEM((gates.shape[0], every, d), F32), pltpu.SemaphoreType.DMA((2,))],
+            far_out=(0,),
         )
         first, second = call(
             functools.partial(place_kernel, n_qa),
             (native, native),
-            [came["parts"], *(came[k] for k in range(n_qa))],
+            [came[k] for k in range(n_qa)],
+            [pltpu.VMEM((2, *native.shape), F32), pltpu.SemaphoreType.DMA((2,))],
+            far_out=(0, 1),
         )
     return first.reshape(layout), second.reshape(layout), whole.reshape(gates.shape)
 

time: 63.3 us -> 57.7 us (0.912); the launches traced: 63.1 us -> 56.8 us
  starting transfers between devices: 38.2 us -> 24.6 us
  waiting for transfers between devices: 9.44 us -> 19 us
  Pallas kernels: 14.7 us -> 12.4 us
    ppermute x26 -> x24, waiting for transfers between devices: 8.99 us -> 19 us  [exchange(): return lax.ppermute(x, ('qa', 'qb'), pairs)]
    ppermute x26 -> x24, starting transfers between devices: 32.2 us -> 24.6 us  [exchange(): return lax.ppermute(x, ('qa', 'qb'), pairs)]
    all_to_all x1 -> x0, starting transfers between devices: 5.95 us -> none  [shards(): parts = lax.all_to_all(sent, 'qa', 0, 0, tiled=True)]
    pallas_call x13 -> x11, Pallas kernels: 14.7 us -> 12.4 us  [call(): pl.pallas_call(body, out_shape=outs + [shape(*x.shape) for x in ride], in...]
  transfers between devices with their start and end apart: 27 -> 24, of which waited for: 7 -> 11; matrix products, arithmetic and copies ran while one was open for 0% -> 0% of each run, Pallas kernels for 18% -> 16%
where the time goes in v4:
time: 57.7 us; the launch traced here: 56.8 us
  starting transfers between devices  24.6 us (43%)
  waiting for transfers between devices  19 us (33%)
  Pallas kernels  12.4 us (21%)
  between operations  0.78 us (1%)
    ppermute x24, starting transfers between devices, exchange(): return lax.ppermute(x, ('qa', 'qb'), pairs)  24.6 us
    ppermute x24, waiting for transfers between devices, exchange(): return lax.ppermute(x, ('qa', 'qb'), pairs)  19 us
    pallas_call x11, Pallas kernels, call(): pl.pallas_call(body, out_shape=outs + [shape(*x.shape) for x in ride], in...  12.4 us
  transfers between devices with their start and end apart: 24, of which 11 were waited for; matrix products, arithmetic and copies ran while one was open for 0% of the time, Pallas kernels for 16%

profile of v4, /device:TPU:0, one launch (start us, length us, event | category | flops | bytes accessed | tf_op | source)
XLA Modules:
  0.0 56.8 jit_solution(15860569480513913947)
XLA Ops:
  0.7 2.6 %shard_map.68 = (f32[2,8,32,128]{3,2,1,0:T(8,128)S(1)}, f32[2,8,32,128]{3,2,1,0:T(8,128)S(1)}, f32[2,8,32,128]{3,2,1,0:T(8,128)S(1)}, f32[2,8,32,128]{3,2,1,0:T(8,128)S(1)}) custom-call(s32[2,4]{1,0:T(2,128)} %refs_0_.5, f32[2,4,128,128]{3,2,1,0:T(8,128)} %refs_1_.3, f32[128,8,128]{2,1,0:T(8,128)} %bitcast.5, f32[128,8,128]{2,1,0:T(8,128)} %bitcast.7), custom_call_target="tpu_custom_call" | custom-call | flops 536870912 | bytes 2621472 | tf_op jit(solution)/shard_map/pallas_call | solution.py:397
  3.2 0.5 collective-permute-start
  3.7 2.6 %collective-permute-start.1 = (f32[2,8,32,128]{3,2,1,0:T(8,128)S(1)}, f32[2,8,32,128]{3,2,1,0:T(8,128)S(1)}, u32[]{:S(2)}, u32[]{:S(2)}) collective-permute-start(f32[2,8,32,128]{3,2,1,0:T(8,128)S(1)} %get-tuple-element.46), channel_id=1, source_target_pairs={{0,2},{1,3},{2,0},{3,1},{4,6},{5,7},{6,4},{7,5},{8,10},{9,11},{10,... | collective-permute-start | bytes 786440 | tf_op jit(solution)/shard_map/ppermute | solution.py:418
  6.4 4.4 %shard_map.67 = (f32[256,128]{1,0:T(8,128)S(1)}, f32[256,128]{1,0:T(8,128)S(1)}, bf16[1,4,256,256]{3,2,1,0:T(8,128)(2,1)S(1)}, bf16[1,5,256,256]{3,2,1,0:T(8,128...) custom-call(s32[2,4]{1,0:T(2,128)S(1)} %copy-done.3, f32[2,4,128,128]{3,2,1,0:T(8,128)S(1)} %copy-done, ...), custom_call_target="tpu_custom_call" | custom-call | flops 5368709120 | bytes 4718624 | tf_op jit(solution)/shard_map/pallas_call | solution.py:397
  11.0 2.5 %collective-permute-done.1.refs_5_.refs_4_ = f32[2,8,32,128]{3,2,1,0:T(8,128)S(1)} collective-permute-done((f32[2,8,32,128]{3,2,1,0:T(8,128)S(1)}, f32[2,8,32,128]{3,2,1,0:T(8,128)S(1)}, u32[]{:S(2)}, u32[]{:S(2)}) %collective-permute-start.1) | collective-permute-done | bytes 262176 | tf_op jit(solution)/shard_map/ppermute | solution.py:418
  13.5 5.1 %collective-permute-done.2.refs_6_.refs_5_ = f32[2,8,32,128]{3,2,1,0:T(8,128)S(1)} collective-permute-done((f32[2,8,32,128]{3,2,1,0:T(8,128)S(1)}, f32[2,8,32,128]{3,2,1,0:T(8,128)S(1)}, u32[]{:S(2)}, u32[]{:S(2)}) %collective-permute-start.2) | collective-permute-done | bytes 262176 | tf_op jit(solution)/shard_map/ppermute | solution.py:418
  18.6 2.4 %shard_map.69 = (f32[256,128]{1,0:T(8,128)S(1)}, f32[256,128]{1,0:T(8,128)S(1)}) custom-call(s32[2,4]{1,0:T(2,128)S(1)} %copy-done.3, bf16[1,4,256,256]{3,2,1,0:T(8,128)(2,1)S(1)} %get-tuple-element.48.refs_1_, bf16[1,5,256,256]{3,2,1,0:T(8,128)(2,1)S(1)} %get-tuple-element.49.refs_2_, f32[2,8,32,128]{3,2,1,0:T(8,128)S(1)} %get-tuple-element.44.refs_3_.refs_2_, ...), custom_call_target="tpu_custom_call" | custom-call | flops 26843545600 | bytes 3670048 | tf_op jit(solution)/shard_map/pallas_call | solution.py:397
  21.2 1.0 %shard_map.70 = (f32[2,8,16,128]{3,2,1,0:T(8,128)S(1)}, f32[2,8,16,128]{3,2,1,0:T(8,128)S(1)}, f32[2,8,16,128]{3,2,1,0:T(8,128)S(1)}, f32[2,8,16,128]{3,2,1,0:T(...) custom-call(bf16[256,256]{1,0:T(8,128)(2,1)S(1)} %get-tuple-element., ...), custom_call_target="tpu_custom_call", output_to_operand_aliasing={{8}: (6, {})} | custom-call | flops 1610612736 | bytes 2621440 | tf_op jit(solution)/shard_map/pallas_call | solution.py:397
  22.3 4.8 %collective-permute-start.9 = (f32[2,8,16,128]{3,2,1,0:T(8,128)S(1)}, f32[2,8,16,128]{3,2,1,0:T(8,128)S(1)}, u32[]{:S(2)}, u32[]{:S(2)}) collective-permute-start(f32[2,8,16,128]{3,2,1,0:T(8,128)S(1)} %get-tuple-element.64), channel_id=1, source_target_pairs={{0,28},{1,29},{2,30},{3,31},{4,24},{5,25},{6,26},{7,27},{8,20},{9,... | collective-permute-start | bytes 393224 | tf_op jit(solution)/shard_map/ppermute | solution.py:418
  27.1 1.6 %collective-permute-start.5 = (f32[128,128]{1,0:T(8,128)S(1)}, f32[128,128]{1,0:T(8,128)S(1)}, u32[]{:S(2)}, u32[]{:S(2)}) collective-permute-start(f32[128,128]{1,0:T(8,128)S(1)} %get-tuple-element.57), channel_id=1, source_target_pairs={{0,2},{1,3},{2,0},{3,1},{4,6},{5,7},{6,4},{7,5},{8,10},{9,11},{10,... | collective-permute-start | bytes 196616 | tf_op jit(solution)/shard_map/ppermute | solution.py:418
  28.7 0.5 collective-permute-start.6
  29.2 1.4 %collective-permute-start.7 = (f32[128,128]{1,0:T(8,128)S(1)}, f32[128,128]{1,0:T(8,128)S(1)}, u32[]{:S(2)}, u32[]{:S(2)}) collective-permute-start(f32[128,128]{1,0:T(8,128)S(1)} %get-tuple-element.59), channel_id=1, source_target_pairs={{0,6},{1,7},{2,4},{3,5},{4,2},{5,3},{6,0},{7,1},{8,14},{9,15},{10,... | collective-permute-start | bytes 196616 | tf_op jit(solution)/shard_map/ppermute | solution.py:418
  30.9 0.6 collective-permute-done.5.refs_1_
  31.5 1.7 %collective-permute-done.6.refs_2_ = f32[128,128]{1,0:T(8,128)S(1)} collective-permute-done((f32[128,128]{1,0:T(8,128)S(1)}, f32[128,128]{1,0:T(8,128)S(1)}, u32[]{:S(2)}, u32[]{:S(2)}) %collective-permute-start.6) | collective-permute-done | bytes 65568 | tf_op jit(solution)/shard_map/ppermute | solution.py:418
  33.2 1.7 %collective-permute-done.7.refs_3_ = f32[128,128]{1,0:T(8,128)S(1)} collective-permute-done((f32[128,128]{1,0:T(8,128)S(1)}, f32[128,128]{1,0:T(8,128)S(1)}, u32[]{:S(2)}, u32[]{:S(2)}) %collective-permute-start.7) | collective-permute-done | bytes 65568 | tf_op jit(solution)/shard_map/ppermute | solution.py:418
  34.8 0.9 %collective-permute-start.8 = (f32[128,128]{1,0:T(8,128)S(1)}, f32[128,128]{1,0:T(8,128)S(1)}, u32[]{:S(2)}, u32[]{:S(2)}) collective-permute-start(f32[128,128]{1,0:T(8,128)S(1)} %get-tuple-element.63.refs_0_), channel_id=1, source_target_pairs={{0,8},{1,9},{2,10},{3,11},{4,12},{5,13},{6,14},{7,15},{8,0},{9,1},... | collective-permute-start | bytes 196616 | tf_op jit(solution)/shard_map/ppermute | solution.py:418
  35.7 2.4 %collective-permute-start.12 = (f32[2,8,16,128]{3,2,1,0:T(8,128)S(1)}, f32[2,8,16,128]{3,2,1,0:T(8,128)S(1)}, u32[]{:S(2)}, u32[]{:S(2)}) collective-permute-start(f32[2,8,16,128]{3,2,1,0:T(8,128)S(1)} %get-tuple-element.69), channel_id=1, source_target_pairs={{0,20},{1,21},{2,22},{3,23},{4,16},{5,17},{6,18},{7,19},{8,28},{9,... | collective-permute-start | bytes 393224 | tf_op jit(solution)/shard_map/ppermute | solution.py:418
  38.2 1.3 %collective-permute-start.15 = (f32[2,8,16,128]{3,2,1,0:T(8,128)S(1)}, f32[2,8,16,128]{3,2,1,0:T(8,128)S(1)}, u32[]{:S(2)}, u32[]{:S(2)}) collective-permute-start(f32[2,8,16,128]{3,2,1,0:T(8,128)S(1)} %get-tuple-element.72), channel_id=1, source_target_pairs={{0,4},{1,5},{2,6},{3,7},{4,0},{5,1},{6,2},{7,3},{8,12},{9,13},{10,... | collective-permute-start | bytes 393224 | tf_op jit(solution)/shard_map/ppermute | solution.py:418
  39.5 0.9 %collective-permute-done.8.refs_1_ = f32[128,128]{1,0:T(8,128)S(1)} collective-permute-done((f32[128,128]{1,0:T(8,128)S(1)}, f32[128,128]{1,0:T(8,128)S(1)}, u32[]{:S(2)}, u32[]{:S(2)}) %collective-permute-start.8) | collective-permute-done | bytes 65568 | tf_op jit(solution)/shard_map/ppermute | solution.py:418
  40.4 1.0 %collective-permute-start.11 = (f32[128,128]{1,0:T(8,128)S(1)}, f32[128,128]{1,0:T(8,128)S(1)}, u32[]{:S(2)}, u32[]{:S(2)}) collective-permute-start(f32[128,128]{1,0:T(8,128)S(1)} %get-tuple-element.68.refs_0_), channel_id=1, source_target_pairs={{0,16},{1,17},{2,18},{3,19},{4,20},{5,21},{6,22},{7,23},{8,24},{9,... | collective-permute-start | bytes 196616 | tf_op jit(solution)/shard_map/ppermute | solution.py:418
  41.4 2.6 %collective-permute-start.16 = (f32[2,8,16,128]{3,2,1,0:T(8,128)S(1)}, f32[2,8,16,128]{3,2,1,0:T(8,128)S(1)}, u32[]{:S(2)}, u32[]{:S(2)}) collective-permute-start(f32[2,8,16,128]{3,2,1,0:T(8,128)S(1)} %get-tuple-element.74), channel_id=1, source_target_pairs={{0,12},{1,13},{2,14},{3,15},{4,8},{5,9},{6,10},{7,11},{8,4},{9,5},... | collective-permute-start | bytes 393224 | tf_op jit(solution)/shard_map/ppermute | solution.py:418
  44.0 2.1 %collective-permute-done.12.refs_2_ = f32[2,8,16,128]{3,2,1,0:T(8,128)S(1)} collective-permute-done((f32[2,8,16,128]{3,2,1,0:T(8,128)S(1)}, f32[2,8,16,128]{3,2,1,0:T(8,128)S(1)}, u32[]{:S(2)}, u32[]{:S(2)}) %collective-permute-start.12) | collective-permute-done | bytes 131104 | tf_op jit(solution)/shard_map/ppermute | solution.py:418
  46.2 1.7 %collective-permute-done.13.refs_3_ = f32[2,8,16,128]{3,2,1,0:T(8,128)S(1)} collective-permute-done((f32[2,8,16,128]{3,2,1,0:T(8,128)S(1)}, f32[2,8,16,128]{3,2,1,0:T(8,128)S(1)}, u32[]{:S(2)}, u32[]{:S(2)}) %collective-permute-start.13) | collective-permute-done | bytes 131104 | tf_op jit(solution)/shard_map/ppermute | solution.py:418
  47.9 1.2 %collective-permute-start.19 = (f32[128,128]{1,0:T(8,128)S(1)}, f32[128,128]{1,0:T(8,128)S(1)}, u32[]{:S(2)}, u32[]{:S(2)}) collective-permute-start(f32[128,128]{1,0:T(8,128)S(1)} %get-tuple-element.71.refs_0_), channel_id=1, source_target_pairs={{0,6},{1,7},{2,4},{3,5},{4,2},{5,3},{6,0},{7,1},{8,14},{9,15},{10,... | collective-permute-start | bytes 196616 | tf_op jit(solution)/shard_map/ppermute | solution.py:418
  49.2 0.8 %collective-permute-start.18 = (f32[128,128]{1,0:T(8,128)S(1)}, f32[128,128]{1,0:T(8,128)S(1)}, u32[]{:S(2)}, u32[]{:S(2)}) collective-permute-start(f32[128,128]{1,0:T(8,128)S(1)} %get-tuple-element.71.refs_0_), channel_id=1, source_target_pairs={{0,4},{1,5},{2,6},{3,7},{4,0},{5,1},{6,2},{7,3},{8,12},{9,13},{10,... | collective-permute-start | bytes 196616 | tf_op jit(solution)/shard_map/ppermute | solution.py:418
  50.0 1.5 %collective-permute-start.14 = (f32[128,128]{1,0:T(8,128)S(1)}, f32[128,128]{1,0:T(8,128)S(1)}, u32[]{:S(2)}, u32[]{:S(2)}) collective-permute-start(f32[128,128]{1,0:T(8,128)S(1)} %get-tuple-element.71.refs_0_), channel_id=1, source_target_pairs={{0,2},{1,3},{2,0},{3,1},{4,6},{5,7},{6,4},{7,5},{8,10},{9,11},{10,... | collective-permute-start | bytes 196616 | tf_op jit(solution)/shard_map/ppermute | solution.py:418
  51.5 1.7 %collective-permute-done.19.refs_3_ = f32[128,128]{1,0:T(8,128)S(1)} collective-permute-done((f32[128,128]{1,0:T(8,128)S(1)}, f32[128,128]{1,0:T(8,128)S(1)}, u32[]{:S(2)}, u32[]{:S(2)}) %collective-permute-start.19) | collective-permute-done | bytes 65568 | tf_op jit(solution)/shard_map/ppermute | solution.py:418
  53.2 0.6 %collective-permute-done.18.refs_2_ = f32[128,128]{1,0:T(8,128)S(1)} collective-permute-done((f32[128,128]{1,0:T(8,128)S(1)}, f32[128,128]{1,0:T(8,128)S(1)}, u32[]{:S(2)}, u32[]{:S(2)}) %collective-permute-start.18) | collective-permute-done | bytes 65568 | tf_op jit(solution)/shard_map/ppermute | solution.py:418
  53.8 0.5 collective-permute-done.14.refs_0_.refs_1_
  54.3 0.5 collective-permute-start.21
  54.8 1.1 %shard_map.76 = (f32[128,8,128]{2,1,0:T(8,128)}, f32[128,8,128]{2,1,0:T(8,128)}) custom-call(f32[2,8,16,128]{3,2,1,0:T(8,128)S(1)} %get-tuple-element.51.refs_0_, f32[2,8,16,128]{3,2,1,0:T(8,128)S(1)} %shard_map.75.refs_1_, f32[2,8,16,128]{3,2,1,0:T(8,128)S(1)} %get-tuple-element.73.refs_2_, f32[2,8,16,128]{3,2,1,0:T(8,128)S(1)} %collective-permute-done.16.refs_3_, ...), custom_call_target="tpu_custom_call" | custom-call | bytes 2097152 | tf_op jit(solution)/shard_map/pallas_call | solution.py:397
  55.9 0.8 %shard_map.77 = f32[2,512,128]{2,1,0:T(8,128)} custom-call(f32[128,128]{1,0:T(8,128)S(1)} %get-tuple-element.71.refs_0_, f32[128,128]{1,0:T(8,128)S(1)} %collective-permute-done.14.refs_0_.refs_1_, f32[128,128]{1,0:T(8,128)S(1)} %collective-permute-done.18.refs_2_, f32[128,128]{1,0:T(8,128)S(1)} %collective-permute-done.19.refs_3_, ...), custom_call_target="tpu_custom_call" | custom-call | bytes 1048576 | tf_op jit(solution)/shard_map/pallas_call | solution.py:397
  (36 shorter events, 1.0 us)
Async XLA Ops:
  0.6 5.8 %copy-start = (f32[2,4,128,128]{3,2,1,0:T(8,128)S(1)}, f32[2,4,128,128]{3,2,1,0:T(8,128)}, u32[]{:S(2)}) copy-start(f32[2,4,128,128]{3,2,1,0:T(8,128)} %refs_1_.3) | copy-start | bytes 1572868
  0.6 5.8 %copy-start.1 = (f32[1,1,128,8,128]{4,3,2,1,0:T(8,128)S(1)}, f32[1,1,128,8,128]{4,3,2,1,0:T(8,128)}, u32[]{:S(2)}) copy-start(f32[1,1,128,8,128]{4,3,2,1,0:T(8,128)} %param.4) | copy-start | bytes 1572868
  0.7 5.8 %copy-start.2 = (f32[1,1,128,8,128]{4,3,2,1,0:T(8,128)S(1)}, f32[1,1,128,8,128]{4,3,2,1,0:T(8,128)}, u32[]{:S(2)}) copy-start(f32[1,1,128,8,128]{4,3,2,1,0:T(8,128)} %param.5) | copy-start | bytes 1572868
  3.2 7.8 %collective-permute-start = (f32[2,8,32,128]{3,2,1,0:T(8,128)S(1)}, f32[2,8,32,128]{3,2,1,0:T(8,128)S(1)}, u32[]{:S(2)}, u32[]{:S(2)}) collective-permute-start(f32[2,8,32,128]{3,2,1,0:T(8,128)S(1)} %get-tuple-element.45), channel_id=1, source_target_pairs={{0,1},{1,0},{2,3},{3,2},{4,5},{5,4},{6,7},{7,6},{8,9},{9,8},{10,11... | collective-permute-start | bytes 786440 | tf_op jit(solution)/shard_map/ppermute | solution.py:418
  3.7 2.7 %copy-start.3 = (s32[2,4]{1,0:T(2,128)S(1)}, s32[2,4]{1,0:T(2,128)}, u32[]{:S(2)}) copy-start(s32[2,4]{1,0:T(2,128)} %refs_0_.5) | copy-start | bytes 100
  3.7 9.8 %collective-permute-start.1 = (f32[2,8,32,128]{3,2,1,0:T(8,128)S(1)}, f32[2,8,32,128]{3,2,1,0:T(8,128)S(1)}, u32[]{:S(2)}, u32[]{:S(2)}) collective-permute-start(f32[2,8,32,128]{3,2,1,0:T(8,128)S(1)} %get-tuple-element.46), channel_id=1, source_target_pairs={{0,2},{1,3},{2,0},{3,1},{4,6},{5,7},{6,4},{7,5},{8,10},{9,11},{10,... | collective-permute-start | bytes 786440 | tf_op jit(solution)/shard_map/ppermute | solution.py:418
  6.3 12.2 %collective-permute-start.2 = (f32[2,8,32,128]{3,2,1,0:T(8,128)S(1)}, f32[2,8,32,128]{3,2,1,0:T(8,128)S(1)}, u32[]{:S(2)}, u32[]{:S(2)}) collective-permute-start(f32[2,8,32,128]{3,2,1,0:T(8,128)S(1)} %get-tuple-element.47), channel_id=1, source_target_pairs={{0,3},{1,2},{2,1},{3,0},{4,7},{5,6},{6,5},{7,4},{8,11},{9,10},{10,... | collective-permute-start | bytes 786440 | tf_op jit(solution)/shard_map/ppermute | solution.py:418
  10.8 16.2 %collective-permute-start.4 = (f32[256,128]{1,0:T(8,128)S(1)}, f32[256,128]{1,0:T(8,128)S(1)}, u32[]{:S(2)}, u32[]{:S(2)}) collective-permute-start(f32[256,128]{1,0:T(8,128)S(1)} %get-tuple-element.54), channel_id=1, source_target_pairs={{0,1},{1,0},{2,3},{3,2},{4,5},{5,4},{6,7},{7,6},{8,9},{9,8},{10,11... | collective-permute-start | bytes 393224 | tf_op jit(solution)/shard_map/ppermute | solution.py:418
  21.0 6.0 %collective-permute-start.3 = (f32[256,128]{1,0:T(8,128)S(1)}, f32[256,128]{1,0:T(8,128)S(1)}, u32[]{:S(2)}, u32[]{:S(2)}) collective-permute-start(f32[256,128]{1,0:T(8,128)S(1)} %get-tuple-element.52), channel_id=1, source_target_pairs={{0,1},{1,0},{2,3},{3,2},{4,5},{5,4},{6,7},{7,6},{8,9},{9,8},{10,11... | collective-permute-start | bytes 393224 | tf_op jit(solution)/shard_map/ppermute | solution.py:418
  22.3 16.0 %collective-permute-start.9 = (f32[2,8,16,128]{3,2,1,0:T(8,128)S(1)}, f32[2,8,16,128]{3,2,1,0:T(8,128)S(1)}, u32[]{:S(2)}, u32[]{:S(2)}) collective-permute-start(f32[2,8,16,128]{3,2,1,0:T(8,128)S(1)} %get-tuple-element.64), channel_id=1, source_target_pairs={{0,28},{1,29},{2,30},{3,31},{4,24},{5,25},{6,26},{7,27},{8,20},{9,... | collective-permute-start | bytes 393224 | tf_op jit(solution)/shard_map/ppermute | solution.py:418
  27.1 4.3 %collective-permute-start.5 = (f32[128,128]{1,0:T(8,128)S(1)}, f32[128,128]{1,0:T(8,128)S(1)}, u32[]{:S(2)}, u32[]{:S(2)}) collective-permute-start(f32[128,128]{1,0:T(8,128)S(1)} %get-tuple-element.57), channel_id=1, source_target_pairs={{0,2},{1,3},{2,0},{3,1},{4,6},{5,7},{6,4},{7,5},{8,10},{9,11},{10,... | collective-permute-start | bytes 196616 | tf_op jit(solution)/shard_map/ppermute | solution.py:418
  28.7 4.4 %collective-permute-start.6 = (f32[128,128]{1,0:T(8,128)S(1)}, f32[128,128]{1,0:T(8,128)S(1)}, u32[]{:S(2)}, u32[]{:S(2)}) collective-permute-start(f32[128,128]{1,0:T(8,128)S(1)} %get-tuple-element.58), channel_id=1, source_target_pairs={{0,4},{1,5},{2,6},{3,7},{4,0},{5,1},{6,2},{7,3},{8,12},{9,13},{10,... | collective-permute-start | bytes 196616 | tf_op jit(solution)/shard_map/ppermute | solution.py:418
  29.2 5.6 %collective-permute-start.7 = (f32[128,128]{1,0:T(8,128)S(1)}, f32[128,128]{1,0:T(8,128)S(1)}, u32[]{:S(2)}, u32[]{:S(2)}) collective-permute-start(f32[128,128]{1,0:T(8,128)S(1)} %get-tuple-element.59), channel_id=1, source_target_pairs={{0,6},{1,7},{2,4},{3,5},{4,2},{5,3},{6,0},{7,1},{8,14},{9,15},{10,... | collective-permute-start | bytes 196616 | tf_op jit(solution)/shard_map/ppermute | solution.py:418
  30.7 9.7 %collective-permute-start.10 = (f32[2,8,16,128]{3,2,1,0:T(8,128)S(1)}, f32[2,8,16,128]{3,2,1,0:T(8,128)S(1)}, u32[]{:S(2)}, u32[]{:S(2)}) collective-permute-start(f32[2,8,16,128]{3,2,1,0:T(8,128)S(1)} %get-tuple-element.65), channel_id=1, source_target_pairs={{0,24},{1,25},{2,26},{3,27},{4,28},{5,29},{6,30},{7,31},{8,16},{9,... | collective-permute-start | bytes 393224 | tf_op jit(solution)/shard_map/ppermute | solution.py:418
  34.8 5.6 %collective-permute-start.8 = (f32[128,128]{1,0:T(8,128)S(1)}, f32[128,128]{1,0:T(8,128)S(1)}, u32[]{:S(2)}, u32[]{:S(2)}) collective-permute-start(f32[128,128]{1,0:T(8,128)S(1)} %get-tuple-element.63.refs_0_), channel_id=1, source_target_pairs={{0,8},{1,9},{2,10},{3,11},{4,12},{5,13},{6,14},{7,15},{8,0},{9,1},... | collective-permute-start | bytes 196616 | tf_op jit(solution)/shard_map/ppermute | solution.py:418
  35.7 10.5 %collective-permute-start.12 = (f32[2,8,16,128]{3,2,1,0:T(8,128)S(1)}, f32[2,8,16,128]{3,2,1,0:T(8,128)S(1)}, u32[]{:S(2)}, u32[]{:S(2)}) collective-permute-start(f32[2,8,16,128]{3,2,1,0:T(8,128)S(1)} %get-tuple-element.69), channel_id=1, source_target_pairs={{0,20},{1,21},{2,22},{3,23},{4,16},{5,17},{6,18},{7,19},{8,28},{9,... | collective-permute-start | bytes 393224 | tf_op jit(solution)/shard_map/ppermute | solution.py:418
  38.1 9.8 %collective-permute-start.13 = (f32[2,8,16,128]{3,2,1,0:T(8,128)S(1)}, f32[2,8,16,128]{3,2,1,0:T(8,128)S(1)}, u32[]{:S(2)}, u32[]{:S(2)}) collective-permute-start(f32[2,8,16,128]{3,2,1,0:T(8,128)S(1)} %get-tuple-element.70), channel_id=1, source_target_pairs={{0,8},{1,9},{2,10},{3,11},{4,12},{5,13},{6,14},{7,15},{8,0},{9,1},... | collective-permute-start | bytes 393224 | tf_op jit(solution)/shard_map/ppermute | solution.py:418
  38.2 11.8 %collective-permute-start.15 = (f32[2,8,16,128]{3,2,1,0:T(8,128)S(1)}, f32[2,8,16,128]{3,2,1,0:T(8,128)S(1)}, u32[]{:S(2)}, u32[]{:S(2)}) collective-permute-start(f32[2,8,16,128]{3,2,1,0:T(8,128)S(1)} %get-tuple-element.72), channel_id=1, source_target_pairs={{0,4},{1,5},{2,6},{3,7},{4,0},{5,1},{6,2},{7,3},{8,12},{9,13},{10,... | collective-permute-start | bytes 393224 | tf_op jit(solution)/shard_map/ppermute | solution.py:418
  40.4 7.5 %collective-permute-start.11 = (f32[128,128]{1,0:T(8,128)S(1)}, f32[128,128]{1,0:T(8,128)S(1)}, u32[]{:S(2)}, u32[]{:S(2)}) collective-permute-start(f32[128,128]{1,0:T(8,128)S(1)} %get-tuple-element.68.refs_0_), channel_id=1, source_target_pairs={{0,16},{1,17},{2,18},{3,19},{4,20},{5,21},{6,22},{7,23},{8,24},{9,... | collective-permute-start | bytes 196616 | tf_op jit(solution)/shard_map/ppermute | solution.py:418
  41.4 12.9 %collective-permute-start.16 = (f32[2,8,16,128]{3,2,1,0:T(8,128)S(1)}, f32[2,8,16,128]{3,2,1,0:T(8,128)S(1)}, u32[]{:S(2)}, u32[]{:S(2)}) collective-permute-start(f32[2,8,16,128]{3,2,1,0:T(8,128)S(1)} %get-tuple-element.74), channel_id=1, source_target_pairs={{0,12},{1,13},{2,14},{3,15},{4,8},{5,9},{6,10},{7,11},{8,4},{9,5},... | collective-permute-start | bytes 393224 | tf_op jit(solution)/shard_map/ppermute | solution.py:418
  46.1 8.7 %collective-permute-start.17 = (f32[2,8,16,128]{3,2,1,0:T(8,128)S(1)}, f32[2,8,16,128]{3,2,1,0:T(8,128)S(1)}, u32[]{:S(2)}, u32[]{:S(2)}) collective-permute-start(f32[2,8,16,128]{3,2,1,0:T(8,128)S(1)} %get-tuple-element.75), channel_id=1, source_target_pairs={{0,16},{1,17},{2,18},{3,19},{4,20},{5,21},{6,22},{7,23},{8,24},{9,... | collective-permute-start | bytes 393224 | tf_op jit(solution)/shard_map/ppermute | solution.py:418
  47.9 5.2 %collective-permute-start.19 = (f32[128,128]{1,0:T(8,128)S(1)}, f32[128,128]{1,0:T(8,128)S(1)}, u32[]{:S(2)}, u32[]{:S(2)}) collective-permute-start(f32[128,128]{1,0:T(8,128)S(1)} %get-tuple-element.71.refs_0_), channel_id=1, source_target_pairs={{0,6},{1,7},{2,4},{3,5},{4,2},{5,3},{6,0},{7,1},{8,14},{9,15},{10,... | collective-permute-start | bytes 196616 | tf_op jit(solution)/shard_map/ppermute | solution.py:418
  49.2 4.6 %collective-permute-start.18 = (f32[128,128]{1,0:T(8,128)S(1)}, f32[128,128]{1,0:T(8,128)S(1)}, u32[]{:S(2)}, u32[]{:S(2)}) collective-permute-start(f32[128,128]{1,0:T(8,128)S(1)} %get-tuple-element.71.refs_0_), channel_id=1, source_target_pairs={{0,4},{1,5},{2,6},{3,7},{4,0},{5,1},{6,2},{7,3},{8,12},{9,13},{10,... | collective-permute-start | bytes 196616 | tf_op jit(solution)/shard_map/ppermute | solution.py:418
  50.0 4.3 %collective-permute-start.14 = (f32[128,128]{1,0:T(8,128)S(1)}, f32[128,128]{1,0:T(8,128)S(1)}, u32[]{:S(2)}, u32[]{:S(2)}) collective-permute-start(f32[128,128]{1,0:T(8,128)S(1)} %get-tuple-element.71.refs_0_), channel_id=1, source_target_pairs={{0,2},{1,3},{2,0},{3,1},{4,6},{5,7},{6,4},{7,5},{8,10},{9,11},{10,... | collective-permute-start | bytes 196616 | tf_op jit(solution)/shard_map/ppermute | solution.py:418
  53.2 2.7 %collective-permute-start.20 = (f32[128,128]{1,0:T(8,128)S(1)}, f32[128,128]{1,0:T(8,128)S(1)}, u32[]{:S(2)}, u32[]{:S(2)}) collective-permute-start(f32[128,128]{1,0:T(8,128)S(1)} %get-tuple-element.71.refs_0_), channel_id=1, source_target_pairs={{0,1},{1,0},{2,3},{3,2},{4,5},{5,4},{6,7},{7,6},{8,9},{9,8},{10,11... | collective-permute-start | bytes 196616 | tf_op jit(solution)/shard_map/ppermute | solution.py:418
  53.8 2.1 %collective-permute-start.23 = (f32[128,128]{1,0:T(8,128)S(1)}, f32[128,128]{1,0:T(8,128)S(1)}, u32[]{:S(2)}, u32[]{:S(2)}) collective-permute-start(f32[128,128]{1,0:T(8,128)S(1)} %collective-permute-done.19.refs_3_), channel_id=1, source_target_pairs={{0,1},{1,0},{2,3},{3,2},{4,5},{5,4},{6,7},{7,6},{8,9},{9,8},{10,11... | collective-permute-start | bytes 196616 | tf_op jit(solution)/shard_map/ppermute | solution.py:418
  54.3 1.6 %collective-permute-start.22 = (f32[128,128]{1,0:T(8,128)S(1)}, f32[128,128]{1,0:T(8,128)S(1)}, u32[]{:S(2)}, u32[]{:S(2)}) collective-permute-start(f32[128,128]{1,0:T(8,128)S(1)} %collective-permute-done.18.refs_2_), channel_id=1, source_target_pairs={{0,1},{1,0},{2,3},{3,2},{4,5},{5,4},{6,7},{7,6},{8,9},{9,8},{10,11... | collective-permute-start | bytes 196616 | tf_op jit(solution)/shard_map/ppermute | solution.py:418
  54.3 1.6 %collective-permute-start.21 = (f32[128,128]{1,0:T(8,128)S(1)}, f32[128,128]{1,0:T(8,128)S(1)}, u32[]{:S(2)}, u32[]{:S(2)}) collective-permute-start(f32[128,128]{1,0:T(8,128)S(1)} %collective-permute-done.14.refs_0_.refs_1_), channel_id=1, source_target_pairs={{0,1},{1,0},{2,3},{3,2},{4,5},{5,4},{6,7},{7,6},{8,9},{9,8},{10,11... | collective-permute-start | bytes 196616 | tf_op jit(solution)/shard_map/ppermute | solution.py:418

commit v5 on v4

--- a/solution.py
+++ b/solution.py
@@ -312,7 +312,8 @@
 
 
 def plane_partners(n_qb):
-    return [(dx, dy) for dx in range(2) for dy in range(n_qb // 2)]
+    pairs = [(dx, dy) for dx in range(2) for dy in range(n_qb // 2)]
+    return sorted(pairs, key=lambda p: (p[0] > 0, p[0] * -p[1] if p[0] else p[1]))
 
 
 def place_of(n_qb, dx, dy):

time: 57.7 us -> 57.3 us (level)
  waiting for transfers between devices: 19 us -> 17.4 us
  starting transfers between devices: 24.6 us -> 26.2 us
    ppermute x24, starting transfers between devices: 24.6 us -> 26.2 us  [exchange(): return lax.ppermute(x, ('qa', 'qb'), pairs)]
    ppermute x24, waiting for transfers between devices: 19 us -> 17.4 us  [exchange(): return lax.ppermute(x, ('qa', 'qb'), pairs)]
  transfers between devices with their start and end apart: 24 -> 24, of which waited for: 11 -> 9; matrix products, arithmetic and copies ran while one was open for 0% -> 0% of each run, Pallas kernels for 16% -> 16%
where the time goes in v5:
time: 57.3 us; the launch traced here: 56.8 us
  starting transfers between devices  26.2 us (46%)
  waiting for transfers between devices  17.4 us (30%)
  Pallas kernels  12.4 us (22%)
  between operations  0.79 us (1%)
    ppermute x24, starting transfers between devices, exchange(): return lax.ppermute(x, ('qa', 'qb'), pairs)  26.2 us
    ppermute x24, waiting for transfers between devices, exchange(): return lax.ppermute(x, ('qa', 'qb'), pairs)  17.4 us
    pallas_call x11, Pallas kernels, call(): pl.pallas_call(body, out_shape=outs + [shape(*x.shape) for x in ride], in...  12.4 us
  transfers between devices with their start and end apart: 24, of which 9 were waited for; matrix products, arithmetic and copies ran while one was open for 0% of the time, Pallas kernels for 16%

profile of v5, /device:TPU:0, one launch (start us, length us, event | category | flops | bytes accessed | tf_op | source)
XLA Modules:
  0.0 56.8 jit_solution(17759038992113844417)
XLA Ops:
  0.7 2.6 %shard_map.68 = (f32[2,8,32,128]{3,2,1,0:T(8,128)S(1)}, f32[2,8,32,128]{3,2,1,0:T(8,128)S(1)}, f32[2,8,32,128]{3,2,1,0:T(8,128)S(1)}, f32[2,8,32,128]{3,2,1,0:T(8,128)S(1)}) custom-call(s32[2,4]{1,0:T(2,128)} %refs_0_.5, f32[2,4,128,128]{3,2,1,0:T(8,128)} %refs_1_.3, f32[128,8,128]{2,1,0:T(8,128)} %bitcast.5, f32[128,8,128]{2,1,0:T(8,128)} %bitcast.7), custom_call_target="tpu_custom_call" | custom-call | flops 536870912 | bytes 2621472 | tf_op jit(solution)/shard_map/pallas_call | solution.py:398
  3.2 0.5 collective-permute-start
  3.7 2.6 %collective-permute-start.1 = (f32[2,8,32,128]{3,2,1,0:T(8,128)S(1)}, f32[2,8,32,128]{3,2,1,0:T(8,128)S(1)}, u32[]{:S(2)}, u32[]{:S(2)}) collective-permute-start(f32[2,8,32,128]{3,2,1,0:T(8,128)S(1)} %get-tuple-element.46), channel_id=1, source_target_pairs={{0,2},{1,3},{2,0},{3,1},{4,6},{5,7},{6,4},{7,5},{8,10},{9,11},{10,... | collective-permute-start | bytes 786440 | tf_op jit(solution)/shard_map/ppermute | solution.py:419
  6.4 4.4 %shard_map.67 = (f32[256,128]{1,0:T(8,128)S(1)}, f32[256,128]{1,0:T(8,128)S(1)}, bf16[1,4,256,256]{3,2,1,0:T(8,128)(2,1)S(1)}, bf16[1,5,256,256]{3,2,1,0:T(8,128...) custom-call(s32[2,4]{1,0:T(2,128)S(1)} %copy-done.3, f32[2,4,128,128]{3,2,1,0:T(8,128)S(1)} %copy-done, ...), custom_call_target="tpu_custom_call" | custom-call | flops 5368709120 | bytes 4718624 | tf_op jit(solution)/shard_map/pallas_call | solution.py:398
  10.8 0.2 collective-permute-start.4
  11.0 2.5 %collective-permute-done.1.refs_5_.refs_4_ = f32[2,8,32,128]{3,2,1,0:T(8,128)S(1)} collective-permute-done((f32[2,8,32,128]{3,2,1,0:T(8,128)S(1)}, f32[2,8,32,128]{3,2,1,0:T(8,128)S(1)}, u32[]{:S(2)}, u32[]{:S(2)}) %collective-permute-start.1) | collective-permute-done | bytes 262176 | tf_op jit(solution)/shard_map/ppermute | solution.py:419
  13.5 5.1 %collective-permute-done.2.refs_6_.refs_5_ = f32[2,8,32,128]{3,2,1,0:T(8,128)S(1)} collective-permute-done((f32[2,8,32,128]{3,2,1,0:T(8,128)S(1)}, f32[2,8,32,128]{3,2,1,0:T(8,128)S(1)}, u32[]{:S(2)}, u32[]{:S(2)}) %collective-permute-start.2) | collective-permute-done | bytes 262176 | tf_op jit(solution)/shard_map/ppermute | solution.py:419
  18.6 2.4 %shard_map.69 = (f32[256,128]{1,0:T(8,128)S(1)}, f32[256,128]{1,0:T(8,128)S(1)}) custom-call(s32[2,4]{1,0:T(2,128)S(1)} %copy-done.3, bf16[1,4,256,256]{3,2,1,0:T(8,128)(2,1)S(1)} %get-tuple-element.48.refs_1_, bf16[1,5,256,256]{3,2,1,0:T(8,128)(2,1)S(1)} %get-tuple-element.49.refs_2_, f32[2,8,32,128]{3,2,1,0:T(8,128)S(1)} %get-tuple-element.44.refs_3_.refs_2_, ...), custom_call_target="tpu_custom_call" | custom-call | flops 26843545600 | bytes 3670048 | tf_op jit(solution)/shard_map/pallas_call | solution.py:398
  21.2 1.0 %shard_map.70 = (f32[2,8,16,128]{3,2,1,0:T(8,128)S(1)}, f32[2,8,16,128]{3,2,1,0:T(8,128)S(1)}, f32[2,8,16,128]{3,2,1,0:T(8,128)S(1)}, f32[2,8,16,128]{3,2,1,0:T(...) custom-call(bf16[256,256]{1,0:T(8,128)(2,1)S(1)} %get-tuple-element., ...), custom_call_target="tpu_custom_call", output_to_operand_aliasing={{8}: (6, {})} | custom-call | flops 1610612736 | bytes 2621440 | tf_op jit(solution)/shard_map/pallas_call | solution.py:398
  22.3 4.8 %collective-permute-start.9 = (f32[2,8,16,128]{3,2,1,0:T(8,128)S(1)}, f32[2,8,16,128]{3,2,1,0:T(8,128)S(1)}, u32[]{:S(2)}, u32[]{:S(2)}) collective-permute-start(f32[2,8,16,128]{3,2,1,0:T(8,128)S(1)} %get-tuple-element.64), channel_id=1, source_target_pairs={{0,28},{1,29},{2,30},{3,31},{4,24},{5,25},{6,26},{7,27},{8,20},{9,... | collective-permute-start | bytes 393224 | tf_op jit(solution)/shard_map/ppermute | solution.py:419
  27.1 1.6 %collective-permute-start.5 = (f32[128,128]{1,0:T(8,128)S(1)}, f32[128,128]{1,0:T(8,128)S(1)}, u32[]{:S(2)}, u32[]{:S(2)}) collective-permute-start(f32[128,128]{1,0:T(8,128)S(1)} %get-tuple-element.57), channel_id=1, source_target_pairs={{0,2},{1,3},{2,0},{3,1},{4,6},{5,7},{6,4},{7,5},{8,10},{9,11},{10,... | collective-permute-start | bytes 196616 | tf_op jit(solution)/shard_map/ppermute | solution.py:419
  28.7 0.5 collective-permute-start.6
  29.2 1.5 %collective-permute-start.7 = (f32[128,128]{1,0:T(8,128)S(1)}, f32[128,128]{1,0:T(8,128)S(1)}, u32[]{:S(2)}, u32[]{:S(2)}) collective-permute-start(f32[128,128]{1,0:T(8,128)S(1)} %get-tuple-element.59), channel_id=1, source_target_pairs={{0,4},{1,5},{2,6},{3,7},{4,0},{5,1},{6,2},{7,3},{8,12},{9,13},{10,... | collective-permute-start | bytes 196616 | tf_op jit(solution)/shard_map/ppermute | solution.py:419
  30.7 0.2 collective-permute-start.10
  30.9 0.6 collective-permute-done.5.refs_1_
  31.5 2.7 %collective-permute-done.6.refs_2_ = f32[128,128]{1,0:T(8,128)S(1)} collective-permute-done((f32[128,128]{1,0:T(8,128)S(1)}, f32[128,128]{1,0:T(8,128)S(1)}, u32[]{:S(2)}, u32[]{:S(2)}) %collective-permute-start.6) | collective-permute-done | bytes 65568 | tf_op jit(solution)/shard_map/ppermute | solution.py:419
  34.1 1.3 %collective-permute-start.8 = (f32[128,128]{1,0:T(8,128)S(1)}, f32[128,128]{1,0:T(8,128)S(1)}, u32[]{:S(2)}, u32[]{:S(2)}) collective-permute-start(f32[128,128]{1,0:T(8,128)S(1)} %get-tuple-element.63.refs_0_), channel_id=1, source_target_pairs={{0,8},{1,9},{2,10},{3,11},{4,12},{5,13},{6,14},{7,15},{8,0},{9,1},... | collective-permute-start | bytes 196616 | tf_op jit(solution)/shard_map/ppermute | solution.py:419
  35.4 2.7 %collective-permute-start.12 = (f32[2,8,16,128]{3,2,1,0:T(8,128)S(1)}, f32[2,8,16,128]{3,2,1,0:T(8,128)S(1)}, u32[]{:S(2)}, u32[]{:S(2)}) collective-permute-start(f32[2,8,16,128]{3,2,1,0:T(8,128)S(1)} %get-tuple-element.69), channel_id=1, source_target_pairs={{0,20},{1,21},{2,22},{3,23},{4,16},{5,17},{6,18},{7,19},{8,28},{9,... | collective-permute-start | bytes 393224 | tf_op jit(solution)/shard_map/ppermute | solution.py:419
  38.2 0.9 %collective-permute-start.15 = (f32[2,8,16,128]{3,2,1,0:T(8,128)S(1)}, f32[2,8,16,128]{3,2,1,0:T(8,128)S(1)}, u32[]{:S(2)}, u32[]{:S(2)}) collective-permute-start(f32[2,8,16,128]{3,2,1,0:T(8,128)S(1)} %get-tuple-element.72), channel_id=1, source_target_pairs={{0,4},{1,5},{2,6},{3,7},{4,0},{5,1},{6,2},{7,3},{8,12},{9,13},{10,... | collective-permute-start | bytes 393224 | tf_op jit(solution)/shard_map/ppermute | solution.py:419
  39.2 3.0 %collective-permute-start.11 = (f32[128,128]{1,0:T(8,128)S(1)}, f32[128,128]{1,0:T(8,128)S(1)}, u32[]{:S(2)}, u32[]{:S(2)}) collective-permute-start(f32[128,128]{1,0:T(8,128)S(1)} %get-tuple-element.68.refs_0_), channel_id=1, source_target_pairs={{0,16},{1,17},{2,18},{3,19},{4,20},{5,21},{6,22},{7,23},{8,24},{9,... | collective-permute-start | bytes 196616 | tf_op jit(solution)/shard_map/ppermute | solution.py:419
  42.2 1.5 %collective-permute-start.16 = (f32[2,8,16,128]{3,2,1,0:T(8,128)S(1)}, f32[2,8,16,128]{3,2,1,0:T(8,128)S(1)}, u32[]{:S(2)}, u32[]{:S(2)}) collective-permute-start(f32[2,8,16,128]{3,2,1,0:T(8,128)S(1)} %get-tuple-element.74), channel_id=1, source_target_pairs={{0,12},{1,13},{2,14},{3,15},{4,8},{5,9},{6,10},{7,11},{8,4},{9,5},... | collective-permute-start | bytes 393224 | tf_op jit(solution)/shard_map/ppermute | solution.py:419
  43.8 1.9 %collective-permute-done.12.refs_2_ = f32[2,8,16,128]{3,2,1,0:T(8,128)S(1)} collective-permute-done((f32[2,8,16,128]{3,2,1,0:T(8,128)S(1)}, f32[2,8,16,128]{3,2,1,0:T(8,128)S(1)}, u32[]{:S(2)}, u32[]{:S(2)}) %collective-permute-start.12) | collective-permute-done | bytes 131104 | tf_op jit(solution)/shard_map/ppermute | solution.py:419
  45.7 0.4 collective-permute-start.17
  46.0 2.1 %collective-permute-done.13.refs_3_ = f32[2,8,16,128]{3,2,1,0:T(8,128)S(1)} collective-permute-done((f32[2,8,16,128]{3,2,1,0:T(8,128)S(1)}, f32[2,8,16,128]{3,2,1,0:T(8,128)S(1)}, u32[]{:S(2)}, u32[]{:S(2)}) %collective-permute-start.13) | collective-permute-done | bytes 131104 | tf_op jit(solution)/shard_map/ppermute | solution.py:419
  48.2 1.8 %collective-permute-start.18 = (f32[128,128]{1,0:T(8,128)S(1)}, f32[128,128]{1,0:T(8,128)S(1)}, u32[]{:S(2)}, u32[]{:S(2)}) collective-permute-start(f32[128,128]{1,0:T(8,128)S(1)} %get-tuple-element.71.refs_0_), channel_id=1, source_target_pairs={{0,6},{1,7},{2,4},{3,5},{4,2},{5,3},{6,0},{7,1},{8,14},{9,15},{10,... | collective-permute-start | bytes 196616 | tf_op jit(solution)/shard_map/ppermute | solution.py:419
  50.1 1.7 %collective-permute-start.14 = (f32[128,128]{1,0:T(8,128)S(1)}, f32[128,128]{1,0:T(8,128)S(1)}, u32[]{:S(2)}, u32[]{:S(2)}) collective-permute-start(f32[128,128]{1,0:T(8,128)S(1)} %get-tuple-element.71.refs_0_), channel_id=1, source_target_pairs={{0,2},{1,3},{2,0},{3,1},{4,6},{5,7},{6,4},{7,5},{8,10},{9,11},{10,... | collective-permute-start | bytes 196616 | tf_op jit(solution)/shard_map/ppermute | solution.py:419
  51.7 0.8 %collective-permute-done.19.refs_3_ = f32[128,128]{1,0:T(8,128)S(1)} collective-permute-done((f32[128,128]{1,0:T(8,128)S(1)}, f32[128,128]{1,0:T(8,128)S(1)}, u32[]{:S(2)}, u32[]{:S(2)}) %collective-permute-start.19) | collective-permute-done | bytes 65568 | tf_op jit(solution)/shard_map/ppermute | solution.py:419
  52.5 1.0 %collective-permute-done.18.refs_2_ = f32[128,128]{1,0:T(8,128)S(1)} collective-permute-done((f32[128,128]{1,0:T(8,128)S(1)}, f32[128,128]{1,0:T(8,128)S(1)}, u32[]{:S(2)}, u32[]{:S(2)}) %collective-permute-start.18) | collective-permute-done | bytes 65568 | tf_op jit(solution)/shard_map/ppermute | solution.py:419
  53.5 0.9 %collective-permute-done.14.refs_0_.refs_1_ = f32[128,128]{1,0:T(8,128)S(1)} collective-permute-done((f32[128,128]{1,0:T(8,128)S(1)}, f32[128,128]{1,0:T(8,128)S(1)}, u32[]{:S(2)}, u32[]{:S(2)}) %collective-permute-start.14) | collective-permute-done | bytes 65568 | tf_op jit(solution)/shard_map/ppermute | solution.py:419
  54.3 0.5 collective-permute-start.21
  54.8 1.1 %shard_map.76 = (f32[128,8,128]{2,1,0:T(8,128)}, f32[128,8,128]{2,1,0:T(8,128)}) custom-call(f32[2,8,16,128]{3,2,1,0:T(8,128)S(1)} %get-tuple-element.51.refs_0_, f32[2,8,16,128]{3,2,1,0:T(8,128)S(1)} %shard_map.75.refs_1_, f32[2,8,16,128]{3,2,1,0:T(8,128)S(1)} %get-tuple-element.73.refs_2_, f32[2,8,16,128]{3,2,1,0:T(8,128)S(1)} %collective-permute-done.16.refs_3_, ...), custom_call_target="tpu_custom_call" | custom-call | bytes 2097152 | tf_op jit(solution)/shard_map/pallas_call | solution.py:398
  56.0 0.8 %shard_map.77 = f32[2,512,128]{2,1,0:T(8,128)} custom-call(f32[128,128]{1,0:T(8,128)S(1)} %get-tuple-element.71.refs_0_, f32[128,128]{1,0:T(8,128)S(1)} %collective-permute-done.14.refs_0_.refs_1_, f32[128,128]{1,0:T(8,128)S(1)} %collective-permute-done.18.refs_2_, f32[128,128]{1,0:T(8,128)S(1)} %collective-permute-done.19.refs_3_, ...), custom_call_target="tpu_custom_call" | custom-call | bytes 1048576 | tf_op jit(solution)/shard_map/pallas_call | solution.py:398
  (36 shorter events, 0.5 us)
Async XLA Ops:
  0.6 5.8 %copy-start = (f32[2,4,128,128]{3,2,1,0:T(8,128)S(1)}, f32[2,4,128,128]{3,2,1,0:T(8,128)}, u32[]{:S(2)}) copy-start(f32[2,4,128,128]{3,2,1,0:T(8,128)} %refs_1_.3) | copy-start | bytes 1572868
  0.6 5.8 %copy-start.1 = (f32[1,1,128,8,128]{4,3,2,1,0:T(8,128)S(1)}, f32[1,1,128,8,128]{4,3,2,1,0:T(8,128)}, u32[]{:S(2)}) copy-start(f32[1,1,128,8,128]{4,3,2,1,0:T(8,128)} %param.4) | copy-start | bytes 1572868
  0.7 5.8 %copy-start.2 = (f32[1,1,128,8,128]{4,3,2,1,0:T(8,128)S(1)}, f32[1,1,128,8,128]{4,3,2,1,0:T(8,128)}, u32[]{:S(2)}) copy-start(f32[1,1,128,8,128]{4,3,2,1,0:T(8,128)} %param.5) | copy-start | bytes 1572868
  3.2 7.8 %collective-permute-start = (f32[2,8,32,128]{3,2,1,0:T(8,128)S(1)}, f32[2,8,32,128]{3,2,1,0:T(8,128)S(1)}, u32[]{:S(2)}, u32[]{:S(2)}) collective-permute-start(f32[2,8,32,128]{3,2,1,0:T(8,128)S(1)} %get-tuple-element.45), channel_id=1, source_target_pairs={{0,1},{1,0},{2,3},{3,2},{4,5},{5,4},{6,7},{7,6},{8,9},{9,8},{10,11... | collective-permute-start | bytes 786440 | tf_op jit(solution)/shard_map/ppermute | solution.py:419
  3.7 2.7 %copy-start.3 = (s32[2,4]{1,0:T(2,128)S(1)}, s32[2,4]{1,0:T(2,128)}, u32[]{:S(2)}) copy-start(s32[2,4]{1,0:T(2,128)} %refs_0_.5) | copy-start | bytes 100
  3.7 9.8 %collective-permute-start.1 = (f32[2,8,32,128]{3,2,1,0:T(8,128)S(1)}, f32[2,8,32,128]{3,2,1,0:T(8,128)S(1)}, u32[]{:S(2)}, u32[]{:S(2)}) collective-permute-start(f32[2,8,32,128]{3,2,1,0:T(8,128)S(1)} %get-tuple-element.46), channel_id=1, source_target_pairs={{0,2},{1,3},{2,0},{3,1},{4,6},{5,7},{6,4},{7,5},{8,10},{9,11},{10,... | collective-permute-start | bytes 786440 | tf_op jit(solution)/shard_map/ppermute | solution.py:419
  6.3 12.2 %collective-permute-start.2 = (f32[2,8,32,128]{3,2,1,0:T(8,128)S(1)}, f32[2,8,32,128]{3,2,1,0:T(8,128)S(1)}, u32[]{:S(2)}, u32[]{:S(2)}) collective-permute-start(f32[2,8,32,128]{3,2,1,0:T(8,128)S(1)} %get-tuple-element.47), channel_id=1, source_target_pairs={{0,3},{1,2},{2,1},{3,0},{4,7},{5,6},{6,5},{7,4},{8,11},{9,10},{10,... | collective-permute-start | bytes 786440 | tf_op jit(solution)/shard_map/ppermute | solution.py:419
  10.8 16.3 %collective-permute-start.4 = (f32[256,128]{1,0:T(8,128)S(1)}, f32[256,128]{1,0:T(8,128)S(1)}, u32[]{:S(2)}, u32[]{:S(2)}) collective-permute-start(f32[256,128]{1,0:T(8,128)S(1)} %get-tuple-element.54), channel_id=1, source_target_pairs={{0,1},{1,0},{2,3},{3,2},{4,5},{5,4},{6,7},{7,6},{8,9},{9,8},{10,11... | collective-permute-start | bytes 393224 | tf_op jit(solution)/shard_map/ppermute | solution.py:419
  21.1 6.0 %collective-permute-start.3 = (f32[256,128]{1,0:T(8,128)S(1)}, f32[256,128]{1,0:T(8,128)S(1)}, u32[]{:S(2)}, u32[]{:S(2)}) collective-permute-start(f32[256,128]{1,0:T(8,128)S(1)} %get-tuple-element.52), channel_id=1, source_target_pairs={{0,1},{1,0},{2,3},{3,2},{4,5},{5,4},{6,7},{7,6},{8,9},{9,8},{10,11... | collective-permute-start | bytes 393224 | tf_op jit(solution)/shard_map/ppermute | solution.py:419
  22.3 16.0 %collective-permute-start.9 = (f32[2,8,16,128]{3,2,1,0:T(8,128)S(1)}, f32[2,8,16,128]{3,2,1,0:T(8,128)S(1)}, u32[]{:S(2)}, u32[]{:S(2)}) collective-permute-start(f32[2,8,16,128]{3,2,1,0:T(8,128)S(1)} %get-tuple-element.64), channel_id=1, source_target_pairs={{0,28},{1,29},{2,30},{3,31},{4,24},{5,25},{6,26},{7,27},{8,20},{9,... | collective-permute-start | bytes 393224 | tf_op jit(solution)/shard_map/ppermute | solution.py:419
  27.1 4.3 %collective-permute-start.5 = (f32[128,128]{1,0:T(8,128)S(1)}, f32[128,128]{1,0:T(8,128)S(1)}, u32[]{:S(2)}, u32[]{:S(2)}) collective-permute-start(f32[128,128]{1,0:T(8,128)S(1)} %get-tuple-element.57), channel_id=1, source_target_pairs={{0,2},{1,3},{2,0},{3,1},{4,6},{5,7},{6,4},{7,5},{8,10},{9,11},{10,... | collective-permute-start | bytes 196616 | tf_op jit(solution)/shard_map/ppermute | solution.py:419
  28.7 5.4 %collective-permute-start.6 = (f32[128,128]{1,0:T(8,128)S(1)}, f32[128,128]{1,0:T(8,128)S(1)}, u32[]{:S(2)}, u32[]{:S(2)}) collective-permute-start(f32[128,128]{1,0:T(8,128)S(1)} %get-tuple-element.58), channel_id=1, source_target_pairs={{0,6},{1,7},{2,4},{3,5},{4,2},{5,3},{6,0},{7,1},{8,14},{9,15},{10,... | collective-permute-start | bytes 196616 | tf_op jit(solution)/shard_map/ppermute | solution.py:419
  29.2 4.9 %collective-permute-start.7 = (f32[128,128]{1,0:T(8,128)S(1)}, f32[128,128]{1,0:T(8,128)S(1)}, u32[]{:S(2)}, u32[]{:S(2)}) collective-permute-start(f32[128,128]{1,0:T(8,128)S(1)} %get-tuple-element.59), channel_id=1, source_target_pairs={{0,4},{1,5},{2,6},{3,7},{4,0},{5,1},{6,2},{7,3},{8,12},{9,13},{10,... | collective-permute-start | bytes 196616 | tf_op jit(solution)/shard_map/ppermute | solution.py:419
  30.7 8.5 %collective-permute-start.10 = (f32[2,8,16,128]{3,2,1,0:T(8,128)S(1)}, f32[2,8,16,128]{3,2,1,0:T(8,128)S(1)}, u32[]{:S(2)}, u32[]{:S(2)}) collective-permute-start(f32[2,8,16,128]{3,2,1,0:T(8,128)S(1)} %get-tuple-element.65), channel_id=1, source_target_pairs={{0,24},{1,25},{2,26},{3,27},{4,28},{5,29},{6,30},{7,31},{8,16},{9,... | collective-permute-start | bytes 393224 | tf_op jit(solution)/shard_map/ppermute | solution.py:419
  34.1 5.0 %collective-permute-start.8 = (f32[128,128]{1,0:T(8,128)S(1)}, f32[128,128]{1,0:T(8,128)S(1)}, u32[]{:S(2)}, u32[]{:S(2)}) collective-permute-start(f32[128,128]{1,0:T(8,128)S(1)} %get-tuple-element.63.refs_0_), channel_id=1, source_target_pairs={{0,8},{1,9},{2,10},{3,11},{4,12},{5,13},{6,14},{7,15},{8,0},{9,1},... | collective-permute-start | bytes 196616 | tf_op jit(solution)/shard_map/ppermute | solution.py:419
  35.4 10.2 %collective-permute-start.12 = (f32[2,8,16,128]{3,2,1,0:T(8,128)S(1)}, f32[2,8,16,128]{3,2,1,0:T(8,128)S(1)}, u32[]{:S(2)}, u32[]{:S(2)}) collective-permute-start(f32[2,8,16,128]{3,2,1,0:T(8,128)S(1)} %get-tuple-element.69), channel_id=1, source_target_pairs={{0,20},{1,21},{2,22},{3,23},{4,16},{5,17},{6,18},{7,19},{8,28},{9,... | collective-permute-start | bytes 393224 | tf_op jit(solution)/shard_map/ppermute | solution.py:419
  38.1 10.0 %collective-permute-start.13 = (f32[2,8,16,128]{3,2,1,0:T(8,128)S(1)}, f32[2,8,16,128]{3,2,1,0:T(8,128)S(1)}, u32[]{:S(2)}, u32[]{:S(2)}) collective-permute-start(f32[2,8,16,128]{3,2,1,0:T(8,128)S(1)} %get-tuple-element.70), channel_id=1, source_target_pairs={{0,8},{1,9},{2,10},{3,11},{4,12},{5,13},{6,14},{7,15},{8,0},{9,1},... | collective-permute-start | bytes 393224 | tf_op jit(solution)/shard_map/ppermute | solution.py:419
  38.2 11.8 %collective-permute-start.15 = (f32[2,8,16,128]{3,2,1,0:T(8,128)S(1)}, f32[2,8,16,128]{3,2,1,0:T(8,128)S(1)}, u32[]{:S(2)}, u32[]{:S(2)}) collective-permute-start(f32[2,8,16,128]{3,2,1,0:T(8,128)S(1)} %get-tuple-element.72), channel_id=1, source_target_pairs={{0,4},{1,5},{2,6},{3,7},{4,0},{5,1},{6,2},{7,3},{8,12},{9,13},{10,... | collective-permute-start | bytes 393224 | tf_op jit(solution)/shard_map/ppermute | solution.py:419
  39.2 9.0 %collective-permute-start.11 = (f32[128,128]{1,0:T(8,128)S(1)}, f32[128,128]{1,0:T(8,128)S(1)}, u32[]{:S(2)}, u32[]{:S(2)}) collective-permute-start(f32[128,128]{1,0:T(8,128)S(1)} %get-tuple-element.68.refs_0_), channel_id=1, source_target_pairs={{0,16},{1,17},{2,18},{3,19},{4,20},{5,21},{6,22},{7,23},{8,24},{9,... | collective-permute-start | bytes 196616 | tf_op jit(solution)/shard_map/ppermute | solution.py:419
  42.2 12.1 %collective-permute-start.16 = (f32[2,8,16,128]{3,2,1,0:T(8,128)S(1)}, f32[2,8,16,128]{3,2,1,0:T(8,128)S(1)}, u32[]{:S(2)}, u32[]{:S(2)}) collective-permute-start(f32[2,8,16,128]{3,2,1,0:T(8,128)S(1)} %get-tuple-element.74), channel_id=1, source_target_pairs={{0,12},{1,13},{2,14},{3,15},{4,8},{5,9},{6,10},{7,11},{8,4},{9,5},... | collective-permute-start | bytes 393224 | tf_op jit(solution)/shard_map/ppermute | solution.py:419
  45.7 9.2 %collective-permute-start.17 = (f32[2,8,16,128]{3,2,1,0:T(8,128)S(1)}, f32[2,8,16,128]{3,2,1,0:T(8,128)S(1)}, u32[]{:S(2)}, u32[]{:S(2)}) collective-permute-start(f32[2,8,16,128]{3,2,1,0:T(8,128)S(1)} %get-tuple-element.75), channel_id=1, source_target_pairs={{0,16},{1,17},{2,18},{3,19},{4,20},{5,21},{6,22},{7,23},{8,24},{9,... | collective-permute-start | bytes 393224 | tf_op jit(solution)/shard_map/ppermute | solution.py:419
  48.2 4.3 %collective-permute-start.19 = (f32[128,128]{1,0:T(8,128)S(1)}, f32[128,128]{1,0:T(8,128)S(1)}, u32[]{:S(2)}, u32[]{:S(2)}) collective-permute-start(f32[128,128]{1,0:T(8,128)S(1)} %get-tuple-element.71.refs_0_), channel_id=1, source_target_pairs={{0,4},{1,5},{2,6},{3,7},{4,0},{5,1},{6,2},{7,3},{8,12},{9,13},{10,... | collective-permute-start | bytes 196616 | tf_op jit(solution)/shard_map/ppermute | solution.py:419
  48.2 5.2 %collective-permute-start.18 = (f32[128,128]{1,0:T(8,128)S(1)}, f32[128,128]{1,0:T(8,128)S(1)}, u32[]{:S(2)}, u32[]{:S(2)}) collective-permute-start(f32[128,128]{1,0:T(8,128)S(1)} %get-tuple-element.71.refs_0_), channel_id=1, source_target_pairs={{0,6},{1,7},{2,4},{3,5},{4,2},{5,3},{6,0},{7,1},{8,14},{9,15},{10,... | collective-permute-start | bytes 196616 | tf_op jit(solution)/shard_map/ppermute | solution.py:419
  50.1 4.3 %collective-permute-start.14 = (f32[128,128]{1,0:T(8,128)S(1)}, f32[128,128]{1,0:T(8,128)S(1)}, u32[]{:S(2)}, u32[]{:S(2)}) collective-permute-start(f32[128,128]{1,0:T(8,128)S(1)} %get-tuple-element.71.refs_0_), channel_id=1, source_target_pairs={{0,2},{1,3},{2,0},{3,1},{4,6},{5,7},{6,4},{7,5},{8,10},{9,11},{10,... | collective-permute-start | bytes 196616 | tf_op jit(solution)/shard_map/ppermute | solution.py:419
  52.5 3.4 %collective-permute-start.20 = (f32[128,128]{1,0:T(8,128)S(1)}, f32[128,128]{1,0:T(8,128)S(1)}, u32[]{:S(2)}, u32[]{:S(2)}) collective-permute-start(f32[128,128]{1,0:T(8,128)S(1)} %get-tuple-element.71.refs_0_), channel_id=1, source_target_pairs={{0,1},{1,0},{2,3},{3,2},{4,5},{5,4},{6,7},{7,6},{8,9},{9,8},{10,11... | collective-permute-start | bytes 196616 | tf_op jit(solution)/shard_map/ppermute | solution.py:419
  53.5 2.5 %collective-permute-start.23 = (f32[128,128]{1,0:T(8,128)S(1)}, f32[128,128]{1,0:T(8,128)S(1)}, u32[]{:S(2)}, u32[]{:S(2)}) collective-permute-start(f32[128,128]{1,0:T(8,128)S(1)} %collective-permute-done.19.refs_3_), channel_id=1, source_target_pairs={{0,1},{1,0},{2,3},{3,2},{4,5},{5,4},{6,7},{7,6},{8,9},{9,8},{10,11... | collective-permute-start | bytes 196616 | tf_op jit(solution)/shard_map/ppermute | solution.py:419
  54.3 1.6 %collective-permute-start.22 = (f32[128,128]{1,0:T(8,128)S(1)}, f32[128,128]{1,0:T(8,128)S(1)}, u32[]{:S(2)}, u32[]{:S(2)}) collective-permute-start(f32[128,128]{1,0:T(8,128)S(1)} %collective-permute-done.18.refs_2_), channel_id=1, source_target_pairs={{0,1},{1,0},{2,3},{3,2},{4,5},{5,4},{6,7},{7,6},{8,9},{9,8},{10,11... | collective-permute-start | bytes 196616 | tf_op jit(solution)/shard_map/ppermute | solution.py:419
  54.3 1.6 %collective-permute-start.21 = (f32[128,128]{1,0:T(8,128)S(1)}, f32[128,128]{1,0:T(8,128)S(1)}, u32[]{:S(2)}, u32[]{:S(2)}) collective-permute-start(f32[128,128]{1,0:T(8,128)S(1)} %collective-permute-done.14.refs_0_.refs_1_), channel_id=1, source_target_pairs={{0,1},{1,0},{2,3},{3,2},{4,5},{5,4},{6,7},{7,6},{8,9},{9,8},{10,11... | collective-permute-start | bytes 196616 | tf_op jit(solution)/shard_map/ppermute | solution.py:419
